TPU v7x, 32 devices: a whole 2x2x4 slice. The times are simulated.
32 devices in a mesh: fsdp: 8 (over z, x), tensor: 4 (over y, core).
Axes of the slice: x: 2, y: 2, z: 4, core: 2. Of those that a mesh axis runs over, the one named last changes fastest.
Arguments:
- activations: float32 [8, 197, 768], P('fsdp'), may hold values from -6 to 6
- image_live: int32 [8], P('fsdp'), may hold values 0 or 1
- expert_routes: int32 [8, 197, 2], P('fsdp'), may hold values from 0 to 3, all different within a row; in each aligned block of 197 rows (0 to 196, 197 to 393, ..., all dimensions but the last counted through in order) at most 123 rows name the same one
- attn_gain_one: bfloat16 [768], P('fsdp'), may hold values from 0.5 to 1.5
- qkv_weight_one: bfloat16 [3, 768, 768], P(None, 'fsdp', 'tensor'), may hold values from -0.21875 to 0.21875
- out_weight_one: bfloat16 [768, 768], P('tensor', 'fsdp'), may hold values from -0.625 to 0.625
- first_feedforward_gain: bfloat16 [768], P('fsdp'), may hold values from 0.5 to 1.5
- up_weight_one: bfloat16 [768, 3072], P('fsdp', 'tensor'), may hold values from -0.21875 to 0.21875
- down_weight_one: bfloat16 [3072, 768], P('tensor', 'fsdp'), may hold values from -0.15625 to 0.15625
- attn_gain_two: bfloat16 [768], P('fsdp'), may hold values from 0.5 to 1.5
- qkv_weight_two: bfloat16 [3, 768, 768], P(None, 'fsdp', 'tensor'), may hold values from -0.21875 to 0.21875
- out_weight_two: bfloat16 [768, 768], P('tensor', 'fsdp'), may hold values from -0.625 to 0.625
- moe_gain_two: bfloat16 [768], P('fsdp'), may hold values from 0.5 to 1.5
- router_weight: bfloat16 [768, 4], P('fsdp'), may hold values from -0.15625 to 0.15625
- expert_up: bfloat16 [4, 768, 3072], P(None, 'fsdp', 'tensor'), may hold values from -0.21875 to 0.21875
- expert_down: bfloat16 [4, 3072, 768], P(None, 'tensor', 'fsdp'), may hold values from -0.3125 to 0.3125
- cotangent: float32 [8, 197, 768], P('fsdp'), may hold values from -6 to 6
Outputs:
- result: float32 [8, 197, 768], P('fsdp')
- input_grad: float32 [8, 197, 768], P('fsdp')
- grad_attn_gain_one: float32 [768], P('fsdp')
- grad_qkv_weight_one: float32 [3, 768, 768], P(None, 'fsdp', 'tensor')
- grad_out_weight_one: float32 [768, 768], P('tensor', 'fsdp')
- grad_mlp_gain_one: float32 [768], P('fsdp')
- grad_up_weight_one: float32 [768, 3072], P('fsdp', 'tensor')
- grad_down_weight_one: float32 [3072, 768], P('tensor', 'fsdp')
- grad_attn_gain_two: float32 [768], P('fsdp')
- grad_qkv_weight_two: float32 [3, 768, 768], P(None, 'fsdp', 'tensor')
- grad_out_weight_two: float32 [768, 768], P('tensor', 'fsdp')
- grad_moe_gain_two: float32 [768], P('fsdp')
- grad_router_weight: float32 [768, 4], P('fsdp')
- grad_expert_up: float32 [4, 768, 3072], P(None, 'fsdp', 'tensor')
- grad_expert_down: float32 [4, 3072, 768], P(None, 'tensor', 'fsdp')
Inputs may be any that keep to these rules, and one draw needn't show every extreme that they name: `expert_routes`: each token names two different experts; among the 197 tokens of one index of fsdp no expert is named more than 123 times, a bound that some block reaches.
All inputs are finite; a program needn't handle non-finite values. No bound on the sum of `image_live` on one device may be relied on, other than what follows from the above.
Results may differ from a plain program's by a relative error of at most 0.019.
Values may be sent and summed in bfloat16 or wider, within the bound.
No kernel may reach another device: no remote copies, remote signals or barrier semaphores. Data moves between devices by JAX's collectives and lax.ppermute only.
A program may use at most 128 MiB of HBM per device.

v0:
```python
import jax
import jax.numpy as jnp
from jax import lax
from jax.sharding import PartitionSpec as P

HD = 64


epsilon = 1e-06
root_half = 0.7071067811865476
inv_root_two_pi = 0.3989422804014327
highest = lax.Precision.HIGHEST


def norm_gain(field, gain_vec):
    centred = field - jnp.mean(field, axis=-1, keepdims=True)
    spread = jnp.mean(centred * centred, axis=-1, keepdims=True)
    return centred * lax.rsqrt(spread + epsilon) * gain_vec


def gelu(field):
    return 0.5 * field * (1.0 + jax.scipy.special.erf(field * root_half))


def gelu_slope(field):
    return 0.5 * (
        1.0 + jax.scipy.special.erf(field * root_half)
    ) + field * inv_root_two_pi * jnp.exp(-0.5 * field * field)


def norm_back(field, gain_vec, incoming_gradient):
    unused, pull = jax.vjp(norm_gain, field, gain_vec)
    return pull(incoming_gradient)


def joined(branch):
    return lax.psum(branch, "tensor")


def back_joined(branch):
    return lax.psum(branch, "tensor")


def attn_forward(field, gain_vec, weight_qkv, weight_out):
    batch_size, length, model_width = field.shape
    head_count = weight_qkv.shape[2] // HD
    score_scale = HD ** (-0.5)
    normed = norm_gain(field, gain_vec).astype(jnp.bfloat16)
    packed = jnp.einsum(
        "bsd,tde->tbse", normed, weight_qkv, preferred_element_type=jnp.float32
    ).astype(jnp.bfloat16)
    packed = packed.reshape(3, batch_size, length, head_count, HD)
    scores = (
        jnp.einsum("bqhe,bkhe->bhqk", packed[0], packed[1], preferred_element_type=jnp.float32)
        * score_scale
    )
    log_totals = jax.nn.logsumexp(scores, axis=-1, keepdims=True)
    prob_table = jnp.exp(scores - log_totals)
    mixed_heads = jnp.einsum(
        "bhqk,bkhe->bqhe",
        prob_table.astype(jnp.bfloat16),
        packed[2],
        preferred_element_type=jnp.float32,
    )
    mixed_heads = mixed_heads.astype(jnp.bfloat16).reshape(batch_size, length, head_count * HD)
    branch = jnp.einsum("bse,ed->bsd", mixed_heads, weight_out, preferred_element_type=jnp.float32)
    return (branch, (normed, packed, log_totals, mixed_heads))


def attn_backward(field, gain_vec, weight_qkv, weight_out, kept, incoming_gradient):
    normed, packed, log_totals, mixed_heads = kept
    batch_size, length, model_width = field.shape
    head_count = weight_qkv.shape[2] // HD
    score_scale = HD ** (-0.5)
    upstream_low = incoming_gradient.astype(jnp.bfloat16)
    grad_out = jnp.einsum(
        "bse,bsd->ed", mixed_heads, upstream_low, preferred_element_type=jnp.float32
    )
    grad_mixed = jnp.einsum(
        "bsd,ed->bse", upstream_low, weight_out, preferred_element_type=jnp.float32
    )
    grad_mixed = grad_mixed.astype(jnp.bfloat16).reshape(batch_size, length, head_count, HD)
    scores = (
        jnp.einsum("bqhe,bkhe->bhqk", packed[0], packed[1], preferred_element_type=jnp.float32)
        * score_scale
    )
    prob_table = jnp.exp(scores - log_totals)
    grad_probs = jnp.einsum(
        "bqhe,bkhe->bhqk", grad_mixed, packed[2], preferred_element_type=jnp.float32
    )
    grad_value = jnp.einsum(
        "bhqk,bqhe->bkhe",
        prob_table.astype(jnp.bfloat16),
        grad_mixed,
        preferred_element_type=jnp.float32,
    )
    row_delta = jnp.sum(prob_table * grad_probs, axis=-1, keepdims=True)
    grad_scores = (prob_table * (grad_probs - row_delta)).astype(jnp.bfloat16)
    grad_query = (
        jnp.einsum("bhqk,bkhe->bqhe", grad_scores, packed[1], preferred_element_type=jnp.float32)
        * score_scale
    )
    grad_key = (
        jnp.einsum("bhqk,bqhe->bkhe", grad_scores, packed[0], preferred_element_type=jnp.float32)
        * score_scale
    )
    grad_packed = jnp.stack([grad_query, grad_key, grad_value]).astype(jnp.bfloat16)
    grad_packed = grad_packed.reshape(3, batch_size, length, head_count * HD)
    grad_qkv = jnp.einsum("bsd,tbse->tde", normed, grad_packed, preferred_element_type=jnp.float32)
    grad_normed = back_joined(
        jnp.einsum("tbse,tde->bsd", grad_packed, weight_qkv, preferred_element_type=jnp.float32)
    )
    grad_field, grad_gain = norm_back(field, gain_vec, grad_normed)
    return (incoming_gradient + grad_field, grad_gain, grad_qkv, grad_out)


def mlp_forward(field, gain_vec, weight_up, weight_down):
    normed = norm_gain(field, gain_vec).astype(jnp.bfloat16)
    hidden = jnp.einsum("bsd,df->bsf", normed, weight_up, preferred_element_type=jnp.float32)
    active = gelu(hidden).astype(jnp.bfloat16)
    branch = jnp.einsum("bsf,fd->bsd", active, weight_down, preferred_element_type=jnp.float32)
    return (branch, (normed, hidden, active))


def mlp_backward(field, gain_vec, weight_up, weight_down, kept, incoming_gradient):
    normed, hidden, active = kept
    upstream_low = incoming_gradient.astype(jnp.bfloat16)
    grad_down = jnp.einsum("bsf,bsd->fd", active, upstream_low, preferred_element_type=jnp.float32)
    grad_active = jnp.einsum(
        "bsd,fd->bsf", upstream_low, weight_down, preferred_element_type=jnp.float32
    )
    grad_hidden = (grad_active * gelu_slope(hidden)).astype(jnp.bfloat16)
    grad_up = jnp.einsum("bsd,bsf->df", normed, grad_hidden, preferred_element_type=jnp.float32)
    grad_normed = back_joined(
        jnp.einsum("bsf,df->bsd", grad_hidden, weight_up, preferred_element_type=jnp.float32)
    )
    grad_field, grad_gain = norm_back(field, gain_vec, grad_normed)
    return (incoming_gradient + grad_field, grad_gain, grad_up, grad_down)


def route_forward(field, gain_vec, weight_router, weight_up, weight_down, routes_in):
    batch_size, length, model_width = field.shape
    token_count = batch_size * length
    experts = weight_router.shape[1]
    slot_depth = 5 * token_count // 8
    flat_rows = field.reshape(token_count, model_width)
    normed = norm_gain(flat_rows, gain_vec).astype(jnp.bfloat16)
    logits = jnp.dot(normed, weight_router, preferred_element_type=jnp.float32)
    prob_table = jax.nn.softmax(logits, axis=-1)
    route_ids = routes_in.reshape(token_count, 2)
    route_hits = (route_ids[:, :, None] == jnp.arange(experts, dtype=jnp.int32)).astype(jnp.int32)
    expert_loads = jnp.sum(route_hits, axis=1)
    before = jnp.cumsum(expert_loads, axis=0) - expert_loads
    slot_ids = route_ids * slot_depth + jnp.take_along_axis(before, route_ids, axis=1)
    flat_slots = slot_ids.reshape(-1)
    token_ids = jnp.repeat(jnp.arange(token_count, dtype=jnp.int32), 2)
    slot_owner = jnp.zeros((experts * slot_depth,), jnp.int32).at[flat_slots].set(token_ids)
    gate_values = jnp.take_along_axis(prob_table, route_ids, axis=1)
    slot_gate = (
        jnp.zeros((experts * slot_depth,), jnp.float32).at[flat_slots].set(gate_values.reshape(-1))
    )
    expert_inputs = normed[slot_owner].reshape(experts, slot_depth, model_width)
    hidden = jnp.einsum(
        "ecd,edf->ecf", expert_inputs, weight_up, preferred_element_type=jnp.float32
    )
    active = gelu(hidden).astype(jnp.bfloat16)
    outputs = jnp.einsum("ecf,efd->ecd", active, weight_down, preferred_element_type=jnp.float32)
    outputs = outputs.reshape(experts * slot_depth, model_width)
    branch = (
        gate_values[:, 0:1] * outputs[slot_ids[:, 0]]
        + gate_values[:, 1:2] * outputs[slot_ids[:, 1]]
    )
    kept = (
        normed,
        prob_table,
        route_ids,
        slot_ids,
        slot_owner,
        slot_gate,
        expert_inputs,
        hidden,
        active,
        outputs,
    )
    return (branch.reshape(batch_size, length, model_width), kept)


def routing_backward(
    field, gain_vec, weight_router, weight_up, weight_down, kept, incoming_gradient
):
    (
        normed,
        prob_table,
        route_ids,
        slot_ids,
        slot_owner,
        slot_gate,
        expert_inputs,
        hidden,
        active,
        outputs,
    ) = kept
    batch_size, length, model_width = field.shape
    token_count = batch_size * length
    experts = weight_router.shape[1]
    slot_depth = 5 * token_count // 8
    flat_rows = field.reshape(token_count, model_width)
    upstream_rows = incoming_gradient.reshape(token_count, model_width)
    grad_slots = (slot_gate[:, None] * upstream_rows[slot_owner]).astype(jnp.bfloat16)
    grad_slots = grad_slots.reshape(experts, slot_depth, model_width)
    grad_down = jnp.einsum("ecf,ecd->efd", active, grad_slots, preferred_element_type=jnp.float32)
    grad_active = jnp.einsum(
        "ecd,efd->ecf", grad_slots, weight_down, preferred_element_type=jnp.float32
    )
    grad_hidden = (grad_active * gelu_slope(hidden)).astype(jnp.bfloat16)
    grad_up = jnp.einsum(
        "ecd,ecf->edf", expert_inputs, grad_hidden, preferred_element_type=jnp.float32
    )
    grad_inputs = jnp.einsum(
        "ecf,edf->ecd", grad_hidden, weight_up, preferred_element_type=jnp.float32
    )
    grad_inputs = grad_inputs.reshape(experts * slot_depth, model_width)
    grad_normed = grad_inputs[slot_ids[:, 0]] + grad_inputs[slot_ids[:, 1]]
    gate_first = jnp.sum(upstream_rows * outputs[slot_ids[:, 0]], axis=-1)
    gate_second = jnp.sum(upstream_rows * outputs[slot_ids[:, 1]], axis=-1)
    grad_gates = jnp.stack([gate_first, gate_second], axis=-1)
    grad_normed, grad_gates = lax.psum((grad_normed, grad_gates), "tensor")
    picks = (route_ids[:, :, None] == jnp.arange(experts, dtype=jnp.int32)).astype(jnp.float32)
    grad_probs = jnp.sum(grad_gates[:, :, None] * picks, axis=1)
    grad_logits = prob_table * (
        grad_probs - jnp.sum(prob_table * grad_probs, axis=-1, keepdims=True)
    )
    router_gradient = jnp.dot(normed.astype(jnp.float32).T, grad_logits, precision=highest)
    grad_normed = grad_normed + jnp.dot(
        grad_logits, weight_router.astype(jnp.float32).T, precision=highest
    )
    grad_field, grad_gain = norm_back(flat_rows, gain_vec, grad_normed)
    return (
        incoming_gradient + grad_field.reshape(field.shape),
        grad_gain,
        router_gradient,
        grad_up,
        grad_down,
    )


def shards(
    activations,
    image_live,
    expert_routes,
    attn_gain_one,
    qkv_weight_one,
    out_weight_one,
    first_feedforward_gain,
    up_weight_one,
    down_weight_one,
    attn_gain_two,
    qkv_weight_two,
    out_weight_two,
    moe_gain_two,
    router_weight,
    expert_up,
    expert_down,
    cotangent,
):
    layer_first = (
        attn_gain_one,
        qkv_weight_one,
        out_weight_one,
        first_feedforward_gain,
        up_weight_one,
        down_weight_one,
    )
    layer_second = (
        attn_gain_two,
        qkv_weight_two,
        out_weight_two,
        moe_gain_two,
        router_weight,
        expert_up,
        expert_down,
    )
    full_one = (
        lax.all_gather(layer_first[0], "fsdp", axis=0, tiled=True),
        lax.all_gather(layer_first[1], "fsdp", axis=1, tiled=True),
        lax.all_gather(layer_first[2], "fsdp", axis=1, tiled=True),
        lax.all_gather(layer_first[3], "fsdp", axis=0, tiled=True),
        lax.all_gather(layer_first[4], "fsdp", axis=0, tiled=True),
        lax.all_gather(layer_first[5], "fsdp", axis=1, tiled=True),
    )
    full_two = (
        lax.all_gather(layer_second[0], "fsdp", axis=0, tiled=True),
        lax.all_gather(layer_second[1], "fsdp", axis=1, tiled=True),
        lax.all_gather(layer_second[2], "fsdp", axis=1, tiled=True),
        lax.all_gather(layer_second[3], "fsdp", axis=0, tiled=True),
        lax.all_gather(layer_second[4], "fsdp", axis=0, tiled=True),
        lax.all_gather(layer_second[5], "fsdp", axis=1, tiled=True),
        lax.all_gather(layer_second[6], "fsdp", axis=2, tiled=True),
    )
    branch, kept_attn_one = attn_forward(
        activations, full_one[0].astype(jnp.float32), full_one[1], full_one[2]
    )
    after_one = activations + joined(branch)
    branch, kept_mlp = mlp_forward(
        after_one, full_one[3].astype(jnp.float32), full_one[4], full_one[5]
    )
    second = after_one + joined(branch)
    branch, kept_attn_two = attn_forward(
        second, full_two[0].astype(jnp.float32), full_two[1], full_two[2]
    )
    after_three = second + joined(branch)
    branch, kept_route = route_forward(
        after_three,
        full_two[3].astype(jnp.float32),
        full_two[4],
        full_two[5],
        full_two[6],
        expert_routes,
    )
    result = after_three + joined(branch)
    back_two = (
        lax.all_gather(layer_second[0], "fsdp", axis=0, tiled=True),
        lax.all_gather(layer_second[1], "fsdp", axis=1, tiled=True),
        lax.all_gather(layer_second[2], "fsdp", axis=1, tiled=True),
        lax.all_gather(layer_second[3], "fsdp", axis=0, tiled=True),
        lax.all_gather(layer_second[4], "fsdp", axis=0, tiled=True),
        lax.all_gather(layer_second[5], "fsdp", axis=1, tiled=True),
        lax.all_gather(layer_second[6], "fsdp", axis=2, tiled=True),
    )
    incoming_gradient = cotangent * image_live.astype(jnp.float32)[:, None, None]
    (
        incoming_gradient,
        fourth_gain_gradient,
        router_gradient,
        expert_up_gradient,
        expert_down_gradient,
    ) = routing_backward(
        after_three,
        back_two[3].astype(jnp.float32),
        back_two[4],
        back_two[5],
        back_two[6],
        kept_route,
        incoming_gradient,
    )
    incoming_gradient, grad_gain_c, grad_qkv_c, third_output_gradient = attn_backward(
        second,
        back_two[0].astype(jnp.float32),
        back_two[1],
        back_two[2],
        kept_attn_two,
        incoming_gradient,
    )
    sums_two = (
        lax.psum_scatter(grad_gain_c, "fsdp", scatter_dimension=0, tiled=True),
        lax.psum_scatter(grad_qkv_c, "fsdp", scatter_dimension=1, tiled=True),
        lax.psum_scatter(third_output_gradient, "fsdp", scatter_dimension=1, tiled=True),
        lax.psum_scatter(fourth_gain_gradient, "fsdp", scatter_dimension=0, tiled=True),
        lax.psum_scatter(router_gradient, "fsdp", scatter_dimension=0, tiled=True),
        lax.psum_scatter(expert_up_gradient, "fsdp", scatter_dimension=1, tiled=True),
        lax.psum_scatter(expert_down_gradient, "fsdp", scatter_dimension=2, tiled=True),
    )
    back_one = (
        lax.all_gather(layer_first[0], "fsdp", axis=0, tiled=True),
        lax.all_gather(layer_first[1], "fsdp", axis=1, tiled=True),
        lax.all_gather(layer_first[2], "fsdp", axis=1, tiled=True),
        lax.all_gather(layer_first[3], "fsdp", axis=0, tiled=True),
        lax.all_gather(layer_first[4], "fsdp", axis=0, tiled=True),
        lax.all_gather(layer_first[5], "fsdp", axis=1, tiled=True),
    )
    incoming_gradient, grad_gain_b, grad_up_b, grad_down_b = mlp_backward(
        after_one,
        back_one[3].astype(jnp.float32),
        back_one[4],
        back_one[5],
        kept_mlp,
        incoming_gradient,
    )
    incoming_gradient, grad_gain_a, grad_qkv_a, grad_out_a = attn_backward(
        activations,
        back_one[0].astype(jnp.float32),
        back_one[1],
        back_one[2],
        kept_attn_one,
        incoming_gradient,
    )
    sums_one = (
        lax.psum_scatter(grad_gain_a, "fsdp", scatter_dimension=0, tiled=True),
        lax.psum_scatter(grad_qkv_a, "fsdp", scatter_dimension=1, tiled=True),
        lax.psum_scatter(grad_out_a, "fsdp", scatter_dimension=1, tiled=True),
        lax.psum_scatter(grad_gain_b, "fsdp", scatter_dimension=0, tiled=True),
        lax.psum_scatter(grad_up_b, "fsdp", scatter_dimension=0, tiled=True),
        lax.psum_scatter(grad_down_b, "fsdp", scatter_dimension=1, tiled=True),
    )
    return (
        result,
        incoming_gradient,
        sums_one[0],
        sums_one[1],
        sums_one[2],
        sums_one[3],
        sums_one[4],
        sums_one[5],
        sums_two[0],
        sums_two[1],
        sums_two[2],
        sums_two[3],
        sums_two[4],
        sums_two[5],
        sums_two[6],
    )


def solution(mesh):
    return jax.shard_map(
        shards,
        mesh=mesh,
        in_specs=(
            P("fsdp", None, None),
            P("fsdp"),
            P("fsdp", None, None),
            P("fsdp"),
            P(None, "fsdp", "tensor"),
            P("tensor", "fsdp"),
            P("fsdp"),
            P("fsdp", "tensor"),
            P("tensor", "fsdp"),
            P("fsdp"),
            P(None, "fsdp", "tensor"),
            P("tensor", "fsdp"),
            P("fsdp"),
            P("fsdp", None),
            P(None, "fsdp", "tensor"),
            P(None, "tensor", "fsdp"),
            P("fsdp", None, None),
        ),
        out_specs=(
            P("fsdp", None, None),
            P("fsdp", None, None),
            P("fsdp"),
            P(None, "fsdp", "tensor"),
            P("tensor", "fsdp"),
            P("fsdp"),
            P("fsdp", "tensor"),
            P("tensor", "fsdp"),
            P("fsdp"),
            P(None, "fsdp", "tensor"),
            P("tensor", "fsdp"),
            P("fsdp"),
            P("fsdp", None),
            P(None, "fsdp", "tensor"),
            P(None, "tensor", "fsdp"),
        ),
        check_vma=False,
    )
```

profile of v0, /device:TPU:0, one launch (start us, length us, event | category | flops | bytes accessed | tf_op | source)
XLA Modules:
  0.0 1376.0 jit_solution(11531656225984385246)
XLA Ops:
  9.1 38.8 %all_gather.53 = bf16[3,768,192]{2,0,1:T(4,128)(2,1)S(1)} all-gather(bf16[3,96,192]{2,0,1:T(4,128)(2,1)S(1)} %copy.149), channel_id=1, replica_groups=mesh['fsdp'=8,'tensor'=4] {'fsdp'}, dimensions={1}, use_global_device_ids=true | all-gather | bytes 995328 | tf_op jit(solution)/shard_map/all_gather | solution.py:285
  51.2 19.9 %all-reduce.11 = (bf16[768]{0:T(1024)(128)(2,1)S(1)}, bf16[768]{0:T(1024)(128)(2,1)S(1)}, bf16[768]{0:T(1024)(128)(2,1)S(1)}, bf16[768]{0:T(1024)(128)(2,1)S(1)}) all-reduce(bf16[768]{0:T(1024)(128)(2,1)S(1)} %dynamic-update-slice, bf16[768]{0:T(1024)(128)(2,1)S(1)} %dynamic-update-slice.1, ...), channel_id=1, replica_groups=mesh['fsdp'=8,'tensor'=4] {'fsdp'}, use_global_device_ids=true, to_apply=%add.1 | all-reduce | flops 3072 | bytes 12288
  74.3 31.1 %all_gather.54 = bf16[192,768]{0,1:T(8,128)(2,1)S(1)} all-gather(bf16[192,96]{0,1:T(8,128)(2,1)S(1)} %copy.152), channel_id=1, replica_groups=mesh['fsdp'=8,'tensor'=4] {'fsdp'}, dimensions={1}, use_global_device_ids=true | all-gather | bytes 331776 | tf_op jit(solution)/shard_map/all_gather | solution.py:286
  108.8 29.6 %all-reduce.20.cloned.1.call-done = f32[1,197,768]{2,1,0:T(8,128)} async-done(((f32[1,197,768]{2,1,0:T(8,128)}), f32[1,197,768]{2,1,0:T(8,128)}) %all-reduce.20.cloned.1.call-update) | async-done | bytes 605200 | tf_op jit(solution)/shard_map/psum | solution.py:37
  139.9 9.0 all-gather.6.cloned.1.call-done
  150.7 40.3 %all-gather.8.cloned.1.call-done = bf16[768,768]{0,1:T(8,128)(2,1)} async-done(((bf16[768,96]{0,1:T(8,128)(2,1)}), bf16[768,768]{0,1:T(8,128)(2,1)}) %all-gather.8.cloned.1.call-update) | async-done | bytes 1179664 | tf_op jit(solution)/shard_map/all_gather | solution.py:289
  193.7 36.1 %all_gather.59 = bf16[3,768,192]{2,0,1:T(4,128)(2,1)S(1)} all-gather(bf16[3,96,192]{2,0,1:T(4,128)(2,1)S(1)} %copy.154), channel_id=1, replica_groups=mesh['fsdp'=8,'tensor'=4] {'fsdp'}, dimensions={1}, use_global_device_ids=true | all-gather | bytes 995328 | tf_op jit(solution)/shard_map/all_gather | solution.py:293
  231.9 31.1 %all_gather.60 = bf16[192,768]{0,1:T(8,128)(2,1)S(1)} all-gather(bf16[192,96]{0,1:T(8,128)(2,1)S(1)} %copy.157), channel_id=1, replica_groups=mesh['fsdp'=8,'tensor'=4] {'fsdp'}, dimensions={1}, use_global_device_ids=true | all-gather | bytes 331776 | tf_op jit(solution)/shard_map/all_gather | solution.py:294
  279.2 18.9 %all-gather = bf16[8,96,4]{1,2,0:T(4,128)(2,1)S(1)} all-gather(bf16[1,96,4]{1,2,0:T(4,128)(2,1)S(1)} %bitcast.295), channel_id=1, replica_groups=mesh['fsdp'=8,'tensor'=4] {'fsdp'}, dimensions={0}, use_global_device_ids=true | all-gather | bytes 6912 | tf_op jit(solution)/shard_map/all_gather | solution.py:296
  313.5 35.6 %all-gather.10.cloned.1.call-done = bf16[4,768,768]{2,1,0:T(8,128)(2,1)} async-done(((bf16[4,96,768]{2,1,0:T(8,128)(2,1)}), bf16[4,768,768]{2,1,0:T(8,128)(2,1)}) %all-gather.10.cloned.1.call-update) | async-done | bytes 4718608 | tf_op jit(solution)/shard_map/all_gather | solution.py:297
  353.4 75.8 %all-gather.12.cloned.1.call-done = bf16[4,768,768]{1,2,0:T(8,128)(2,1)} async-done(((bf16[4,768,96]{1,2,0:T(8,128)(2,1)}), bf16[4,768,768]{1,2,0:T(8,128)(2,1)}) %all-gather.12.cloned.1.call-update) | async-done | bytes 4718608 | tf_op jit(solution)/shard_map/all_gather | solution.py:298
  475.1 31.9 %all-reduce.26.cloned.1.call-done = f32[197,768]{1,0:T(8,128)} async-done(((f32[197,768]{1,0:T(8,128)}), f32[197,768]{1,0:T(8,128)}) %all-reduce.26.cloned.1.call-update) | async-done | bytes 605200 | tf_op jit(solution)/shard_map/psum | solution.py:227
  514.4 32.4 %all-reduce.28.cloned.1.call-done = f32[1,197,768]{2,1,0:T(8,128)} async-done(((f32[1,197,768]{2,1,0:T(8,128)}), f32[1,197,768]{2,1,0:T(8,128)}) %all-reduce.28.cloned.1.call-update) | async-done | bytes 605200 | tf_op jit(solution)/shard_map/psum | solution.py:41
  557.9 30.0 %all-reduce.30.cloned.1.call-done = f32[1,197,768]{2,1,0:T(8,128)} async-done(((f32[1,197,768]{2,1,0:T(8,128)}), f32[1,197,768]{2,1,0:T(8,128)}) %all-reduce.30.cloned.1.call-update) | async-done | bytes 605200 | tf_op jit(solution)/shard_map/psum | solution.py:41
  631.6 6.6 fusion.31
  640.3 45.4 %reduce-scatter.34.cloned.1.call-done = f32[96,192]{1,0:T(8,128)} async-done(((f32[768,192]{1,0:T(8,128)}), f32[96,192]{1,0:T(8,128)}) %reduce-scatter.34.cloned.1.call-update) | async-done | bytes 73744
  692.7 35.1 %all-reduce.9 = (f32[768]{0:T(1024)S(1)}, f32[768]{0:T(1024)S(1)}, f32[768]{0:T(1024)S(1)}, f32[768]{0:T(1024)S(1)}) all-reduce(f32[768]{0:T(1024)S(1)} %get-tuple-element.96, f32[768]{0:T(1024)S(1)} %get-tuple-element.94, f32[768]{0:T(1024)S(1)} %get-tuple-element.92, ...), channel_id=2, replica_groups=mesh['fsdp'=8,'tensor'=4] {'fsdp'}, use_global_device_ids=true, to_apply=%region_43.44.clone | all-reduce | flops 3072 | bytes 24576
  730.1 20.4 %reduce-scatter.30.cloned.1.call-done = f32[96,192]{1,0:T(8,128)} async-done(((f32[768,192]{1,0:T(8,128)}), f32[96,192]{1,0:T(8,128)}) %reduce-scatter.30.cloned.1.call-update) | async-done | bytes 73744
  752.1 67.8 %reduce-scatter.32.cloned.1.call-done = f32[96,576]{1,0:T(8,128)} async-done(((f32[768,576]{1,0:T(8,128)}), f32[96,576]{1,0:T(8,128)}) %reduce-scatter.32.cloned.1.call-update) | async-done | bytes 221200
  821.8 67.3 %reduce-scatter.28.cloned.1.call-done = f32[96,576]{1,0:T(8,128)} async-done(((f32[768,576]{1,0:T(8,128)}), f32[96,576]{1,0:T(8,128)}) %reduce-scatter.28.cloned.1.call-update) | async-done | bytes 221200
  891.0 71.0 %reduce-scatter.20.cloned.1.call-done = f32[96,768]{1,0:T(8,128)} async-done(((f32[768,768]{1,0:T(8,128)}), f32[96,768]{1,0:T(8,128)}) %reduce-scatter.20.cloned.1.call-update) | async-done | bytes 294928 | tf_op jit(solution)/shard_map/reduce_scatter | solution.py:392
  962.0 72.3 %reduce-scatter.22.cloned.1.call-done = f32[768,96]{0,1:T(8,128)} async-done(((f32[768,768]{0,1:T(8,128)}), f32[768,96]{0,1:T(8,128)}) %reduce-scatter.22.cloned.1.call-update) | async-done | bytes 294928 | tf_op jit(solution)/shard_map/reduce_scatter | solution.py:393
  1034.3 166.9 %reduce-scatter.24.cloned.1.call-done = f32[4,96,768]{2,1,0:T(8,128)} async-done(((f32[4,768,768]{2,1,0:T(8,128)}), f32[4,96,768]{2,1,0:T(8,128)}) %reduce-scatter.24.cloned.1.call-update) | async-done | bytes 1179664 | tf_op jit(solution)/shard_map/reduce_scatter | solution.py:360
  1201.2 166.7 %reduce-scatter.26.cloned.1.call-done = f32[4,768,96]{1,2,0:T(8,128)} async-done(((f32[4,768,768]{1,2,0:T(8,128)}), f32[4,768,96]{1,2,0:T(8,128)}) %reduce-scatter.26.cloned.1.call-update) | async-done | bytes 1179664 | tf_op jit(solution)/shard_map/reduce_scatter | solution.py:361
  (386 shorter events, 176.4 us)
Async XLA Ops:
  8.0 130.4 %all-reduce.20.cloned.1.call-start = ((), (), s32[]{:S(2)}) async-start(), calls=%async_computation.9 | async-start | bytes 1228800 | tf_op jit(solution)/shard_map/psum | solution.py:37
  107.4 41.5 %all-gather.6.cloned.1.call-start = ((), (), s32[]{:S(2)}) async-start(), calls=%async_computation.10 | async-start | bytes 1327104 | tf_op jit(solution)/shard_map/all_gather | solution.py:288
  108.0 83.0 %all-gather.8.cloned.1.call-start = ((), (), s32[]{:S(2)}) async-start(), calls=%async_computation.11 | async-start | bytes 1327104 | tf_op jit(solution)/shard_map/all_gather | solution.py:289
  108.6 154.5 %all-reduce.22.cloned.1.call-start = ((), (), s32[]{:S(2)}) async-start(), calls=%async_computation.12 | async-start | bytes 1228800 | tf_op jit(solution)/shard_map/psum | solution.py:37
  150.6 43.0 %copy-start.21 = (f32[197,768]{1,0:T(8,128)}, f32[197,768]{1,0:T(8,128)S(1)}, u32[]{:S(2)}) copy-start(f32[197,768]{1,0:T(8,128)S(1)} %fusion.65) | copy-start | bytes 1815556
  193.7 113.3 %all-reduce.24.cloned.1.call-start = ((), (), s32[]{:S(2)}) async-start(), calls=%async_computation.13 | async-start | bytes 1228800 | tf_op jit(solution)/shard_map/psum | solution.py:37
  267.9 81.2 %all-gather.10.cloned.1.call-start = ((), (), s32[]{:S(2)}) async-start(), calls=%async_computation.14 | async-start | bytes 5308416 | tf_op jit(solution)/shard_map/all_gather | solution.py:297
  268.4 160.7 %all-gather.12.cloned.1.call-start = ((), (), s32[]{:S(2)}) async-start(), calls=%async_computation.15 | async-start | bytes 5308416 | tf_op jit(solution)/shard_map/all_gather | solution.py:298
  269.2 237.8 %all-reduce.26.cloned.1.call-start = ((), (), s32[]{:S(2)}) async-start(), calls=%async_computation.16 | async-start | bytes 1228800 | tf_op jit(solution)/shard_map/psum | solution.py:227
  306.9 129.4 %copy-start.65 = (s32[1024]{0:T(1024)}, s32[1024]{0:T(1024)S(1)}, u32[]{:S(2)}) copy-start(s32[1024]{0:T(1024)S(1)} %get-tuple-element.149) | copy-start | bytes 12292
  306.9 131.2 %copy-start.66 = (s32[1024]{0:T(1024)}, s32[1024]{0:T(1024)S(1)}, u32[]{:S(2)}) copy-start(s32[1024]{0:T(1024)S(1)} %get-tuple-element.150) | copy-start | bytes 12292
  312.6 40.7 %copy-start.17 = (bf16[4,123,768]{2,1,0:T(8,128)(2,1)}, bf16[4,123,768]{2,1,0:T(8,128)(2,1)S(1)}, u32[]{:S(2)}) copy-start(bf16[4,123,768]{2,1,0:T(8,128)(2,1)S(1)} %reshape.855) | copy-start | bytes 2267140
  474.7 72.1 %all-reduce.28.cloned.1.call-start = ((), (), s32[]{:S(2)}) async-start(), calls=%async_computation.17 | async-start | bytes 1228800 | tf_op jit(solution)/shard_map/psum | solution.py:41
  513.0 74.9 %all-reduce.30.cloned.1.call-start = ((), (), s32[]{:S(2)}) async-start(), calls=%async_computation.18 | async-start | bytes 1228800 | tf_op jit(solution)/shard_map/psum | solution.py:41
  554.0 84.9 %reduce-scatter.36.cloned.1.call-start = ((), (), s32[]{:S(2)}) async-start(), calls=%async_computation.27 | async-start | bytes 442368
  556.5 129.2 %reduce-scatter.34.cloned.1.call-start = ((), (), s32[]{:S(2)}) async-start(), calls=%async_computation.26 | async-start | bytes 884736
  557.9 129.5 %all-reduce.32.cloned.1.call-start = ((), (), s32[]{:S(2)}) async-start(), calls=%async_computation.28 | async-start | bytes 2457600 | tf_op jit(solution)/shard_map/psum | solution.py:37
  594.3 156.1 %reduce-scatter.30.cloned.1.call-start = ((), (), s32[]{:S(2)}) async-start(), calls=%async_computation.24 | async-start | bytes 884736
  595.7 224.2 %reduce-scatter.32.cloned.1.call-start = ((), (), s32[]{:S(2)}) async-start(), calls=%async_computation.25 | async-start | bytes 2211840
  606.5 282.6 %reduce-scatter.28.cloned.1.call-start = ((), (), s32[]{:S(2)}) async-start(), calls=%async_computation.23 | async-start | bytes 2211840
  618.3 343.7 %reduce-scatter.20.cloned.1.call-start = ((), (), s32[]{:S(2)}) async-start(), calls=%async_computation.19 | async-start | bytes 2654208 | tf_op jit(solution)/shard_map/reduce_scatter | solution.py:392
  620.4 413.9 %reduce-scatter.22.cloned.1.call-start = ((), (), s32[]{:S(2)}) async-start(), calls=%async_computation.20 | async-start | bytes 2654208 | tf_op jit(solution)/shard_map/reduce_scatter | solution.py:393
  623.7 577.5 %reduce-scatter.24.cloned.1.call-start = ((), (), s32[]{:S(2)}) async-start(), calls=%async_computation.21 | async-start | bytes 10616832 | tf_op jit(solution)/shard_map/reduce_scatter | solution.py:360
  630.2 737.7 %reduce-scatter.26.cloned.1.call-start = ((), (), s32[]{:S(2)}) async-start(), calls=%async_computation.22 | async-start | bytes 10616832 | tf_op jit(solution)/shard_map/reduce_scatter | solution.py:361
  (77 other events, 554.4 us)
Sparse Core Ops, SparseCore 0:
  107.5 30.8 all-reduce.19
  193.8 32.0 all-reduce.21
  268.0 32.6 all-reduce.23
  474.8 32.1 all-reduce.25
  513.1 33.6 all-reduce.27
  554.1 33.8 all-reduce.29
  594.5 38.3 all-reduce.31
Sparse Core Ops, SparseCore 1:
  110.1 38.8 all-gather.5
  151.0 40.0 all-gather.7
  270.5 78.5 all-gather.9
  351.3 77.8 all-gather.11
  558.9 61.5 reduce-scatter.35
  624.2 61.4 reduce-scatter.33
  688.9 61.5 reduce-scatter.29
  754.2 65.7 reduce-scatter.31
  823.3 65.8 reduce-scatter.27
  893.6 68.4 reduce-scatter.19
  966.4 67.9 reduce-scatter.21
  1038.9 162.3 reduce-scatter.23
  1205.7 162.2 reduce-scatter.25
where the time goes:
time: 1390 us; the launch traced here: 1380 us
  waiting for transfers between devices  965 us (69%)
  blocking collectives  217 us (16%)
  local copies, waits for them, and re-layouts  89.6 us (6%)
  matrix products  60.6 us (4%)
  other arithmetic  23.3 us (2%)
  between operations  19.7 us (1%)
    unnamed x25, waiting for transfers between devices  203 us
    reduce_scatter x1, waiting for transfers between devices, shards(): lax.psum_scatter(expert_up_gradient, 'fsdp', scatter_dimension=1, tiled=T...  167 us
    reduce_scatter x1, waiting for transfers between devices, shards(): lax.psum_scatter(expert_down_gradient, 'fsdp', scatter_dimension=2, tiled...  167 us
    all_gather x1, waiting for transfers between devices, shards(): lax.all_gather(layer_second[6], 'fsdp', axis=2, tiled=True)  75.8 us
    reduce_scatter x1, waiting for transfers between devices, shards(): lax.psum_scatter(grad_down_b, 'fsdp', scatter_dimension=1, tiled=True)  72.3 us
    reduce_scatter x1, waiting for transfers between devices, shards(): lax.psum_scatter(grad_up_b, 'fsdp', scatter_dimension=0, tiled=True)  71 us
    psum x2, waiting for transfers between devices, back_joined(): return lax.psum(branch, 'tensor')  62.4 us
    unnamed x2, blocking collectives  55 us
  transfers between devices with their start and end apart: 20, of which 16 were waited for; matrix products, arithmetic and copies ran while one was open for 7% of the time, Pallas kernels for 0%

commit v1 on v0

v1 whole, which is shorter than its diff:
```python
import functools

import jax
import jax.numpy as jnp
from jax import lax
from jax.experimental import pallas as pl
from jax.experimental.pallas import tpu as pltpu
from jax.sharding import PartitionSpec as P

HD = 64
PLANES = 4
epsilon = 1e-06
root_half = 0.7071067811865476
inv_root_two_pi = 0.3989422804014327
highest = lax.Precision.HIGHEST
bf16 = jnp.bfloat16
f32 = jnp.float32


def nn(a, b):
    return lax.dot_general(a, b, (((1,), (0,)), ((), ())), preferred_element_type=f32)


def nt(a, b):
    return lax.dot_general(a, b, (((1,), (1,)), ((), ())), preferred_element_type=f32)


def tn(a, b):
    return lax.dot_general(a, b, (((0,), (0,)), ((), ())), preferred_element_type=f32)


def norm_parts(x):
    c = x - jnp.mean(x, axis=-1, keepdims=True)
    rs = lax.rsqrt(jnp.mean(c * c, axis=-1, keepdims=True) + epsilon)
    return c * rs, rs


def norm_pull(x, gain, dh):
    hat, rs = norm_parts(x)
    t = dh * gain
    mean_t = jnp.mean(t, axis=-1, keepdims=True)
    mean_th = jnp.mean(t * hat, axis=-1, keepdims=True)
    return rs * (t - mean_t - hat * mean_th), jnp.sum(dh * hat, axis=0, keepdims=True)


def join_halves(core, own, other):
    low = jnp.where(core == 0, own, other)
    high = jnp.where(core == 0, other, own)
    return jnp.concatenate([low, high], axis=1)


def split_halves(core, full):
    half = full.shape[1] // 2
    low, high = full[:, :half], full[:, half:]
    return jnp.where(core == 0, low, high), jnp.where(core == 0, high, low)


def row_of(index, shape):
    return lax.broadcasted_iota(jnp.int32, shape, 0) == index


def assemble(dst, me, refs, pick=()):
    parts = len(refs)
    rows = dst.shape[0] // (parts * PLANES)
    for a, ref in enumerate(refs):
        for m in range(PLANES):
            start = pl.multiple_of((me ^ (m * parts + a)) * rows, rows)
            dst[pl.ds(start, rows), :] = ref[(m,) + pick].astype(dst.dtype)


def scatter_blocks(src, me, refs, pick=()):
    parts = len(refs)
    rows = src.shape[0] // (parts * PLANES)
    for a, ref in enumerate(refs):
        for m in range(PLANES):
            start = pl.multiple_of((me ^ (m * parts + a)) * rows, rows)
            ref[(m,) + pick] = src[pl.ds(start, rows), :].astype(ref.dtype)


def head_tiles(y, head):
    at = 256 * head
    qk, vt = y[:, at : at + 128], y[:, at + 128 : at + 256]
    low = lax.broadcasted_iota(jnp.int32, qk.shape, 1) < HD
    q = jnp.where(low, qk, 0.0).astype(bf16)
    k = jnp.where(low, pltpu.roll(qk, HD, 1), 0.0).astype(bf16)
    v = jnp.where(low, 0.0, pltpu.roll(vt, HD, 1)).astype(bf16)
    return q, k, v


def probs_of(q, k, tokens):
    s = nt(q, k) * (HD**-0.5)
    s = jnp.where(lax.broadcasted_iota(jnp.int32, s.shape, 1) < tokens, s, -1e30)
    e = jnp.exp(s - jnp.max(s, axis=-1, keepdims=True))
    return e / jnp.sum(e, axis=-1, keepdims=True)


def attn_fwd_kernel(tokens, parts, gain_row, first, scal, *refs):
    me, core = scal[0], scal[1]
    refs = list(refs)
    x_ref = refs.pop(0)
    if first:
        x = x_ref[...]
    else:
        own, other, rows_ref = refs.pop(0), refs.pop(0), refs.pop(0)
        x = x_ref[...] + join_halves(core, own[...], other[...])
    blocks = [refs.pop(0) for _ in range(parts)]
    if first:
        keep_ref, send_ref, rows_ref, w = refs
    else:
        x_out, keep_ref, send_ref, w = refs
    assemble(w, me, blocks)
    model = w.shape[0]
    if first:
        eye = (
            lax.broadcasted_iota(jnp.int32, (8, 128), 0)
            == lax.broadcasted_iota(jnp.int32, (8, 128), 1)
        ).astype(bf16)
        rows_ref[...] = nt(eye, w[:, model:].astype(bf16))
    else:
        x_out[...] = x
    hat, _ = norm_parts(x)
    h = (hat * rows_ref[gain_row : gain_row + 1, :]).astype(bf16)
    y = nn(h, w[:, :model].astype(bf16))
    branch = jnp.zeros(x.shape, f32)
    for head in range(model // 256):
        q, k, v = head_tiles(y, head)
        p = probs_of(q, k, tokens).astype(bf16)
        o = nn(p, v).astype(bf16)
        at = 256 * head + 128
        branch += nt(o, w[:, at : at + 128].astype(bf16))
    keep, send = split_halves(core, branch)
    keep_ref[...] = keep
    send_ref[...] = send.astype(send_ref.dtype)


def mlp_fwd_kernel(parts, gain_row, scal, x_ref, own, other, rows_ref, *refs):
    me, core = scal[0], scal[1]
    blocks, (x_out, keep_ref, send_ref, up, down) = refs[:parts], refs[parts:]
    assemble(up, me, blocks, (0,))
    assemble(down, me, blocks, (1,))
    x = x_ref[...] + join_halves(core, own[...], other[...])
    x_out[...] = x
    hat, _ = norm_parts(x)
    h = (hat * rows_ref[gain_row : gain_row + 1, :]).astype(bf16)
    u = nn(h, up[...].astype(bf16))
    r = (0.5 * u * (1.0 + lax.erf(u * root_half))).astype(bf16)
    keep, send = split_halves(core, nt(r, down[...].astype(bf16)))
    keep_ref[...] = keep
    send_ref[...] = send.astype(send_ref.dtype)


def router_probs(h, rows_ref):
    logits = nt(h, rows_ref[...].astype(bf16))
    lane = lax.broadcasted_iota(jnp.int32, logits.shape, 1)
    logits = jnp.where(lane < PLANES, logits, -1e30)
    e = jnp.exp(logits - jnp.max(logits, axis=-1, keepdims=True))
    return e / jnp.sum(e, axis=-1, keepdims=True), lane


def routed(routes, lane):
    return (routes[:, 0:1] == lane) | (routes[:, 1:2] == lane)


def moe_pre_kernel(tokens, gain_row, scal, x_ref, own, other, rows_ref, routes, x_out, h_out, half_out):
    core = scal[1]
    x = x_ref[...] + join_halves(core, own[...], other[...])
    x_out[...] = x
    hat, _ = norm_parts(x)
    h = (hat * rows_ref[gain_row : gain_row + 1, :]).astype(bf16)
    probs, lane = router_probs(h, rows_ref)
    gates = jnp.where(routed(routes[...], lane), probs, 0.0).astype(bf16)
    eye = (
        lax.broadcasted_iota(jnp.int32, (8, 8), 0) == lax.broadcasted_iota(jnp.int32, (8, 8), 1)
    ).astype(bf16)
    gate_rows = nt(eye, gates)
    padded, model = x.shape
    half = model // 2
    live = lax.broadcasted_iota(jnp.int32, x.shape, 0) < tokens
    h = jnp.where(live, h.astype(f32), 0.0)
    wide = jnp.concatenate([gate_rows, jnp.zeros((8, half - padded), f32)], axis=1)
    block = jnp.concatenate([jnp.zeros((padded - 8, half), f32), wide], axis=0)
    low, high = h[:, :half] + block, h[:, half:] + block
    h_out[...] = jnp.concatenate([low, high], axis=1).astype(bf16)
    half_out[...] = jnp.where(core == 0, low, high).astype(bf16)


def moe_kernel(parts, scal, *refs):
    me, core, expert = scal[0], scal[1], scal[2]
    refs = list(refs)
    h_refs = [refs.pop(0) for _ in range(1 + 2 * (PLANES - 1))]
    g_refs = [refs.pop(0) for _ in range(1 + 2 * (PLANES - 1))]
    blocks = [refs.pop(0) for _ in range(parts)]
    y_keep, y_send, d_keep, d_send = [refs.pop(0) for _ in range(4)]
    grads = [refs.pop(0) for _ in range(parts)]
    up, down, hs, gs, rs, dus, dys, acc = refs
    assemble(up, me, blocks, (0,))
    assemble(down, me, blocks, (1,))
    for dst, src in ((hs, h_refs), (gs, g_refs)):
        dst[0] = src[0][...]
        for m in range(1, PLANES):
            dst[m] = join_halves(core, src[m][...], src[PLANES - 1 + m][...])
    padded, model = hs.shape[1:]
    half = model // 2

    def step(m, carry):
        h, g = hs[m], gs[m]
        rows = h.astype(f32)[padded - 8 :, :256]
        pick = row_of(expert, (8, 128)).astype(f32)
        gate = tn(rows, pick)[:padded, :1]
        u = nn(h, up[...].astype(bf16))
        cdf = 0.5 * (1.0 + lax.erf(u * root_half))
        r = (u * cdf).astype(bf16)
        t = nn(g, down[...].astype(bf16))
        slope = cdf + u * inv_root_two_pi * jnp.exp(-0.5 * u * u)
        du = (gate * t * slope).astype(bf16)
        rs[m] = r
        dus[m] = du
        dys[m] = (gate * g.astype(f32)).astype(bf16)
        dots = nt(jnp.ones((8, r.shape[1]), bf16), (r.astype(f32) * t).astype(bf16))
        dots = jnp.where(row_of(expert, dots.shape), dots, 0.0)
        y = gate * nt(r, down[...].astype(bf16))
        keep, send = split_halves(core, y)
        y_keep[m] = keep
        y_send[m] = send.astype(y_send.dtype)
        dh = nt(du, up[...].astype(bf16))
        wide = jnp.concatenate([dots, jnp.zeros((8, model - padded), f32)], axis=1)
        dh = dh + jnp.concatenate([jnp.zeros((padded - 8, model), f32), wide], axis=0)
        keep, send = split_halves(core, dh)
        d_keep[m] = keep
        d_send[m] = send.astype(d_send.dtype)
        return carry

    lax.fori_loop(0, PLANES, step, 0)
    flat = (PLANES * padded, model)
    acc[...] = tn(hs[...].reshape(flat), dus[...].reshape(flat))
    scatter_blocks(acc, me, grads, (0,))
    acc[...] = tn(dys[...].reshape(flat), rs[...].reshape(flat))
    scatter_blocks(acc, me, grads, (1,))


def plain_pull(x_ref, own, other, g_ref, rows_ref, small_ref, gain_row, core):
    dh = join_halves(core, own[...], other[...])
    dx, dgain = norm_pull(x_ref[...], rows_ref[gain_row : gain_row + 1, :], dh)
    small = small_ref[...] + jnp.where(row_of(gain_row, small_ref.shape), dgain, 0.0)
    return g_ref[...] + dx, small


def router_pull(tokens, x_ref, own, other, g_ref, rows_ref, routes, gain_row, core):
    dh = join_halves(core, own[...], other[...])
    padded, model = dh.shape
    gain = rows_ref[gain_row : gain_row + 1, :]
    hat, _ = norm_parts(x_ref[...])
    live = lax.broadcasted_iota(jnp.int32, dh.shape, 0) < tokens
    h = (hat * gain).astype(bf16)
    probs, lane = router_probs(h, rows_ref)
    dots = dh[padded - 8 :, :256]
    eye = (
        lax.broadcasted_iota(jnp.int32, (8, 8), 0) == lax.broadcasted_iota(jnp.int32, (8, 8), 1)
    ).astype(f32)
    dprobs = lax.dot_general(
        dots, eye, (((0,), (0,)), ((), ())), precision=highest, preferred_element_type=f32
    )[:padded]
    keep = routed(routes[...], lane) & (lax.broadcasted_iota(jnp.int32, lane.shape, 0) < tokens)
    dprobs = jnp.where(keep, dprobs, 0.0)
    dlogits = probs * (dprobs - jnp.sum(probs * dprobs, axis=-1, keepdims=True))
    small = lax.dot_general(
        dlogits, h.astype(f32), (((0,), (0,)), ((), ())), precision=highest, preferred_element_type=f32
    )
    router = jnp.where(lax.broadcasted_iota(jnp.int32, small.shape, 0) < PLANES, rows_ref[...], 0.0)
    dh = jnp.where(live, dh, 0.0) + lax.dot_general(
        dlogits, router, (((1,), (0,)), ((), ())), precision=highest, preferred_element_type=f32
    )
    dx, dgain = norm_pull(x_ref[...], gain, dh)
    small = small + jnp.where(row_of(gain_row, small.shape), dgain, 0.0)
    return g_ref[...] + dx, small


def attn_bwd_kernel(tokens, parts, rows_at, last, scal, *refs):
    me, core = scal[0], scal[1]
    refs = list(refs)
    x_up, own, other, g_ref, rows_ref, extra, x_ref = [refs.pop(0) for _ in range(7)]
    blocks = [refs.pop(0) for _ in range(parts)]
    g_out, small_out, keep_ref, send_ref = [refs.pop(0) for _ in range(4)]
    grads = [refs.pop(0) for _ in range(parts)]
    w, acc = refs
    assemble(w, me, blocks)
    up_row, gain_row = rows_at
    if last:
        g, small = plain_pull(x_up, own, other, g_ref, rows_ref, extra, up_row, core)
    else:
        g, small = router_pull(tokens, x_up, own, other, g_ref, rows_ref, extra, up_row, core)
    g_out[...] = g
    small_out[...] = small
    model = acc.shape[1]
    hat, _ = norm_parts(x_ref[...])
    h = (hat * rows_ref[gain_row : gain_row + 1, :]).astype(bf16)
    db = g.astype(bf16)
    y = nn(h, w[:, :model].astype(bf16))
    dh = jnp.zeros(g.shape, f32)
    left, right = [], []
    for head in range(model // 256):
        at = 256 * head
        q, k, v = head_tiles(y, head)
        p = probs_of(q, k, tokens)
        pb = p.astype(bf16)
        o = nn(pb, v).astype(bf16)
        wqk = w[:, at : at + 128].astype(bf16)
        wvo = w[:, at + 128 : at + 256].astype(bf16)
        do = nn(db, wvo)
        low = lax.broadcasted_iota(jnp.int32, do.shape, 1) < HD
        do = jnp.where(low, 0.0, do).astype(bf16)
        dp = nt(do, v)
        dv = tn(pb, do)
        ds = (p * (dp - jnp.sum(p * dp, axis=-1, keepdims=True))).astype(bf16)
        dq = nn(ds, k) * (HD**-0.5)
        dk = tn(ds, q) * (HD**-0.5)
        dqk = (dq + pltpu.roll(dk, HD, 1)).astype(bf16)
        dvt = pltpu.roll(dv, HD, 1).astype(bf16)
        dh += nt(dqk, wqk) + nt(dvt, wvo)
        left += [dqk, dvt]
        right += [jnp.zeros_like(o), o]
    keep, send = split_halves(core, dh)
    keep_ref[...] = keep
    send_ref[...] = send.astype(send_ref.dtype)
    acc[...] = tn(h, jnp.concatenate(left, axis=1)) + tn(db, jnp.concatenate(right, axis=1))
    scatter_blocks(acc, me, grads)


def mlp_bwd_kernel(parts, rows_at, scal, x_up, own, other, g_ref, rows_ref, extra, x_ref, *refs):
    me, core = scal[0], scal[1]
    refs = list(refs)
    blocks = [refs.pop(0) for _ in range(parts)]
    g_out, small_out, keep_ref, send_ref = [refs.pop(0) for _ in range(4)]
    grads = [refs.pop(0) for _ in range(parts)]
    up, down, acc = refs
    assemble(up, me, blocks, (0,))
    assemble(down, me, blocks, (1,))
    up_row, gain_row = rows_at
    g, small = plain_pull(x_up, own, other, g_ref, rows_ref, extra, up_row, core)
    g_out[...] = g
    small_out[...] = small
    hat, _ = norm_parts(x_ref[...])
    h = (hat * rows_ref[gain_row : gain_row + 1, :]).astype(bf16)
    dm = g.astype(bf16)
    u = nn(h, up[...].astype(bf16))
    cdf = 0.5 * (1.0 + lax.erf(u * root_half))
    r = (u * cdf).astype(bf16)
    slope = cdf + u * inv_root_two_pi * jnp.exp(-0.5 * u * u)
    du = (nn(dm, down[...].astype(bf16)) * slope).astype(bf16)
    keep, send = split_halves(core, nt(du, up[...].astype(bf16)))
    keep_ref[...] = keep
    send_ref[...] = send.astype(send_ref.dtype)
    acc[...] = tn(h, du)
    scatter_blocks(acc, me, grads, (0,))
    acc[...] = tn(dm, r)
    scatter_blocks(acc, me, grads, (1,))


def final_kernel(tokens, gain_row, scal, x_ref, own, other, g_ref, rows_ref, extra, g_out, *refs):
    me, core = scal[0], scal[1]
    grads, acc = refs[:-1], refs[-1]
    g, small = plain_pull(x_ref, own, other, g_ref, rows_ref, extra, gain_row, core)
    g_out[...] = g[:tokens]
    eye = (
        lax.broadcasted_iota(jnp.int32, (8, 128), 0) == lax.broadcasted_iota(jnp.int32, (8, 128), 1)
    ).astype(f32)
    acc[...] = lax.dot_general(
        small, eye, (((0,), (0,)), ((), ())), precision=highest, preferred_element_type=f32
    )
    scatter_blocks(acc, me, grads)


def run(kernel, scal, ins, outs, scratch, flops):
    vmem = pl.BlockSpec(memory_space=pltpu.VMEM)
    size = lambda s: s.size * s.dtype.itemsize
    return pl.pallas_call(
        kernel,
        out_shape=outs,
        in_specs=[pl.BlockSpec(memory_space=pltpu.SMEM)] + [vmem] * len(ins),
        out_specs=[vmem] * len(outs),
        scratch_shapes=scratch,
        compiler_params=pltpu.CompilerParams(vmem_limit_bytes=48 * 2**20),
        cost_estimate=pl.CostEstimate(
            flops=int(flops),
            bytes_accessed=int(sum(size(a) for a in ins) + sum(size(o) for o in outs)),
            transcendentals=0,
        ),
    )(scal, *ins)


def shape(dims, kind):
    return jax.ShapeDtypeStruct(tuple(dims), kind)


def tie(value, *after):
    return lax.optimization_barrier((value,) + after)[0]


def shards(
    fsdp,
    tensor,
    activations,
    image_live,
    expert_routes,
    attn_gain_one,
    qkv_weight_one,
    out_weight_one,
    first_feedforward_gain,
    up_weight_one,
    down_weight_one,
    attn_gain_two,
    qkv_weight_two,
    out_weight_two,
    moe_gain_two,
    router_weight,
    expert_up,
    expert_down,
    cotangent,
):
    parts = fsdp // PLANES
    tokens, model = activations.shape[1:]
    padded = -(-(tokens + 8) // 16) * 16
    half = model // 2
    rows = model // fsdp
    heads = qkv_weight_one.shape[2] // HD
    hidden = up_weight_one.shape[1]
    held = bf16 if rows % 16 == 0 else f32
    me = lax.axis_index("fsdp")
    place = lax.axis_index("tensor")
    core, plane = place % 2, me // parts
    scal = jnp.stack([me, core, plane, place]).astype(jnp.int32)

    def across(value, k):
        return lax.ppermute(value, "fsdp", [(i, i ^ k) for i in range(fsdp)])

    def over(value, k):
        return lax.ppermute(value, "tensor", [(i, i ^ k) for i in range(tensor)])

    def spread(stacked):
        arrays, bit = [stacked], 1
        while bit < parts:
            arrays += [across(a, bit) for a in arrays]
            bit *= 2
        return arrays

    def gather_planes(block):
        return jnp.stack([block] + [across(block, m * parts) for m in range(1, PLANES)])

    def fold(arrays):
        arrays, bit = list(arrays), parts // 2
        while bit:
            for a in range(bit):
                arrays[a] = arrays[a].astype(f32) + across(arrays[a + bit].astype(bf16), bit).astype(f32)
            bit //= 2
        return arrays[0]

    def reduce_planes(stacked):
        total = stacked[0].astype(f32)
        for m in range(1, PLANES):
            total = total + across(stacked[m].astype(bf16), m * parts).astype(f32)
        return total

    def pair(total):
        low = total.astype(bf16)
        total = low.astype(f32) + over(low, 2).astype(f32)
        return total, over(total, 1)

    def joined(keep, send):
        return pair(keep + over(send, 1))

    def attn_pack(qkv, out):
        by_head = jnp.moveaxis(qkv.reshape(3, rows, heads, HD), 0, 2)
        out = out.reshape(heads, HD, rows).transpose(2, 0, 1)[:, :, None]
        return jnp.concatenate([by_head, out], axis=2).reshape(rows, heads * 4 * HD)

    def attn_unpack(grad):
        grad = grad.reshape(rows, heads, 4, HD)
        qkv = jnp.moveaxis(grad[:, :, :3], 2, 0).reshape(3, rows, heads * HD)
        return qkv, grad[:, :, 3].transpose(1, 2, 0).reshape(heads * HD, rows)

    smalls = jnp.concatenate(
        [
            router_weight,
            attn_gain_one[:, None],
            first_feedforward_gain[:, None],
            attn_gain_two[:, None],
            moe_gain_two[:, None],
        ],
        axis=1,
    )
    smalls = jnp.pad(smalls, ((0, 0), (0, 128 - smalls.shape[1])))
    one = jnp.concatenate([attn_pack(qkv_weight_one, out_weight_one), smalls], axis=1)
    one = gather_planes(one)
    w_one = spread(one)
    mlp = jnp.stack([up_weight_one, down_weight_one.T])
    mlp = gather_planes(tie(mlp, one))
    w_mlp = spread(mlp)
    two = gather_planes(tie(attn_pack(qkv_weight_two, out_weight_two), mlp))
    w_two = spread(two)
    experts = jnp.stack([expert_up, jnp.swapaxes(expert_down, 1, 2)], axis=1)
    experts = tie(experts, two)
    mine = [lax.dynamic_index_in_dim(experts, plane ^ m, 0, keepdims=False) for m in range(PLANES)]
    mine = jnp.stack([mine[0]] + [across(mine[m], m * parts) for m in range(1, PLANES)])
    w_moe = spread(mine)

    def image_blocks(own, own_half):
        near = [across(own_half, m * parts) for m in range(1, PLANES)]
        return [own] + near + [over(n, 1) for n in near]

    pad = ((0, padded - tokens), (0, 0))
    stream0 = jnp.pad(activations[0], pad)
    grad3 = jnp.pad(cotangent[0] * image_live[0].astype(f32), pad)
    routes = jnp.pad(expert_routes[0], pad, constant_values=-1)
    grad_low = tie(grad3.astype(bf16), mine)
    grad_half = jnp.where(core == 0, grad_low[:, :half], grad_low[:, half:])
    g_blocks = image_blocks(grad_low, grad_half)

    stream = shape((padded, model), f32)
    pieces = [shape((padded, half), f32)] * 2
    wide = pltpu.VMEM((model, model + 128), held)
    square = pltpu.VMEM((model, model), held)
    total = pltpu.VMEM((model, model), f32)
    unit = 2 * padded * model * model

    keep, send, small_rows = run(
        functools.partial(attn_fwd_kernel, tokens, parts, 4, True),
        scal,
        [stream0] + w_one,
        pieces + [shape((8, model), f32)],
        [wide],
        3 * unit,
    )
    own, other = joined(keep, send)
    stream1, keep, send = run(
        functools.partial(mlp_fwd_kernel, parts, 5),
        scal,
        [stream0, own, other, small_rows] + w_mlp,
        [stream] + pieces,
        [square, square],
        2 * unit,
    )
    own, other = joined(keep, send)
    stream2, keep, send = run(
        functools.partial(attn_fwd_kernel, tokens, parts, 6, False),
        scal,
        [stream1, own, other, small_rows] + w_two,
        [stream] + pieces,
        [square],
        3 * unit,
    )
    own, other = joined(keep, send)
    stream3, h_full, h_half = run(
        functools.partial(moe_pre_kernel, tokens, 7),
        scal,
        [stream2, own, other, small_rows, routes],
        [stream, shape((padded, model), bf16), shape((padded, half), bf16)],
        [],
        unit / 50,
    )
    h_blocks = image_blocks(h_full, h_half)
    images = pltpu.VMEM((PLANES, padded, model), bf16)
    image_hidden = pltpu.VMEM((PLANES, padded, hidden), bf16)
    block_pieces = [shape((PLANES, padded, half), f32), shape((PLANES, padded, half), bf16)]
    y_keep, y_send, d_keep, d_send, *expert_grads = run(
        functools.partial(moe_kernel, parts),
        scal,
        h_blocks + g_blocks + w_moe,
        block_pieces * 2 + [shape((PLANES, 2, rows, hidden), bf16)] * parts,
        [square, square, images, images, image_hidden, image_hidden, images, total],
        24 * unit,
    )

    def home(keep, send):
        summed = keep + over(send, 1).astype(f32)
        return pair(reduce_planes(summed))

    own, other = home(d_keep, d_send)
    block_grads = [shape((PLANES, rows, model), bf16)] * parts
    grad2, small, keep, send, *two_grads = run(
        functools.partial(attn_bwd_kernel, tokens, parts, (7, 6), False),
        scal,
        [stream3, own, other, grad3, small_rows, routes, stream2] + w_two,
        [stream, shape((8, model), f32)] + pieces + block_grads,
        [square, total],
        8 * unit,
    )
    own, other = joined(keep, send)
    y_keep, y_send = lax.optimization_barrier((y_keep, y_send, keep))[:2]
    y_own, y_other = home(y_keep, y_send)
    expert_sum = fold(expert_grads)
    grad1, small, keep, send, *mlp_grads = run(
        functools.partial(mlp_bwd_kernel, parts, (6, 5)),
        scal,
        [stream2, own, other, grad2, small_rows, small, stream1] + w_mlp,
        [stream, shape((8, model), f32)]
        + pieces
        + [shape((PLANES, 2, rows, hidden), bf16)] * parts,
        [square, square, total],
        5 * unit,
    )
    own, other = joined(keep, send)
    grad0, small, keep, send, *one_grads = run(
        functools.partial(attn_bwd_kernel, tokens, parts, (5, 4), True),
        scal,
        [stream1, own, other, grad1, small_rows, small, stream0] + w_one,
        [stream, shape((8, model), f32)] + pieces + block_grads,
        [wide, total],
        8 * unit,
    )
    own, other = joined(keep, send)
    input_grad, *small_grads = run(
        functools.partial(final_kernel, tokens, 4),
        scal,
        [stream0, own, other, grad0, small_rows, small],
        [shape((tokens, model), f32)] + [shape((PLANES, rows, 128), bf16)] * parts,
        [pltpu.VMEM((model, 128), f32)],
        unit / 50,
    )

    low = jnp.where(core == 0, y_own, y_other)
    high = jnp.where(core == 0, y_other, y_own)
    result = (stream3 + jnp.concatenate([low, high], axis=1))[:tokens]

    came = [expert_sum[0]]
    for m in range(1, PLANES):
        came.append(across(expert_sum[m].astype(bf16), m * parts).astype(f32))
    bit0, bit1 = plane % 2 == 1, plane // 2 == 1

    def of_expert(x):
        a, b = jnp.where(bit0, came[x ^ 1], came[x]), jnp.where(bit0, came[x ^ 3], came[x ^ 2])
        return jnp.where(bit1, b, a)

    by_expert = jnp.stack([of_expert(x) for x in range(PLANES)])
    two_sum = reduce_planes(fold(two_grads))
    mlp_sum = reduce_planes(fold(mlp_grads))
    one_sum = reduce_planes(fold(one_grads))
    small_sum = reduce_planes(fold(small_grads))
    qkv_one, out_one = attn_unpack(one_sum)
    qkv_two, out_two = attn_unpack(two_sum)
    return (
        result[None],
        input_grad[None],
        small_sum[:, 4],
        qkv_one,
        out_one,
        small_sum[:, 5],
        mlp_sum[0],
        mlp_sum[1].T,
        small_sum[:, 6],
        qkv_two,
        out_two,
        small_sum[:, 7],
        small_sum[:, :PLANES],
        by_expert[:, 0],
        jnp.swapaxes(by_expert[:, 1], 1, 2),
    )


def solution(mesh):
    return jax.shard_map(
        functools.partial(shards, mesh.shape["fsdp"], mesh.shape["tensor"]),
        mesh=mesh,
        in_specs=(
            P("fsdp", None, None),
            P("fsdp"),
            P("fsdp", None, None),
            P("fsdp"),
            P(None, "fsdp", "tensor"),
            P("tensor", "fsdp"),
            P("fsdp"),
            P("fsdp", "tensor"),
            P("tensor", "fsdp"),
            P("fsdp"),
            P(None, "fsdp", "tensor"),
            P("tensor", "fsdp"),
            P("fsdp"),
            P("fsdp", None),
            P(None, "fsdp", "tensor"),
            P(None, "tensor", "fsdp"),
            P("fsdp", None, None),
        ),
        out_specs=(
            P("fsdp", None, None),
            P("fsdp", None, None),
            P("fsdp"),
            P(None, "fsdp", "tensor"),
            P("tensor", "fsdp"),
            P("fsdp"),
            P("fsdp", "tensor"),
            P("tensor", "fsdp"),
            P("fsdp"),
            P(None, "fsdp", "tensor"),
            P("tensor", "fsdp"),
            P("fsdp"),
            P("fsdp", None),
            P(None, "fsdp", "tensor"),
            P(None, "tensor", "fsdp"),
        ),
        check_vma=False,
    )
```

time: 1390 us -> 357 us (0.26)
  waiting for transfers between devices: 965 us -> 173 us
  blocking collectives: 217 us -> 0 us
  starting transfers between devices: 1.32 us -> 90.1 us
  local copies, waits for them, and re-layouts: 89.6 us -> 28.8 us
  matrix products: 60.6 us -> 0 us
  Pallas kernels: 0 us -> 42.6 us
  between operations: 19.7 us -> 2.15 us
    reduce_scatter x4 -> x0, waiting for transfers between devices: 477 us -> none  [the longest x1 167 us: shards(): lax.psum_scatter(expert_up_gradient, 'fsdp', scatter_dimension=1, tiled=T...]
    unnamed x25 -> x0, waiting for transfers between devices: 203 us -> none
    ppermute x0 -> x78, waiting for transfers between devices: none -> 173 us  [the longest x48 153 us: across(): return lax.ppermute(value, 'fsdp', [(i, i ^ k) for i in range(fsdp)])]
    all_gather x4 -> x0, waiting for transfers between devices: 161 us -> none  [the longest x1 75.8 us: shards(): lax.all_gather(layer_second[6], 'fsdp', axis=2, tiled=True)]
    all_gather x5 -> x0, blocking collectives: 156 us -> none  [the longest x1 38.8 us: shards(): lax.all_gather(layer_first[1], 'fsdp', axis=1, tiled=True)]
    psum x7 -> x0, waiting for transfers between devices: 124 us -> none  [the longest x2 62.4 us: back_joined(): return lax.psum(branch, 'tensor')]
    ppermute x0 -> x78, starting transfers between devices: none -> 90.1 us  [the longest x48 74.9 us: across(): return lax.ppermute(value, 'fsdp', [(i, i ^ k) for i in range(fsdp)])]
    dot_general x34 -> x0, matrix products: 55.6 us -> none  [the longest x1 6.56 us: routing_backward(): jnp.einsum('ecf,ecd->efd', active, grad_slots, preferred_element_type=jnp...]
  transfers between devices with their start and end apart: 20 -> 78, of which waited for: 16 -> 32; matrix products, arithmetic and copies ran while one was open for 7% -> 9% of each run, Pallas kernels for 0% -> 8%
where the time goes in v1:
time: 357 us; the launch traced here: 356 us
  waiting for transfers between devices  173 us (48%)
  starting transfers between devices  90.1 us (25%)
  Pallas kernels  42.6 us (12%)
  local copies, waits for them, and re-layouts  28.8 us (8%)
  other arithmetic  18.9 us (5%)
    ppermute x48, waiting for transfers between devices, across(): return lax.ppermute(value, 'fsdp', [(i, i ^ k) for i in range(fsdp)])  153 us
    ppermute x48, starting transfers between devices, across(): return lax.ppermute(value, 'fsdp', [(i, i ^ k) for i in range(fsdp)])  74.9 us
    pallas_call x9, Pallas kernels, run(): pl.pallas_call(kernel, out_shape=outs, in_specs=[pl.BlockSpec(memory_spac...  42.6 us
    ppermute x30, waiting for transfers between devices, over(): return lax.ppermute(value, 'tensor', [(i, i ^ k) for i in range(tensor)])  20.1 us
    unnamed x85, local copies, waits for them, and re-layouts  18.9 us
    ppermute x30, starting transfers between devices, over(): return lax.ppermute(value, 'tensor', [(i, i ^ k) for i in range(tensor)])  15.2 us
  transfers between devices with their start and end apart: 78, of which 32 were waited for; matrix products, arithmetic and copies ran while one was open for 9% of the time, Pallas kernels for 8%

profile of v1, /device:TPU:0, one launch (start us, length us, event | category | flops | bytes accessed | tf_op | source)
XLA Modules:
  0.0 355.7 jit_solution(18374412551286346079)
XLA Ops:
  3.7 5.1 %collective-permute-start.2 = (bf16[96,896]{1,0:T(8,128)(2,1)S(1)}, bf16[96,896]{1,0:T(8,128)(2,1)S(1)}, u32[]{:S(2)}, u32[]{:S(2)}) collective-permute-start(bf16[96,896]{1,0:T(8,128)(2,1)S(1)} %get-tuple-element.201), channel_id=1, source_target_pairs={{0,24},{4,28},{8,16},{12,20},{16,8},{20,12},{24,0},{28,4},{1,25},{... | collective-permute-start | bytes 516104 | tf_op jit(solution)/shard_map/ppermute | solution.py:434
  9.4 4.7 %collective-permute-done.2 = bf16[96,896]{1,0:T(8,128)(2,1)S(1)} collective-permute-done((bf16[96,896]{1,0:T(8,128)(2,1)S(1)}, bf16[96,896]{1,0:T(8,128)(2,1)S(1)}, u32[]{:S(2)}, u32[]{:S(2)}) %collective-permute-start.2) | collective-permute-done | bytes 172064 | tf_op jit(solution)/shard_map/ppermute | solution.py:434
  14.1 9.3 %collective-permute-done.1 = bf16[96,896]{1,0:T(8,128)(2,1)S(1)} collective-permute-done((bf16[96,896]{1,0:T(8,128)(2,1)S(1)}, bf16[96,896]{1,0:T(8,128)(2,1)S(1)}, u32[]{:S(2)}, u32[]{:S(2)}) %collective-permute-start.1) | collective-permute-done | bytes 172064 | tf_op jit(solution)/shard_map/ppermute | solution.py:434
  29.7 10.3 %collective-permute-done.3.refs_2_.refs_8_ = bf16[4,96,896]{2,1,0:T(8,128)(2,1)S(1)} collective-permute-done((bf16[4,96,896]{2,1,0:T(8,128)(2,1)S(1)}, bf16[4,96,896]{2,1,0:T(8,128)(2,1)S(1)}, u32[]{:S(2)}, u32[]{:S(2)}) %collective-permute-start.3) | collective-permute-done | bytes 688160 | tf_op jit(solution)/shard_map/ppermute | solution.py:434
  43.0 7.8 %collective-permute-done.8 = bf16[2,96,768]{2,1,0:T(8,128)(2,1)S(1)} collective-permute-done((bf16[2,96,768]{2,1,0:T(8,128)(2,1)S(1)}, bf16[2,96,768]{2,1,0:T(8,128)(2,1)S(1)}, u32[]{:S(2)}, u32[]{:S(2)}) %collective-permute-start.8) | collective-permute-done | bytes 294944 | tf_op jit(solution)/shard_map/ppermute | solution.py:434
  58.0 19.6 %collective-permute-done.10.refs_1_ = bf16[4,2,96,768]{3,2,1,0:T(8,128)(2,1)S(1)} collective-permute-done((bf16[4,2,96,768]{3,2,1,0:T(8,128)(2,1)S(1)}, bf16[4,2,96,768]{3,2,1,0:T(8,128)(2,1)S(1)}, u32[]{:S(2)}, u32[]{:S(2)}) %collective-permute-start.10) | collective-permute-done | bytes 1179680 | tf_op jit(solution)/shard_map/ppermute | solution.py:434
  89.9 5.8 %collective-permute-done.15 = bf16[96,768]{1,0:T(8,128)(2,1)S(1)} collective-permute-done((bf16[96,768]{1,0:T(8,128)(2,1)S(1)}, bf16[96,768]{1,0:T(8,128)(2,1)S(1)}, u32[]{:S(2)}, u32[]{:S(2)}) %collective-permute-start.15) | collective-permute-done | bytes 147488 | tf_op jit(solution)/shard_map/ppermute | solution.py:434
  102.5 8.7 %collective-permute-done.17.refs_5_.refs_8_ = bf16[4,96,768]{2,1,0:T(8,128)(2,1)S(1)} collective-permute-done((bf16[4,96,768]{2,1,0:T(8,128)(2,1)S(1)}, bf16[4,96,768]{2,1,0:T(8,128)(2,1)S(1)}, u32[]{:S(2)}, u32[]{:S(2)}) %collective-permute-start.17) | collective-permute-done | bytes 589856 | tf_op jit(solution)/shard_map/ppermute | solution.py:434
  118.4 7.5 %collective-permute-done.28 = bf16[2,96,768]{2,1,0:T(8,128)(2,1)S(1)} collective-permute-done((bf16[2,96,768]{2,1,0:T(8,128)(2,1)S(1)}, bf16[2,96,768]{2,1,0:T(8,128)(2,1)S(1)}, u32[]{:S(2)}, u32[]{:S(2)}) %collective-permute-start.28) | collective-permute-done | bytes 294944 | tf_op jit(solution)/shard_map/ppermute | solution.py:434
  139.7 5.1 %collective-permute-done.30.refs_8_ = bf16[208,384]{1,0:T(8,128)(2,1)} collective-permute-done((bf16[208,384]{1,0:T(8,128)(2,1)S(1)}, bf16[208,384]{1,0:T(8,128)(2,1)}, u32[]{:S(2)}, u32[]{:S(2)}) %collective-permute-start.30) | collective-permute-done | bytes 159776 | tf_op jit(solution)/shard_map/ppermute | solution.py:434
  144.9 5.3 %collective-permute-done.31.refs_9_ = bf16[208,384]{1,0:T(8,128)(2,1)} collective-permute-done((bf16[208,384]{1,0:T(8,128)(2,1)S(1)}, bf16[208,384]{1,0:T(8,128)(2,1)}, u32[]{:S(2)}, u32[]{:S(2)}) %collective-permute-start.31) | collective-permute-done | bytes 159776 | tf_op jit(solution)/shard_map/ppermute | solution.py:434
  156.8 5.1 %collective-permute-done.21.refs_1_ = bf16[208,384]{1,0:T(8,128)(2,1)S(1)} collective-permute-done((bf16[208,384]{1,0:T(8,128)(2,1)S(1)}, bf16[208,384]{1,0:T(8,128)(2,1)S(1)}, u32[]{:S(2)}, u32[]{:S(2)}) %collective-permute-start.21) | collective-permute-done | bytes 159776 | tf_op jit(solution)/shard_map/ppermute | solution.py:434
  161.9 5.3 %collective-permute-done.22.refs_2_ = bf16[208,384]{1,0:T(8,128)(2,1)S(1)} collective-permute-done((bf16[208,384]{1,0:T(8,128)(2,1)S(1)}, bf16[208,384]{1,0:T(8,128)(2,1)S(1)}, u32[]{:S(2)}, u32[]{:S(2)}) %collective-permute-start.22) | collective-permute-done | bytes 159776 | tf_op jit(solution)/shard_map/ppermute | solution.py:434
  168.8 12.7 %shard_map.284 = (f32[4,208,384]{2,1,0:T(8,128)}, bf16[4,208,384]{2,1,0:T(8,128)(2,1)S(1)}, f32[4,208,384]{2,1,0:T(8,128)}, bf16[4,208,384]{2,1,0:T(8,128)(2,1)S...) custom-call(s32[4]{0:T(128)S(1)} %pad_add_fusion.scal, ...), custom_call_target="tpu_custom_call" | custom-call | flops 5888802816 | bytes 11108352 | tf_op jit(solution)/shard_map/pallas_call | solution.py:376
  193.9 9.5 %collective-permute-done.39 = bf16[208,384]{1,0:T(8,128)(2,1)S(1)} collective-permute-done((bf16[208,384]{1,0:T(8,128)(2,1)S(1)}, bf16[208,384]{1,0:T(8,128)(2,1)S(1)}, u32[]{:S(2)}, u32[]{:S(2)}) %collective-permute-start.39) | collective-permute-done | bytes 159776 | tf_op jit(solution)/shard_map/ppermute | solution.py:434
  221.6 7.3 %shard_map.285 = (f32[208,768]{1,0:T(8,128)S(1)}, f32[8,768]{1,0:T(8,128)S(1)}, f32[208,384]{1,0:T(8,128)S(1)}, f32[208,384]{1,0:T(8,128)S(1)}, bf16[4,96,768]{2...) custom-call(s32[4]{0:T(128)S(1)} %pad_add_fusion.scal, f32[208,768]{1,0:T(8,128)S(1)} %copy-done.9, ...), custom_call_target="tpu_custom_call" | custom-call | flops 1962934272 | bytes 6243968 | tf_op jit(solution)/shard_map/pallas_call | solution.py:376
  229.5 7.9 %collective-permute-done.76 = bf16[2,96,768]{2,1,0:T(8,128)(2,1)S(1)} collective-permute-done((bf16[2,96,768]{2,1,0:T(8,128)(2,1)}, bf16[2,96,768]{2,1,0:T(8,128)(2,1)S(1)}, u32[]{:S(2)}, u32[]{:S(2)}) %collective-permute-start.76) | collective-permute-done | bytes 294944 | tf_op jit(solution)/shard_map/ppermute | solution.py:434
  244.9 5.4 %collective-permute-done.70 = bf16[4,96,768]{2,1,0:T(8,128)(2,1)S(1)} collective-permute-done((bf16[4,96,768]{2,1,0:T(8,128)(2,1)S(1)}, bf16[4,96,768]{2,1,0:T(8,128)(2,1)S(1)}, u32[]{:S(2)}, u32[]{:S(2)}) %collective-permute-start.70) | collective-permute-done | bytes 589856 | tf_op jit(solution)/shard_map/ppermute | solution.py:434
  256.3 5.5 %shard_map.286 = (f32[208,768]{1,0:T(8,128)S(1)}, f32[8,768]{1,0:T(8,128)S(1)}, f32[208,384]{1,0:T(8,128)S(1)}, f32[208,384]{1,0:T(8,128)}, bf16[4,2,96,768]{3,2...) custom-call(s32[4]{0:T(128)S(1)} %pad_add_fusion.scal, f32[208,768]{1,0:T(8,128)S(1)} %copy-done.3, ...), custom_call_target="tpu_custom_call" | custom-call | flops 1226833920 | bytes 8626176 | tf_op jit(solution)/shard_map/pallas_call | solution.py:376
  272.6 7.4 %collective-permute-done.45 = bf16[208,384]{1,0:T(8,128)(2,1)} collective-permute-done((bf16[208,384]{1,0:T(8,128)(2,1)}, bf16[208,384]{1,0:T(8,128)(2,1)}, u32[]{:S(2)}, u32[]{:S(2)}) %collective-permute-start.45) | collective-permute-done | bytes 159776 | tf_op jit(solution)/shard_map/ppermute | solution.py:434
  292.5 6.4 %shard_map.287 = (f32[208,768]{1,0:T(8,128)S(1)}, f32[8,768]{1,0:T(8,128)S(1)}, f32[208,384]{1,0:T(8,128)S(1)}, f32[208,384]{1,0:T(8,128)S(1)}, bf16[4,96,768]{2...) custom-call(s32[4]{0:T(128)S(1)} %pad_add_fusion.scal, f32[208,768]{1,0:T(8,128)S(1)} %copy-done.7, ...), custom_call_target="tpu_custom_call" | custom-call | flops 1962934272 | bytes 6463488 | tf_op jit(solution)/shard_map/pallas_call | solution.py:376
  310.5 6.9 %collective-permute-done.62 = bf16[4,96,768]{2,1,0:T(8,128)(2,1)S(1)} collective-permute-done((bf16[4,96,768]{2,1,0:T(8,128)(2,1)S(1)}, bf16[4,96,768]{2,1,0:T(8,128)(2,1)S(1)}, u32[]{:S(2)}, u32[]{:S(2)}) %collective-permute-start.62) | collective-permute-done | bytes 589856 | tf_op jit(solution)/shard_map/ppermute | solution.py:434
  319.4 8.8 %collective-permute-start.64 = (bf16[96,768]{1,0:T(8,128)(2,1)S(1)}, bf16[96,768]{1,0:T(8,128)(2,1)S(1)}, u32[]{:S(2)}, u32[]{:S(2)}) collective-permute-start(bf16[96,768]{1,0:T(8,128)(2,1)S(1)} %get-tuple-element.197), channel_id=1, source_target_pairs={{0,16},{4,20},{8,24},{12,28},{16,0},{20,4},{24,8},{28,12},{1,17},{... | collective-permute-start | bytes 442376 | tf_op jit(solution)/shard_map/ppermute | solution.py:434
  328.2 11.5 %collective-permute-done.68 = bf16[2,96,768]{2,1,0:T(8,128)(2,1)S(1)} collective-permute-done((bf16[2,96,768]{2,1,0:T(8,128)(2,1)S(1)}, bf16[2,96,768]{2,1,0:T(8,128)(2,1)S(1)}, u32[]{:S(2)}, u32[]{:S(2)}) %collective-permute-start.68) | collective-permute-done | bytes 294944 | tf_op jit(solution)/shard_map/ppermute | solution.py:434
  (298 shorter events, 165.0 us)
Async XLA Ops:
  23.5 16.6 %collective-permute-start.3 = (bf16[4,96,896]{2,1,0:T(8,128)(2,1)S(1)}, bf16[4,96,896]{2,1,0:T(8,128)(2,1)S(1)}, u32[]{:S(2)}, u32[]{:S(2)}) collective-permute-start(bf16[4,96,896]{2,1,0:T(8,128)(2,1)S(1)} %pad_maximum_fusion.4.refs_1_.refs_7_), channel_id=1, source_target_pairs={{0,4},{4,0},{8,12},{12,8},{16,20},{20,16},{24,28},{28,24},{1,5},{5... | collective-permute-start | bytes 2064392 | tf_op jit(solution)/shard_map/ppermute | solution.py:434
  25.1 17.9 %collective-permute-start.9 = (bf16[2,96,768]{2,1,0:T(8,128)(2,1)S(1)}, bf16[2,96,768]{2,1,0:T(8,128)(2,1)S(1)}, u32[]{:S(2)}, u32[]{:S(2)}) collective-permute-start(bf16[2,96,768]{2,1,0:T(8,128)(2,1)S(1)} %pad_maximum_fusion.7), channel_id=1, source_target_pairs={{0,24},{4,28},{8,16},{12,20},{16,8},{20,12},{24,0},{28,4},{1,25},{... | collective-permute-start | bytes 884744 | tf_op jit(solution)/shard_map/ppermute | solution.py:434
  27.6 23.2 %collective-permute-start.8 = (bf16[2,96,768]{2,1,0:T(8,128)(2,1)S(1)}, bf16[2,96,768]{2,1,0:T(8,128)(2,1)S(1)}, u32[]{:S(2)}, u32[]{:S(2)}) collective-permute-start(bf16[2,96,768]{2,1,0:T(8,128)(2,1)S(1)} %pad_maximum_fusion.7), channel_id=1, source_target_pairs={{0,16},{4,20},{8,24},{12,28},{16,0},{20,4},{24,8},{28,12},{1,17},{... | collective-permute-start | bytes 884744 | tf_op jit(solution)/shard_map/ppermute | solution.py:434
  27.6 23.2 %collective-permute-start.7 = (bf16[2,96,768]{2,1,0:T(8,128)(2,1)S(1)}, bf16[2,96,768]{2,1,0:T(8,128)(2,1)}, u32[]{:S(2)}, u32[]{:S(2)}) collective-permute-start(bf16[2,96,768]{2,1,0:T(8,128)(2,1)S(1)} %pad_maximum_fusion.7), channel_id=1, source_target_pairs={{0,8},{4,12},{8,0},{12,4},{16,24},{20,28},{24,16},{28,20},{1,9},{5... | collective-permute-start | bytes 884744 | tf_op jit(solution)/shard_map/ppermute | solution.py:434
  51.9 25.7 %collective-permute-start.10 = (bf16[4,2,96,768]{3,2,1,0:T(8,128)(2,1)S(1)}, bf16[4,2,96,768]{3,2,1,0:T(8,128)(2,1)S(1)}, u32[]{:S(2)}, u32[]{:S(2)}) collective-permute-start(bf16[4,2,96,768]{3,2,1,0:T(8,128)(2,1)S(1)} %pad_maximum_fusion.1.refs_0_), channel_id=1, source_target_pairs={{0,4},{4,0},{8,12},{12,8},{16,20},{20,16},{24,28},{28,24},{1,5},{5... | collective-permute-start | bytes 3538952 | tf_op jit(solution)/shard_map/ppermute | solution.py:434
  58.0 19.7 %collective-permute-start.6 = (f32[208,384]{1,0:T(8,128)S(1)}, f32[208,384]{1,0:T(8,128)S(1)}, u32[]{:S(2)}, u32[]{:S(2)}) collective-permute-start(f32[208,384]{1,0:T(8,128)S(1)} %convert_add_fusion.13.own), channel_id=1, source_target_pairs={{0,1},{1,0},{2,3},{3,2},{4,5},{5,4},{6,7},{7,6},{8,9},{9,8},{10,11... | collective-permute-start | bytes 958472 | tf_op jit(solution)/shard_map/ppermute | solution.py:437
  96.5 15.5 %collective-permute-start.13 = (f32[208,384]{1,0:T(8,128)S(1)}, f32[208,384]{1,0:T(8,128)S(1)}, u32[]{:S(2)}, u32[]{:S(2)}) collective-permute-start(f32[208,384]{1,0:T(8,128)S(1)} %convert_add_fusion.12.refs_1_), channel_id=1, source_target_pairs={{0,1},{1,0},{2,3},{3,2},{4,5},{5,4},{6,7},{7,6},{8,9},{9,8},{10,11... | collective-permute-start | bytes 958472 | tf_op jit(solution)/shard_map/ppermute | solution.py:437
  98.1 20.3 %collective-permute-start.29 = (bf16[2,96,768]{2,1,0:T(8,128)(2,1)S(1)}, bf16[2,96,768]{2,1,0:T(8,128)(2,1)S(1)}, u32[]{:S(2)}, u32[]{:S(2)}) collective-permute-start(bf16[2,96,768]{2,1,0:T(8,128)(2,1)S(1)} %get-tuple-element.179), channel_id=1, source_target_pairs={{0,24},{4,28},{8,16},{12,20},{16,8},{20,12},{24,0},{28,4},{1,25},{... | collective-permute-start | bytes 884744 | tf_op jit(solution)/shard_map/ppermute | solution.py:434
  99.9 25.9 %collective-permute-start.28 = (bf16[2,96,768]{2,1,0:T(8,128)(2,1)S(1)}, bf16[2,96,768]{2,1,0:T(8,128)(2,1)S(1)}, u32[]{:S(2)}, u32[]{:S(2)}) collective-permute-start(bf16[2,96,768]{2,1,0:T(8,128)(2,1)S(1)} %get-tuple-element.180), channel_id=1, source_target_pairs={{0,16},{4,20},{8,24},{12,28},{16,0},{20,4},{24,8},{28,12},{1,17},{... | collective-permute-start | bytes 884744 | tf_op jit(solution)/shard_map/ppermute | solution.py:434
  99.9 25.9 %collective-permute-start.27 = (bf16[2,96,768]{2,1,0:T(8,128)(2,1)S(1)}, bf16[2,96,768]{2,1,0:T(8,128)(2,1)S(1)}, u32[]{:S(2)}, u32[]{:S(2)}) collective-permute-start(bf16[2,96,768]{2,1,0:T(8,128)(2,1)S(1)} %get-tuple-element.181), channel_id=1, source_target_pairs={{0,8},{4,12},{8,0},{12,4},{16,24},{20,28},{24,16},{28,20},{1,9},{5... | collective-permute-start | bytes 884744 | tf_op jit(solution)/shard_map/ppermute | solution.py:434
  127.0 40.6 %collective-permute-start.36 = (bf16[4,2,96,768]{3,2,1,0:T(8,128)(2,1)}, bf16[4,2,96,768]{3,2,1,0:T(8,128)(2,1)}, u32[]{:S(2)}, u32[]{:S(2)}) collective-permute-start(bf16[4,2,96,768]{3,2,1,0:T(8,128)(2,1)} %pad_maximum_fusion.3.refs_14_), channel_id=1, source_target_pairs={{0,4},{4,0},{8,12},{12,8},{16,20},{20,16},{24,28},{28,24},{1,5},{5... | collective-permute-start | bytes 3538952 | tf_op jit(solution)/shard_map/ppermute | solution.py:434
  181.7 28.1 %collective-permute-start.74 = (bf16[4,2,96,768]{3,2,1,0:T(8,128)(2,1)S(1)}, bf16[4,2,96,768]{3,2,1,0:T(8,128)(2,1)S(1)}, u32[]{:S(2)}, u32[]{:S(2)}) collective-permute-start(bf16[4,2,96,768]{3,2,1,0:T(8,128)(2,1)S(1)} %get-tuple-element.104), channel_id=1, source_target_pairs={{0,4},{4,0},{8,12},{12,8},{16,20},{20,16},{24,28},{28,24},{1,5},{5... | collective-permute-start | bytes 3538952 | tf_op jit(solution)/shard_map/ppermute | solution.py:434
  187.2 16.3 %collective-permute-start.39 = (bf16[208,384]{1,0:T(8,128)(2,1)S(1)}, bf16[208,384]{1,0:T(8,128)(2,1)S(1)}, u32[]{:S(2)}, u32[]{:S(2)}) collective-permute-start(bf16[208,384]{1,0:T(8,128)(2,1)S(1)} %get-tuple-element.189), channel_id=1, source_target_pairs={{0,16},{4,20},{8,24},{12,28},{16,0},{20,4},{24,8},{28,12},{1,17},{... | collective-permute-start | bytes 479240 | tf_op jit(solution)/shard_map/ppermute | solution.py:434
  212.5 24.8 %collective-permute-start.76 = (bf16[2,96,768]{2,1,0:T(8,128)(2,1)}, bf16[2,96,768]{2,1,0:T(8,128)(2,1)S(1)}, u32[]{:S(2)}, u32[]{:S(2)}) collective-permute-start(bf16[2,96,768]{2,1,0:T(8,128)(2,1)} %get-tuple-element.169), channel_id=1, source_target_pairs={{0,16},{4,20},{8,24},{12,28},{16,0},{20,4},{24,8},{28,12},{1,17},{... | collective-permute-start | bytes 884744 | tf_op jit(solution)/shard_map/ppermute | solution.py:434
  216.5 21.3 %collective-permute-start.75 = (bf16[2,96,768]{2,1,0:T(8,128)(2,1)}, bf16[2,96,768]{2,1,0:T(8,128)(2,1)S(1)}, u32[]{:S(2)}, u32[]{:S(2)}) collective-permute-start(bf16[2,96,768]{2,1,0:T(8,128)(2,1)} %get-tuple-element.170), channel_id=1, source_target_pairs={{0,24},{4,28},{8,16},{12,20},{16,8},{20,12},{24,0},{28,4},{1,25},{... | collective-permute-start | bytes 884744 | tf_op jit(solution)/shard_map/ppermute | solution.py:434
  218.3 19.6 %collective-permute-start.77 = (bf16[2,96,768]{2,1,0:T(8,128)(2,1)}, bf16[2,96,768]{2,1,0:T(8,128)(2,1)}, u32[]{:S(2)}, u32[]{:S(2)}) collective-permute-start(bf16[2,96,768]{2,1,0:T(8,128)(2,1)} %get-tuple-element.168), channel_id=1, source_target_pairs={{0,8},{4,12},{8,0},{12,4},{16,24},{20,28},{24,16},{28,20},{1,9},{5... | collective-permute-start | bytes 884744 | tf_op jit(solution)/shard_map/ppermute | solution.py:434
  228.9 26.1 %collective-permute-start.43 = (bf16[4,208,384]{2,1,0:T(8,128)(2,1)S(1)}, bf16[4,208,384]{2,1,0:T(8,128)(2,1)S(1)}, u32[]{:S(2)}, u32[]{:S(2)}) collective-permute-start(bf16[4,208,384]{2,1,0:T(8,128)(2,1)S(1)} %copy-done.15), channel_id=1, source_target_pairs={{0,1},{1,0},{2,3},{3,2},{4,5},{5,4},{6,7},{7,6},{8,9},{9,8},{10,11... | collective-permute-start | bytes 1916936 | tf_op jit(solution)/shard_map/ppermute | solution.py:437
  252.3 15.5 %collective-permute-start.71 = (bf16[96,768]{1,0:T(8,128)(2,1)S(1)}, bf16[96,768]{1,0:T(8,128)(2,1)S(1)}, u32[]{:S(2)}, u32[]{:S(2)}) collective-permute-start(bf16[96,768]{1,0:T(8,128)(2,1)S(1)} %get-tuple-element.190), channel_id=1, source_target_pairs={{0,8},{4,12},{8,0},{12,4},{16,24},{20,28},{24,16},{28,20},{1,9},{5... | collective-permute-start | bytes 442376 | tf_op jit(solution)/shard_map/ppermute | solution.py:434
  268.8 35.4 %collective-permute-start.66 = (bf16[4,2,96,768]{3,2,1,0:T(8,128)(2,1)}, bf16[4,2,96,768]{3,2,1,0:T(8,128)(2,1)}, u32[]{:S(2)}, u32[]{:S(2)}) collective-permute-start(bf16[4,2,96,768]{3,2,1,0:T(8,128)(2,1)} %get-tuple-element.100), channel_id=1, source_target_pairs={{0,4},{4,0},{8,12},{12,8},{16,20},{20,16},{24,28},{28,24},{1,5},{5... | collective-permute-start | bytes 3538952 | tf_op jit(solution)/shard_map/ppermute | solution.py:434
  307.8 31.9 %collective-permute-start.68 = (bf16[2,96,768]{2,1,0:T(8,128)(2,1)S(1)}, bf16[2,96,768]{2,1,0:T(8,128)(2,1)S(1)}, u32[]{:S(2)}, u32[]{:S(2)}) collective-permute-start(bf16[2,96,768]{2,1,0:T(8,128)(2,1)S(1)} %get-tuple-element.175), channel_id=1, source_target_pairs={{0,16},{4,20},{8,24},{12,28},{16,0},{20,4},{24,8},{28,12},{1,17},{... | collective-permute-start | bytes 884744 | tf_op jit(solution)/shard_map/ppermute | solution.py:434
  307.8 31.9 %collective-permute-start.67 = (bf16[2,96,768]{2,1,0:T(8,128)(2,1)S(1)}, bf16[2,96,768]{2,1,0:T(8,128)(2,1)S(1)}, u32[]{:S(2)}, u32[]{:S(2)}) collective-permute-start(bf16[2,96,768]{2,1,0:T(8,128)(2,1)S(1)} %get-tuple-element.173), channel_id=1, source_target_pairs={{0,8},{4,12},{8,0},{12,4},{16,24},{20,28},{24,16},{28,20},{1,9},{5... | collective-permute-start | bytes 884744 | tf_op jit(solution)/shard_map/ppermute | solution.py:434
  310.4 30.2 %collective-permute-start.57 = (f32[208,384]{1,0:T(8,128)S(1)}, f32[208,384]{1,0:T(8,128)S(1)}, u32[]{:S(2)}, u32[]{:S(2)}) collective-permute-start(f32[208,384]{1,0:T(8,128)S(1)} %convert_add_fusion.6.own), channel_id=1, source_target_pairs={{0,1},{1,0},{2,3},{3,2},{4,5},{5,4},{6,7},{7,6},{8,9},{9,8},{10,11... | collective-permute-start | bytes 958472 | tf_op jit(solution)/shard_map/ppermute | solution.py:437
  317.6 26.0 %collective-permute-start.65 = (bf16[96,768]{1,0:T(8,128)(2,1)S(1)}, bf16[96,768]{1,0:T(8,128)(2,1)S(1)}, u32[]{:S(2)}, u32[]{:S(2)}) collective-permute-start(bf16[96,768]{1,0:T(8,128)(2,1)S(1)} %get-tuple-element.196), channel_id=1, source_target_pairs={{0,24},{4,28},{8,16},{12,20},{16,8},{20,12},{24,0},{28,4},{1,25},{... | collective-permute-start | bytes 442376 | tf_op jit(solution)/shard_map/ppermute | solution.py:434
  319.4 25.2 %collective-permute-start.64 = (bf16[96,768]{1,0:T(8,128)(2,1)S(1)}, bf16[96,768]{1,0:T(8,128)(2,1)S(1)}, u32[]{:S(2)}, u32[]{:S(2)}) collective-permute-start(bf16[96,768]{1,0:T(8,128)(2,1)S(1)} %get-tuple-element.197), channel_id=1, source_target_pairs={{0,16},{4,20},{8,24},{12,28},{16,0},{20,4},{24,8},{28,12},{1,17},{... | collective-permute-start | bytes 442376 | tf_op jit(solution)/shard_map/ppermute | solution.py:434
  (92 other events, 815.9 us)

commit v2 on v1

--- a/solution.py
+++ b/solution.py
@@ -189,12 +189,12 @@
     refs = list(refs)
     h_refs = [refs.pop(0) for _ in range(1 + 2 * (PLANES - 1))]
     g_refs = [refs.pop(0) for _ in range(1 + 2 * (PLANES - 1))]
-    blocks = [refs.pop(0) for _ in range(parts)]
+    blocks = [refs.pop(0) for _ in range(2 * parts)]
     y_keep, y_send, d_keep, d_send = [refs.pop(0) for _ in range(4)]
-    grads = [refs.pop(0) for _ in range(parts)]
+    grads = [refs.pop(0) for _ in range(2 * parts)]
     up, down, hs, gs, rs, dus, dys, acc = refs
-    assemble(up, me, blocks, (0,))
-    assemble(down, me, blocks, (1,))
+    assemble(up, me, blocks[:parts])
+    assemble(down, me, blocks[parts:])
     for dst, src in ((hs, h_refs), (gs, g_refs)):
         dst[0] = src[0][...]
         for m in range(1, PLANES):
@@ -232,10 +232,10 @@
 
     lax.fori_loop(0, PLANES, step, 0)
     flat = (PLANES * padded, model)
-    acc[...] = tn(hs[...].reshape(flat), dus[...].reshape(flat))
-    scatter_blocks(acc, me, grads, (0,))
-    acc[...] = tn(dys[...].reshape(flat), rs[...].reshape(flat))
-    scatter_blocks(acc, me, grads, (1,))
+    acc[...] = tn(hs[...].reshape(flat), dus[...].reshape(flat)).astype(acc.dtype)
+    scatter_blocks(acc, me, grads[:parts])
+    acc[...] = tn(dys[...].reshape(flat), rs[...].reshape(flat)).astype(acc.dtype)
+    scatter_blocks(acc, me, grads[parts:])
 
 
 def plain_pull(x_ref, own, other, g_ref, rows_ref, small_ref, gain_row, core):
@@ -322,7 +322,8 @@
     keep, send = split_halves(core, dh)
     keep_ref[...] = keep
     send_ref[...] = send.astype(send_ref.dtype)
-    acc[...] = tn(h, jnp.concatenate(left, axis=1)) + tn(db, jnp.concatenate(right, axis=1))
+    grad = tn(h, jnp.concatenate(left, axis=1)) + tn(db, jnp.concatenate(right, axis=1))
+    acc[...] = grad.astype(acc.dtype)
     scatter_blocks(acc, me, grads)
 
 
@@ -350,9 +351,9 @@
     keep, send = split_halves(core, nt(du, up[...].astype(bf16)))
     keep_ref[...] = keep
     send_ref[...] = send.astype(send_ref.dtype)
-    acc[...] = tn(h, du)
+    acc[...] = tn(h, du).astype(acc.dtype)
     scatter_blocks(acc, me, grads, (0,))
-    acc[...] = tn(dm, r)
+    acc[...] = tn(dm, r).astype(acc.dtype)
     scatter_blocks(acc, me, grads, (1,))
 
 
@@ -370,7 +371,7 @@
     scatter_blocks(acc, me, grads)
 
 
-def run(kernel, scal, ins, outs, scratch, flops):
+def run(kernel, scal, ins, outs, scratch, flops, vmem_mib=24):
     vmem = pl.BlockSpec(memory_space=pltpu.VMEM)
     size = lambda s: s.size * s.dtype.itemsize
     return pl.pallas_call(
@@ -379,7 +380,7 @@
         in_specs=[pl.BlockSpec(memory_space=pltpu.SMEM)] + [vmem] * len(ins),
         out_specs=[vmem] * len(outs),
         scratch_shapes=scratch,
-        compiler_params=pltpu.CompilerParams(vmem_limit_bytes=48 * 2**20),
+        compiler_params=pltpu.CompilerParams(vmem_limit_bytes=vmem_mib * 2**20),
         cost_estimate=pl.CostEstimate(
             flops=int(flops),
             bytes_accessed=int(sum(size(a) for a in ins) + sum(size(o) for o in outs)),
@@ -394,6 +395,10 @@
 
 def tie(value, *after):
     return lax.optimization_barrier((value,) + after)[0]
+
+
+def bar(*values):
+    return lax.optimization_barrier(values)
 
 
 def shards(
@@ -446,6 +451,18 @@
     def gather_planes(block):
         return jnp.stack([block] + [across(block, m * parts) for m in range(1, PLANES)])
 
+    def planes(blocks):
+        return [blocks[0]] + [across(blocks[m].astype(bf16), m * parts) for m in range(1, PLANES)]
+
+    def added(arrays):
+        return sum([a.astype(f32) for a in arrays[1:]], arrays[0].astype(f32))
+
+    def enclosed(stage, *operands):
+        def idle(*args):
+            return jax.tree.map(lambda r: jnp.zeros(r.shape, r.dtype), jax.eval_shape(stage, *args))
+
+        return lax.cond(me < fsdp, stage, idle, *operands)
+
     def fold(arrays):
         arrays, bit = list(arrays), parts // 2
         while bit:
@@ -496,30 +513,24 @@
     mlp = gather_planes(tie(mlp, one))
     w_mlp = spread(mlp)
     two = gather_planes(tie(attn_pack(qkv_weight_two, out_weight_two), mlp))
-    w_two = spread(two)
-    experts = jnp.stack([expert_up, jnp.swapaxes(expert_down, 1, 2)], axis=1)
-    experts = tie(experts, two)
-    mine = [lax.dynamic_index_in_dim(experts, plane ^ m, 0, keepdims=False) for m in range(PLANES)]
-    mine = jnp.stack([mine[0]] + [across(mine[m], m * parts) for m in range(1, PLANES)])
-    w_moe = spread(mine)
-
-    def image_blocks(own, own_half):
-        near = [across(own_half, m * parts) for m in range(1, PLANES)]
-        return [own] + near + [over(n, 1) for n in near]
+
+    def by_plane(experts):
+        return [lax.dynamic_index_in_dim(experts, plane ^ m, 0, keepdims=False) for m in range(PLANES)]
+
+    e_up = planes(tie(by_plane(expert_up), two))
+    e_down = by_plane(jnp.swapaxes(expert_down, 1, 2))
 
     pad = ((0, padded - tokens), (0, 0))
     stream0 = jnp.pad(activations[0], pad)
     grad3 = jnp.pad(cotangent[0] * image_live[0].astype(f32), pad)
     routes = jnp.pad(expert_routes[0], pad, constant_values=-1)
-    grad_low = tie(grad3.astype(bf16), mine)
+    grad_low = grad3.astype(bf16)
     grad_half = jnp.where(core == 0, grad_low[:, :half], grad_low[:, half:])
-    g_blocks = image_blocks(grad_low, grad_half)
 
     stream = shape((padded, model), f32)
     pieces = [shape((padded, half), f32)] * 2
     wide = pltpu.VMEM((model, model + 128), held)
     square = pltpu.VMEM((model, model), held)
-    total = pltpu.VMEM((model, model), f32)
     unit = 2 * padded * model * model
 
     keep, send, small_rows = run(
@@ -531,33 +542,52 @@
         3 * unit,
     )
     own, other = joined(keep, send)
-    stream1, keep, send = run(
-        functools.partial(mlp_fwd_kernel, parts, 5),
-        scal,
-        [stream0, own, other, small_rows] + w_mlp,
-        [stream] + pieces,
-        [square, square],
-        2 * unit,
-    )
-    own, other = joined(keep, send)
-    stream2, keep, send = run(
-        functools.partial(attn_fwd_kernel, tokens, parts, 6, False),
-        scal,
-        [stream1, own, other, small_rows] + w_two,
-        [stream] + pieces,
-        [square],
-        3 * unit,
-    )
-    own, other = joined(keep, send)
-    stream3, h_full, h_half = run(
-        functools.partial(moe_pre_kernel, tokens, 7),
-        scal,
-        [stream2, own, other, small_rows, routes],
-        [stream, shape((padded, model), bf16), shape((padded, half), bf16)],
-        [],
-        unit / 50,
-    )
-    h_blocks = image_blocks(h_full, h_half)
+    own, other, two, e_up, e_down = bar(own, other, two, e_up, e_down)
+    w_two, e_down = spread(two), planes(e_down)
+
+    def stage_two(scal, *ins):
+        stream1, keep, send = run(
+            functools.partial(mlp_fwd_kernel, parts, 5),
+            scal,
+            ins,
+            [stream] + pieces,
+            [square, square],
+            2 * unit,
+        )
+        return stream1, *joined(keep, send)
+
+    stream1, own, other = enclosed(stage_two, scal, stream0, own, other, small_rows, *w_mlp)
+    own, other, w_two, e_down, grad_half = bar(own, other, w_two, e_down, grad_half)
+    w_e_up = spread(jnp.stack(e_up))
+    g_near = planes([grad_half] * PLANES)[1:]
+
+    def stage_three(scal, routes, small_rows, *ins):
+        stream2, keep, send = run(
+            functools.partial(attn_fwd_kernel, tokens, parts, 6, False),
+            scal,
+            [*ins[:3], small_rows, *ins[3:]],
+            [stream] + pieces,
+            [square],
+            3 * unit,
+        )
+        outs = run(
+            functools.partial(moe_pre_kernel, tokens, 7),
+            scal,
+            [stream2, *joined(keep, send), small_rows, routes],
+            [stream, shape((padded, model), bf16), shape((padded, half), bf16)],
+            [],
+            unit / 50,
+        )
+        return stream2, *outs
+
+    stream2, stream3, h_full, h_half = enclosed(
+        stage_three, scal, routes, small_rows, stream1, own, other, *w_two
+    )
+    h_half, w_e_up, g_near = bar(h_half, w_e_up, g_near)
+    h_near = planes([h_half] * PLANES)[1:]
+    w_moe = w_e_up + spread(jnp.stack(e_down))
+    h_blocks = [h_full] + h_near + [over(n, 1) for n in h_near]
+    g_blocks = [grad_low] + g_near + [over(n, 1) for n in g_near]
     images = pltpu.VMEM((PLANES, padded, model), bf16)
     image_hidden = pltpu.VMEM((PLANES, padded, hidden), bf16)
     block_pieces = [shape((PLANES, padded, half), f32), shape((PLANES, padded, half), bf16)]
@@ -565,49 +595,64 @@
         functools.partial(moe_kernel, parts),
         scal,
         h_blocks + g_blocks + w_moe,
-        block_pieces * 2 + [shape((PLANES, 2, rows, hidden), bf16)] * parts,
-        [square, square, images, images, image_hidden, image_hidden, images, total],
+        block_pieces * 2 + [shape((PLANES, rows, hidden), bf16)] * (2 * parts),
+        [square, square, images, images, image_hidden, image_hidden, images, square],
         24 * unit,
+        40,
     )
 
     def home(keep, send):
         summed = keep + over(send, 1).astype(f32)
-        return pair(reduce_planes(summed))
-
-    own, other = home(d_keep, d_send)
+        return planes(list(summed))
+
     block_grads = [shape((PLANES, rows, model), bf16)] * parts
-    grad2, small, keep, send, *two_grads = run(
+    own, other = pair(added(home(d_keep, d_send)))
+    e_up, e_down = fold(expert_grads[:parts]), fold(expert_grads[parts:])
+    own, other, e_up = bar(own, other, e_up)
+    e_up = planes(list(e_up))
+    grad2, small, keep, send, *two_sum = run(
         functools.partial(attn_bwd_kernel, tokens, parts, (7, 6), False),
         scal,
         [stream3, own, other, grad3, small_rows, routes, stream2] + w_two,
         [stream, shape((8, model), f32)] + pieces + block_grads,
-        [square, total],
+        [square, square],
         8 * unit,
     )
+    keep, send, e_up, e_down = bar(keep, send, e_up, e_down)
+    e_down = planes(list(e_down))
+    two_sum = fold(two_sum)
     own, other = joined(keep, send)
-    y_keep, y_send = lax.optimization_barrier((y_keep, y_send, keep))[:2]
-    y_own, y_other = home(y_keep, y_send)
-    expert_sum = fold(expert_grads)
-    grad1, small, keep, send, *mlp_grads = run(
+    own, other, e_down, two_sum = bar(own, other, e_down, two_sum)
+    grad1, small, keep, send, *mlp_sum = run(
         functools.partial(mlp_bwd_kernel, parts, (6, 5)),
         scal,
         [stream2, own, other, grad2, small_rows, small, stream1] + w_mlp,
         [stream, shape((8, model), f32)]
         + pieces
         + [shape((PLANES, 2, rows, hidden), bf16)] * parts,
-        [square, square, total],
+        [square, square, square],
         5 * unit,
     )
+    mlp_sum = fold(mlp_sum)
+    two_sum = planes(list(two_sum))
     own, other = joined(keep, send)
-    grad0, small, keep, send, *one_grads = run(
+    y_keep, y_send = bar(y_keep, y_send, keep)[:2]
+    y_own = home(y_keep, y_send)
+    own, other, mlp_sum, two_sum, y_own = bar(own, other, mlp_sum, two_sum, y_own)
+    mlp_sum = planes(list(mlp_sum))
+    y_own, y_other = pair(added(y_own))
+    grad0, small, keep, send, *one_sum = run(
         functools.partial(attn_bwd_kernel, tokens, parts, (5, 4), True),
         scal,
         [stream1, own, other, grad1, small_rows, small, stream0] + w_one,
         [stream, shape((8, model), f32)] + pieces + block_grads,
-        [wide, total],
+        [wide, square],
         8 * unit,
     )
+    one_sum = fold(one_sum)
     own, other = joined(keep, send)
+    own, other, one_sum, mlp_sum = bar(own, other, one_sum, mlp_sum)
+    one_sum = planes(list(one_sum))
     input_grad, *small_grads = run(
         functools.partial(final_kernel, tokens, 4),
         scal,
@@ -616,25 +661,21 @@
         [pltpu.VMEM((model, 128), f32)],
         unit / 50,
     )
+    small_sum = reduce_planes(fold(small_grads))
+    one_sum, two_sum, mlp_sum = added(one_sum), added(two_sum), added(mlp_sum)
 
     low = jnp.where(core == 0, y_own, y_other)
     high = jnp.where(core == 0, y_other, y_own)
     result = (stream3 + jnp.concatenate([low, high], axis=1))[:tokens]
 
-    came = [expert_sum[0]]
-    for m in range(1, PLANES):
-        came.append(across(expert_sum[m].astype(bf16), m * parts).astype(f32))
     bit0, bit1 = plane % 2 == 1, plane // 2 == 1
 
-    def of_expert(x):
+    def of_expert(came, x):
         a, b = jnp.where(bit0, came[x ^ 1], came[x]), jnp.where(bit0, came[x ^ 3], came[x ^ 2])
-        return jnp.where(bit1, b, a)
-
-    by_expert = jnp.stack([of_expert(x) for x in range(PLANES)])
-    two_sum = reduce_planes(fold(two_grads))
-    mlp_sum = reduce_planes(fold(mlp_grads))
-    one_sum = reduce_planes(fold(one_grads))
-    small_sum = reduce_planes(fold(small_grads))
+        return jnp.where(bit1, b, a).astype(f32)
+
+    grad_up = jnp.stack([of_expert(e_up, x) for x in range(PLANES)])
+    grad_down = jnp.stack([of_expert(e_down, x).T for x in range(PLANES)])
     qkv_one, out_one = attn_unpack(one_sum)
     qkv_two, out_two = attn_unpack(two_sum)
     return (
@@ -651,8 +692,8 @@
         out_two,
         small_sum[:, 7],
         small_sum[:, :PLANES],
-        by_expert[:, 0],
-        jnp.swapaxes(by_expert[:, 1], 1, 2),
+        grad_up,
+        grad_down,
     )
 
 

time: 357 us -> 340 us (0.952)
  waiting for transfers between devices: 173 us -> 152 us
  starting transfers between devices: 90.1 us -> 99.1 us
  local copies, waits for them, and re-layouts: 28.8 us -> 21.1 us
    ppermute x48 -> x56, waiting for transfers between devices: 153 us -> 119 us  [across(): return lax.ppermute(value, 'fsdp', [(i, i ^ k) for i in range(fsdp)])]
    ppermute x48 -> x56, starting transfers between devices: 74.9 us -> 88.2 us  [across(): return lax.ppermute(value, 'fsdp', [(i, i ^ k) for i in range(fsdp)])]
    ppermute x30, waiting for transfers between devices: 20.1 us -> 33.4 us  [over(): return lax.ppermute(value, 'tensor', [(i, i ^ k) for i in range(tensor)])]
    unnamed x85 -> x81, local copies, waits for them, and re-layouts: 18.9 us -> 11.3 us
    ppermute x30, starting transfers between devices: 15.2 us -> 10.8 us  [over(): return lax.ppermute(value, 'tensor', [(i, i ^ k) for i in range(tensor)])]
    another operation x10 -> x14, other arithmetic: 8.79 us -> 7.23 us
  transfers between devices with their start and end apart: 78 -> 86, of which waited for: 32 -> 33; matrix products, arithmetic and copies ran while one was open for 9% -> 10% of each run, Pallas kernels for 8% -> 7%
where the time goes in v2:
time: 340 us; the launch traced here: 339 us
  waiting for transfers between devices  152 us (45%)
  starting transfers between devices  99.1 us (29%)
  Pallas kernels  41.7 us (12%)
  other arithmetic  22.4 us (7%)
  local copies, waits for them, and re-layouts  21.1 us (6%)
    ppermute x56, waiting for transfers between devices, across(): return lax.ppermute(value, 'fsdp', [(i, i ^ k) for i in range(fsdp)])  119 us
    ppermute x56, starting transfers between devices, across(): return lax.ppermute(value, 'fsdp', [(i, i ^ k) for i in range(fsdp)])  88.2 us
    pallas_call x9, Pallas kernels, run(): pl.pallas_call(kernel, out_shape=outs, in_specs=[pl.BlockSpec(memory_spac...  41.7 us
    ppermute x30, waiting for transfers between devices, over(): return lax.ppermute(value, 'tensor', [(i, i ^ k) for i in range(tensor)])  33.4 us
    unnamed x81, local copies, waits for them, and re-layouts  11.3 us
    ppermute x30, starting transfers between devices, over(): return lax.ppermute(value, 'tensor', [(i, i ^ k) for i in range(tensor)])  10.8 us
  transfers between devices with their start and end apart: 86, of which 33 were waited for; matrix products, arithmetic and copies ran while one was open for 10% of the time, Pallas kernels for 7%

profile of v2, /device:TPU:0, one launch (start us, length us, event | category | flops | bytes accessed | tf_op | source)
XLA Modules:
  0.0 338.8 jit_solution(7227618932400556577)
XLA Ops:
  3.6 5.1 %collective-permute-start.8 = (bf16[96,896]{1,0:T(8,128)(2,1)S(1)}, bf16[96,896]{1,0:T(8,128)(2,1)S(1)}, u32[]{:S(2)}, u32[]{:S(2)}) collective-permute-start(bf16[96,896]{1,0:T(8,128)(2,1)S(1)} %get-tuple-element.382), channel_id=1, source_target_pairs={{0,24},{4,28},{8,16},{12,20},{16,8},{20,12},{24,0},{28,4},{1,25},{... | collective-permute-start | bytes 516104 | tf_op jit(solution)/shard_map/ppermute | solution.py:439
  9.4 4.7 %collective-permute-done.8 = bf16[96,896]{1,0:T(8,128)(2,1)S(1)} collective-permute-done((bf16[96,896]{1,0:T(8,128)(2,1)S(1)}, bf16[96,896]{1,0:T(8,128)(2,1)S(1)}, u32[]{:S(2)}, u32[]{:S(2)}) %collective-permute-start.8) | collective-permute-done | bytes 172064 | tf_op jit(solution)/shard_map/ppermute | solution.py:439
  14.1 9.3 %collective-permute-done.7 = bf16[96,896]{1,0:T(8,128)(2,1)S(1)} collective-permute-done((bf16[96,896]{1,0:T(8,128)(2,1)S(1)}, bf16[96,896]{1,0:T(8,128)(2,1)S(1)}, u32[]{:S(2)}, u32[]{:S(2)}) %collective-permute-start.7) | collective-permute-done | bytes 172064 | tf_op jit(solution)/shard_map/ppermute | solution.py:439
  30.6 9.4 %collective-permute-done.9.refs_2_.refs_8_ = bf16[4,96,896]{2,1,0:T(8,128)(2,1)S(1)} collective-permute-done((bf16[4,96,896]{2,1,0:T(8,128)(2,1)S(1)}, bf16[4,96,896]{2,1,0:T(8,128)(2,1)S(1)}, u32[]{:S(2)}, u32[]{:S(2)}) %collective-permute-start.9) | collective-permute-done | bytes 688160 | tf_op jit(solution)/shard_map/ppermute | solution.py:439
  42.9 8.8 %collective-permute-done.14 = bf16[2,96,768]{2,1,0:T(8,128)(2,1)S(1)} collective-permute-done((bf16[2,96,768]{2,1,0:T(8,128)(2,1)S(1)}, bf16[2,96,768]{2,1,0:T(8,128)(2,1)S(1)}, u32[]{:S(2)}, u32[]{:S(2)}) %collective-permute-start.14) | collective-permute-done | bytes 294944 | tf_op jit(solution)/shard_map/ppermute | solution.py:439
  63.7 4.5 %collective-permute-done.17 = bf16[96,768]{1,0:T(8,128)(2,1)S(1)} collective-permute-done((bf16[96,768]{1,0:T(8,128)(2,1)S(1)}, bf16[96,768]{1,0:T(8,128)(2,1)S(1)}, u32[]{:S(2)}, u32[]{:S(2)}) %collective-permute-start.17) | collective-permute-done | bytes 147488 | tf_op jit(solution)/shard_map/ppermute | solution.py:439
  75.4 6.8 %collective-permute-done.20 = bf16[96,768]{1,0:T(8,128)(2,1)S(1)} collective-permute-done((bf16[96,768]{1,0:T(8,128)(2,1)S(1)}, bf16[96,768]{1,0:T(8,128)(2,1)S(1)}, u32[]{:S(2)}, u32[]{:S(2)}) %collective-permute-start.20) | collective-permute-done | bytes 147488 | tf_op jit(solution)/shard_map/ppermute | solution.py:439
  89.7 13.1 %conditional.2 = (f32[208,768]{1,0:T(8,128)}, f32[208,384]{1,0:T(8,128)}, f32[208,384]{1,0:T(8,128)}) conditional(s32[]{:T(128)} %convert_element_type.312, () %tuple.37, (s32[4]{0:T(128)S(1)}, f32[208,768]{1,0:T(8,128)S(1)}, f32[208,384]{1,0:T(8,128)S(1)}, f32[208,384]{1,0:T(8,128)S(1)}, f32[8,768]{1,0:T(8,128)S(1)}, ...), branch_computations={%region_0.1_spmd, %region_1.2_spmd} | conditional | flops 491132928 | bytes 9572496 | solution.py:464
  94.4 5.6 %collective-permute-done.1 = bf16[208,384]{1,0:T(8,128)(2,1)S(1)} collective-permute-done((bf16[208,384]{1,0:T(8,128)(2,1)S(1)}, bf16[208,384]{1,0:T(8,128)(2,1)S(1)}, u32[]{:S(2)}, u32[]{:S(2)}) %collective-permute-start.1) | collective-permute-done | bytes 159776 | tf_op jit(solution)/shard_map/cond/branch_1_fun/ppermute | solution.py:442
  111.2 16.3 %conditional.3 = (f32[208,768]{1,0:T(8,128)}, f32[208,768]{1,0:T(8,128)}, bf16[208,768]{1,0:T(8,128)(2,1)}, bf16[208,384]{1,0:T(8,128)(2,1)S(1)}) conditional(s32[]{:T(128)} %convert_element_type.312, () %tuple.36, (s32[4]{0:T(128)S(1)}, f32[208,768]{1,0:T(8,128)}, f32[208,384]{1,0:T(8,128)}, f32[208,384]{1,0:T(8,128)}, f32[8,768]{1,0:T(8,128)S(1)}, ...), branch_computations={%region_2.3_spmd, %region_3.4_spmd} | conditional | flops 741407040 | bytes 10815256 | solution.py:464
  117.5 5.6 %collective-permute-done.4 = bf16[208,384]{1,0:T(8,128)(2,1)S(1)} collective-permute-done((bf16[208,384]{1,0:T(8,128)(2,1)S(1)}, bf16[208,384]{1,0:T(8,128)(2,1)S(1)}, u32[]{:S(2)}, u32[]{:S(2)}) %collective-permute-start.4) | collective-permute-done | bytes 159776 | tf_op jit(solution)/shard_map/cond/branch_1_fun/ppermute | solution.py:442
  137.4 6.7 %collective-permute-done.32.refs_2_ = bf16[208,384]{1,0:T(8,128)(2,1)S(1)} collective-permute-done((bf16[208,384]{1,0:T(8,128)(2,1)S(1)}, bf16[208,384]{1,0:T(8,128)(2,1)S(1)}, u32[]{:S(2)}, u32[]{:S(2)}) %collective-permute-start.32) | collective-permute-done | bytes 159776 | tf_op jit(solution)/shard_map/ppermute | solution.py:439
  148.2 11.4 %shard_map.281 = (f32[4,208,384]{2,1,0:T(8,128)S(1)}, bf16[4,208,384]{2,1,0:T(8,128)(2,1)S(1)}, f32[4,208,384]{2,1,0:T(8,128)S(1)}, bf16[4,208,384]{2,1,0:T(8,12...) custom-call(s32[4]{0:T(128)S(1)} %pad_add_fusion.scal, ...), custom_call_target="tpu_custom_call" | custom-call | flops 5888802816 | bytes 11108352 | tf_op jit(solution)/shard_map/pallas_call | solution.py:377
  171.0 9.4 %collective-permute-done.43 = bf16[208,384]{1,0:T(8,128)(2,1)S(1)} collective-permute-done((bf16[208,384]{1,0:T(8,128)(2,1)S(1)}, bf16[208,384]{1,0:T(8,128)(2,1)S(1)}, u32[]{:S(2)}, u32[]{:S(2)}) %collective-permute-start.43) | collective-permute-done | bytes 159776 | tf_op jit(solution)/shard_map/ppermute | solution.py:439
  181.7 5.0 %collective-permute-done.45 = bf16[208,384]{1,0:T(8,128)(2,1)} collective-permute-done((bf16[208,384]{1,0:T(8,128)(2,1)S(1)}, bf16[208,384]{1,0:T(8,128)(2,1)}, u32[]{:S(2)}, u32[]{:S(2)}) %collective-permute-start.45) | collective-permute-done | bytes 159776 | tf_op jit(solution)/shard_map/ppermute | solution.py:442
  189.0 7.3 %collective-permute-done.51 = bf16[4,96,768]{2,1,0:T(8,128)(2,1)} collective-permute-done((bf16[4,96,768]{2,1,0:T(8,128)(2,1)}, bf16[4,96,768]{2,1,0:T(8,128)(2,1)}, u32[]{:S(2)}, u32[]{:S(2)}) %collective-permute-start.51) | collective-permute-done | bytes 589856 | tf_op jit(solution)/shard_map/ppermute | solution.py:439
  202.2 7.5 %shard_map.282 = (f32[208,768]{1,0:T(8,128)S(1)}, f32[8,768]{1,0:T(8,128)S(1)}, f32[208,384]{1,0:T(8,128)S(1)}, f32[208,384]{1,0:T(8,128)S(1)}, bf16[4,96,768]{2...) custom-call(s32[4]{0:T(128)S(1)} %pad_add_fusion.scal, f32[208,768]{1,0:T(8,128)S(1)} %copy-done.21, ...), custom_call_target="tpu_custom_call" | custom-call | flops 1962934272 | bytes 6243968 | tf_op jit(solution)/shard_map/pallas_call | solution.py:377
  217.9 4.4 %collective-permute-done.53 = bf16[208,384]{1,0:T(8,128)(2,1)S(1)} collective-permute-done((bf16[208,384]{1,0:T(8,128)(2,1)S(1)}, bf16[208,384]{1,0:T(8,128)(2,1)S(1)}, u32[]{:S(2)}, u32[]{:S(2)}) %collective-permute-start.53) | collective-permute-done | bytes 159776 | tf_op jit(solution)/shard_map/ppermute | solution.py:442
  247.5 12.5 %collective-permute-done.62 = bf16[4,2,96,768]{3,2,1,0:T(8,128)(2,1)S(1)} collective-permute-done((bf16[4,2,96,768]{3,2,1,0:T(8,128)(2,1)S(1)}, bf16[4,2,96,768]{3,2,1,0:T(8,128)(2,1)S(1)}, u32[]{:S(2)}, u32[]{:S(2)}) %collective-permute-start.62) | collective-permute-done | bytes 1179680 | tf_op jit(solution)/shard_map/ppermute | solution.py:439
  262.0 5.3 %collective-permute-done.69 = bf16[208,384]{1,0:T(8,128)(2,1)S(1)} collective-permute-done((bf16[208,384]{1,0:T(8,128)(2,1)S(1)}, bf16[208,384]{1,0:T(8,128)(2,1)S(1)}, u32[]{:S(2)}, u32[]{:S(2)}) %collective-permute-start.69) | collective-permute-done | bytes 159776 | tf_op jit(solution)/shard_map/ppermute | solution.py:439
  269.0 5.6 %shard_map.284 = (f32[208,768]{1,0:T(8,128)S(1)}, f32[8,768]{1,0:T(8,128)S(1)}, f32[208,384]{1,0:T(8,128)S(1)}, f32[208,384]{1,0:T(8,128)S(1)}, bf16[4,96,768]{2...) custom-call(s32[4]{0:T(128)S(1)} %pad_add_fusion.scal, f32[208,768]{1,0:T(8,128)S(1)} %copy-done.20, ...), custom_call_target="tpu_custom_call" | custom-call | flops 1962934272 | bytes 6463488 | tf_op jit(solution)/shard_map/pallas_call | solution.py:377
  295.3 4.2 %collective-permute-done.76 = bf16[2,96,768]{2,1,0:T(8,128)(2,1)} collective-permute-done((bf16[2,96,768]{2,1,0:T(8,128)(2,1)}, bf16[2,96,768]{2,1,0:T(8,128)(2,1)}, u32[]{:S(2)}, u32[]{:S(2)}) %collective-permute-start.76) | collective-permute-done | bytes 294944 | tf_op jit(solution)/shard_map/ppermute | solution.py:439
  299.6 11.0 %collective-permute-done.77 = bf16[2,96,768]{2,1,0:T(8,128)(2,1)} collective-permute-done((bf16[2,96,768]{2,1,0:T(8,128)(2,1)}, bf16[2,96,768]{2,1,0:T(8,128)(2,1)}, u32[]{:S(2)}, u32[]{:S(2)}) %collective-permute-start.77) | collective-permute-done | bytes 294944 | tf_op jit(solution)/shard_map/ppermute | solution.py:439
  316.8 6.9 %collective-permute-start.84 = (bf16[96,768]{1,0:T(8,128)(2,1)S(1)}, bf16[96,768]{1,0:T(8,128)(2,1)S(1)}, u32[]{:S(2)}, u32[]{:S(2)}) collective-permute-start(bf16[96,768]{1,0:T(8,128)(2,1)S(1)} %get-tuple-element.361), channel_id=1, source_target_pairs={{0,16},{4,20},{8,24},{12,28},{16,0},{20,4},{24,8},{28,12},{1,17},{... | collective-permute-start | bytes 442376 | tf_op jit(solution)/shard_map/ppermute | solution.py:439
  (326 shorter events, 179.1 us)
Async XLA Ops:
  26.1 16.9 %collective-permute-start.15 = (bf16[2,96,768]{2,1,0:T(8,128)(2,1)S(1)}, bf16[2,96,768]{2,1,0:T(8,128)(2,1)S(1)}, u32[]{:S(2)}, u32[]{:S(2)}) collective-permute-start(bf16[2,96,768]{2,1,0:T(8,128)(2,1)S(1)} %pad_maximum_fusion.8), channel_id=1, source_target_pairs={{0,24},{4,28},{8,16},{12,20},{16,8},{20,12},{24,0},{28,4},{1,25},{... | collective-permute-start | bytes 884744 | tf_op jit(solution)/shard_map/ppermute | solution.py:439
  28.6 23.2 %collective-permute-start.14 = (bf16[2,96,768]{2,1,0:T(8,128)(2,1)S(1)}, bf16[2,96,768]{2,1,0:T(8,128)(2,1)S(1)}, u32[]{:S(2)}, u32[]{:S(2)}) collective-permute-start(bf16[2,96,768]{2,1,0:T(8,128)(2,1)S(1)} %pad_maximum_fusion.8), channel_id=1, source_target_pairs={{0,16},{4,20},{8,24},{12,28},{16,0},{20,4},{24,8},{28,12},{1,17},{... | collective-permute-start | bytes 884744 | tf_op jit(solution)/shard_map/ppermute | solution.py:439
  28.6 23.2 %collective-permute-start.13 = (bf16[2,96,768]{2,1,0:T(8,128)(2,1)S(1)}, bf16[2,96,768]{2,1,0:T(8,128)(2,1)S(1)}, u32[]{:S(2)}, u32[]{:S(2)}) collective-permute-start(bf16[2,96,768]{2,1,0:T(8,128)(2,1)S(1)} %pad_maximum_fusion.8), channel_id=1, source_target_pairs={{0,8},{4,12},{8,0},{12,4},{16,24},{20,28},{24,16},{28,20},{1,9},{5... | collective-permute-start | bytes 884744 | tf_op jit(solution)/shard_map/ppermute | solution.py:439
  51.9 37.8 %collective-permute-start.22 = (bf16[4,2,96,768]{3,2,1,0:T(8,128)(2,1)S(1)}, bf16[4,2,96,768]{3,2,1,0:T(8,128)(2,1)}, u32[]{:S(2)}, u32[]{:S(2)}) collective-permute-start(bf16[4,2,96,768]{3,2,1,0:T(8,128)(2,1)S(1)} %pad_maximum_fusion.refs_0_), channel_id=1, source_target_pairs={{0,4},{4,0},{8,12},{12,8},{16,20},{20,16},{24,28},{28,24},{1,5},{5... | collective-permute-start | bytes 3538952 | tf_op jit(solution)/shard_map/ppermute | solution.py:439
  60.0 22.3 %collective-permute-start.12 = (f32[208,384]{1,0:T(8,128)S(1)}, f32[208,384]{1,0:T(8,128)S(1)}, u32[]{:S(2)}, u32[]{:S(2)}) collective-permute-start(f32[208,384]{1,0:T(8,128)S(1)} %convert_add_fusion.15), channel_id=1, source_target_pairs={{0,1},{1,0},{2,3},{3,2},{4,5},{5,4},{6,7},{7,6},{8,9},{9,8},{10,11... | collective-permute-start | bytes 958472 | tf_op jit(solution)/shard_map/ppermute | solution.py:442
  83.0 22.6 %collective-permute-start.23 = (bf16[4,96,768]{2,1,0:T(8,128)(2,1)}, bf16[4,96,768]{2,1,0:T(8,128)(2,1)}, u32[]{:S(2)}, u32[]{:S(2)}) collective-permute-start(bf16[4,96,768]{2,1,0:T(8,128)(2,1)} %pad_maximum_fusion.5.refs_7_), channel_id=1, source_target_pairs={{0,4},{4,0},{8,12},{12,8},{16,20},{20,16},{24,28},{28,24},{1,5},{5... | collective-permute-start | bytes 1769480 | tf_op jit(solution)/shard_map/ppermute | solution.py:439
  85.1 20.4 %collective-permute-start.24 = (bf16[96,768]{1,0:T(8,128)(2,1)}, bf16[96,768]{1,0:T(8,128)(2,1)}, u32[]{:S(2)}, u32[]{:S(2)}) collective-permute-start(bf16[96,768]{1,0:T(8,128)(2,1)} %get-tuple-element.193), channel_id=1, source_target_pairs={{0,8},{4,12},{8,0},{12,4},{16,24},{20,28},{24,16},{28,20},{1,9},{5... | collective-permute-start | bytes 442376 | tf_op jit(solution)/shard_map/ppermute | solution.py:439
  87.3 18.3 %collective-permute-start.25 = (bf16[96,768]{1,0:T(8,128)(2,1)}, bf16[96,768]{1,0:T(8,128)(2,1)}, u32[]{:S(2)}, u32[]{:S(2)}) collective-permute-start(bf16[96,768]{1,0:T(8,128)(2,1)} %get-tuple-element.194), channel_id=1, source_target_pairs={{0,16},{4,20},{8,24},{12,28},{16,0},{20,4},{24,8},{28,12},{1,17},{... | collective-permute-start | bytes 442376 | tf_op jit(solution)/shard_map/ppermute | solution.py:439
  87.6 18.0 %collective-permute-start.26 = (bf16[96,768]{1,0:T(8,128)(2,1)}, bf16[96,768]{1,0:T(8,128)(2,1)}, u32[]{:S(2)}, u32[]{:S(2)}) collective-permute-start(bf16[96,768]{1,0:T(8,128)(2,1)} %get-tuple-element.195), channel_id=1, source_target_pairs={{0,24},{4,28},{8,16},{12,20},{16,8},{20,12},{24,0},{28,4},{1,25},{... | collective-permute-start | bytes 442376 | tf_op jit(solution)/shard_map/ppermute | solution.py:439
  104.0 25.0 %collective-permute-start.27 = (bf16[4,96,768]{2,1,0:T(8,128)(2,1)S(1)}, bf16[4,96,768]{2,1,0:T(8,128)(2,1)S(1)}, u32[]{:S(2)}, u32[]{:S(2)}) collective-permute-start(bf16[4,96,768]{2,1,0:T(8,128)(2,1)S(1)} %pad_maximum_fusion.6.refs_14_), channel_id=1, source_target_pairs={{0,4},{4,0},{8,12},{12,8},{16,20},{20,16},{24,28},{28,24},{1,5},{5... | collective-permute-start | bytes 1769480 | tf_op jit(solution)/shard_map/ppermute | solution.py:439
  105.6 23.4 %collective-permute-start.28 = (bf16[208,384]{1,0:T(8,128)(2,1)}, bf16[208,384]{1,0:T(8,128)(2,1)S(1)}, u32[]{:S(2)}, u32[]{:S(2)}) collective-permute-start(bf16[208,384]{1,0:T(8,128)(2,1)} %slice_select_fusion), channel_id=1, source_target_pairs={{0,8},{4,12},{8,0},{12,4},{16,24},{20,28},{24,16},{28,20},{1,9},{5... | collective-permute-start | bytes 479240 | tf_op jit(solution)/shard_map/ppermute | solution.py:439
  106.7 22.3 %collective-permute-start.29 = (bf16[208,384]{1,0:T(8,128)(2,1)}, bf16[208,384]{1,0:T(8,128)(2,1)S(1)}, u32[]{:S(2)}, u32[]{:S(2)}) collective-permute-start(bf16[208,384]{1,0:T(8,128)(2,1)} %slice_select_fusion), channel_id=1, source_target_pairs={{0,16},{4,20},{8,24},{12,28},{16,0},{20,4},{24,8},{28,12},{1,17},{... | collective-permute-start | bytes 479240 | tf_op jit(solution)/shard_map/ppermute | solution.py:439
  107.9 21.1 %collective-permute-start.30 = (bf16[208,384]{1,0:T(8,128)(2,1)}, bf16[208,384]{1,0:T(8,128)(2,1)S(1)}, u32[]{:S(2)}, u32[]{:S(2)}) collective-permute-start(bf16[208,384]{1,0:T(8,128)(2,1)} %slice_select_fusion), channel_id=1, source_target_pairs={{0,24},{4,28},{8,16},{12,20},{16,8},{20,12},{24,0},{28,4},{1,25},{... | collective-permute-start | bytes 479240 | tf_op jit(solution)/shard_map/ppermute | solution.py:439
  127.5 18.7 %collective-permute-start.40 = (bf16[4,96,768]{2,1,0:T(8,128)(2,1)S(1)}, bf16[4,96,768]{2,1,0:T(8,128)(2,1)S(1)}, u32[]{:S(2)}, u32[]{:S(2)}) collective-permute-start(bf16[4,96,768]{2,1,0:T(8,128)(2,1)S(1)} %pad_maximum_fusion.7.refs_16_), channel_id=1, source_target_pairs={{0,4},{4,0},{8,12},{12,8},{16,20},{20,16},{24,28},{28,24},{1,5},{5... | collective-permute-start | bytes 1769480 | tf_op jit(solution)/shard_map/ppermute | solution.py:439
  166.5 21.3 %collective-permute-start.47 = (bf16[4,96,768]{2,1,0:T(8,128)(2,1)}, bf16[4,96,768]{2,1,0:T(8,128)(2,1)}, u32[]{:S(2)}, u32[]{:S(2)}) collective-permute-start(bf16[4,96,768]{2,1,0:T(8,128)(2,1)} %get-tuple-element.222), channel_id=1, source_target_pairs={{0,4},{4,0},{8,12},{12,8},{16,20},{20,16},{24,28},{28,24},{1,5},{5... | collective-permute-start | bytes 1769480 | tf_op jit(solution)/shard_map/ppermute | solution.py:439
  231.7 28.4 %collective-permute-start.62 = (bf16[4,2,96,768]{3,2,1,0:T(8,128)(2,1)S(1)}, bf16[4,2,96,768]{3,2,1,0:T(8,128)(2,1)S(1)}, u32[]{:S(2)}, u32[]{:S(2)}) collective-permute-start(bf16[4,2,96,768]{3,2,1,0:T(8,128)(2,1)S(1)} %get-tuple-element.242), channel_id=1, source_target_pairs={{0,4},{4,0},{8,12},{12,8},{16,20},{20,16},{24,28},{28,24},{1,5},{5... | collective-permute-start | bytes 3538952 | tf_op jit(solution)/shard_map/ppermute | solution.py:439
  242.6 19.4 %collective-permute-start.65 = (bf16[96,768]{1,0:T(8,128)(2,1)S(1)}, bf16[96,768]{1,0:T(8,128)(2,1)S(1)}, u32[]{:S(2)}, u32[]{:S(2)}) collective-permute-start(bf16[96,768]{1,0:T(8,128)(2,1)S(1)} %get-tuple-element.362), channel_id=1, source_target_pairs={{0,24},{4,28},{8,16},{12,20},{16,8},{20,12},{24,0},{28,4},{1,25},{... | collective-permute-start | bytes 442376 | tf_op jit(solution)/shard_map/ppermute | solution.py:439
  244.8 17.2 %collective-permute-start.61 = (f32[208,384]{1,0:T(8,128)S(1)}, f32[208,384]{1,0:T(8,128)S(1)}, u32[]{:S(2)}, u32[]{:S(2)}) collective-permute-start(f32[208,384]{1,0:T(8,128)S(1)} %convert_add_fusion.12.refs_1_), channel_id=1, source_target_pairs={{0,1},{1,0},{2,3},{3,2},{4,5},{5,4},{6,7},{7,6},{8,9},{9,8},{10,11... | collective-permute-start | bytes 958472 | tf_op jit(solution)/shard_map/ppermute | solution.py:442
  245.2 16.8 %collective-permute-start.67 = (bf16[208,384]{1,0:T(8,128)(2,1)S(1)}, bf16[208,384]{1,0:T(8,128)(2,1)S(1)}, u32[]{:S(2)}, u32[]{:S(2)}) collective-permute-start(bf16[208,384]{1,0:T(8,128)(2,1)S(1)} %get-tuple-element.353), channel_id=1, source_target_pairs={{0,8},{4,12},{8,0},{12,4},{16,24},{20,28},{24,16},{28,20},{1,9},{5... | collective-permute-start | bytes 479240 | tf_op jit(solution)/shard_map/ppermute | solution.py:439
  286.8 23.8 %collective-permute-start.77 = (bf16[2,96,768]{2,1,0:T(8,128)(2,1)}, bf16[2,96,768]{2,1,0:T(8,128)(2,1)}, u32[]{:S(2)}, u32[]{:S(2)}) collective-permute-start(bf16[2,96,768]{2,1,0:T(8,128)(2,1)} %get-tuple-element.339), channel_id=1, source_target_pairs={{0,16},{4,20},{8,24},{12,28},{16,0},{20,4},{24,8},{28,12},{1,17},{... | collective-permute-start | bytes 884744 | tf_op jit(solution)/shard_map/ppermute | solution.py:439
  288.1 22.4 %collective-permute-start.78 = (bf16[2,96,768]{2,1,0:T(8,128)(2,1)}, bf16[2,96,768]{2,1,0:T(8,128)(2,1)S(1)}, u32[]{:S(2)}, u32[]{:S(2)}) collective-permute-start(bf16[2,96,768]{2,1,0:T(8,128)(2,1)} %get-tuple-element.338), channel_id=1, source_target_pairs={{0,24},{4,28},{8,16},{12,20},{16,8},{20,12},{24,0},{28,4},{1,25},{... | collective-permute-start | bytes 884744 | tf_op jit(solution)/shard_map/ppermute | solution.py:439
  291.1 19.5 %collective-permute-start.74 = (f32[208,384]{1,0:T(8,128)S(1)}, f32[208,384]{1,0:T(8,128)S(1)}, u32[]{:S(2)}, u32[]{:S(2)}) collective-permute-start(f32[208,384]{1,0:T(8,128)S(1)} %convert_add_fusion.10.own), channel_id=1, source_target_pairs={{0,1},{1,0},{2,3},{3,2},{4,5},{5,4},{6,7},{7,6},{8,9},{9,8},{10,11... | collective-permute-start | bytes 958472 | tf_op jit(solution)/shard_map/ppermute | solution.py:442
  315.0 20.3 %collective-permute-start.85 = (bf16[96,768]{1,0:T(8,128)(2,1)S(1)}, bf16[96,768]{1,0:T(8,128)(2,1)S(1)}, u32[]{:S(2)}, u32[]{:S(2)}) collective-permute-start(bf16[96,768]{1,0:T(8,128)(2,1)S(1)} %get-tuple-element.360), channel_id=1, source_target_pairs={{0,24},{4,28},{8,16},{12,20},{16,8},{20,12},{24,0},{28,4},{1,25},{... | collective-permute-start | bytes 442376 | tf_op jit(solution)/shard_map/ppermute | solution.py:439
  316.8 18.6 %collective-permute-start.84 = (bf16[96,768]{1,0:T(8,128)(2,1)S(1)}, bf16[96,768]{1,0:T(8,128)(2,1)S(1)}, u32[]{:S(2)}, u32[]{:S(2)}) collective-permute-start(bf16[96,768]{1,0:T(8,128)(2,1)S(1)} %get-tuple-element.361), channel_id=1, source_target_pairs={{0,16},{4,20},{8,24},{12,28},{16,0},{20,4},{24,8},{28,12},{1,17},{... | collective-permute-start | bytes 442376 | tf_op jit(solution)/shard_map/ppermute | solution.py:439
  (98 other events, 901.2 us)

commit v3 on v2

--- a/solution.py
+++ b/solution.py
@@ -239,14 +239,14 @@
 
 
 def plain_pull(x_ref, own, other, g_ref, rows_ref, small_ref, gain_row, core):
-    dh = join_halves(core, own[...], other[...])
+    dh = join_halves(core, own[...], other[...]).astype(f32)
     dx, dgain = norm_pull(x_ref[...], rows_ref[gain_row : gain_row + 1, :], dh)
     small = small_ref[...] + jnp.where(row_of(gain_row, small_ref.shape), dgain, 0.0)
     return g_ref[...] + dx, small
 
 
 def router_pull(tokens, x_ref, own, other, g_ref, rows_ref, routes, gain_row, core):
-    dh = join_halves(core, own[...], other[...])
+    dh = join_halves(core, own[...], other[...]).astype(f32)
     padded, model = dh.shape
     gain = rows_ref[gain_row : gain_row + 1, :]
     hat, _ = norm_parts(x_ref[...])
@@ -463,6 +463,14 @@
 
         return lax.cond(me < fsdp, stage, idle, *operands)
 
+    def fold_start(arrays):
+        arrays, bit = list(arrays), parts // 2
+        while bit > 1:
+            for a in range(bit):
+                arrays[a] = arrays[a].astype(f32) + across(arrays[a + bit].astype(bf16), bit).astype(f32)
+            bit //= 2
+        return [arrays[0], across(arrays[1].astype(bf16), 1)] if bit else arrays[:1]
+
     def fold(arrays):
         arrays, bit = list(arrays), parts // 2
         while bit:
@@ -479,11 +487,11 @@
 
     def pair(total):
         low = total.astype(bf16)
-        total = low.astype(f32) + over(low, 2).astype(f32)
+        total = (low.astype(f32) + over(low, 2).astype(f32)).astype(bf16)
         return total, over(total, 1)
 
     def joined(keep, send):
-        return pair(keep + over(send, 1))
+        return pair(keep + over(send, 1).astype(f32))
 
     def attn_pack(qkv, out):
         by_head = jnp.moveaxis(qkv.reshape(3, rows, heads, HD), 0, 2)
@@ -528,7 +536,7 @@
     grad_half = jnp.where(core == 0, grad_low[:, :half], grad_low[:, half:])
 
     stream = shape((padded, model), f32)
-    pieces = [shape((padded, half), f32)] * 2
+    pieces = [shape((padded, half), f32), shape((padded, half), bf16)]
     wide = pltpu.VMEM((model, model + 128), held)
     square = pltpu.VMEM((model, model), held)
     unit = 2 * padded * model * model
@@ -607,7 +615,7 @@
 
     block_grads = [shape((PLANES, rows, model), bf16)] * parts
     own, other = pair(added(home(d_keep, d_send)))
-    e_up, e_down = fold(expert_grads[:parts]), fold(expert_grads[parts:])
+    e_up, e_down = fold(expert_grads[:parts]), fold_start(expert_grads[parts:])
     own, other, e_up = bar(own, other, e_up)
     e_up = planes(list(e_up))
     grad2, small, keep, send, *two_sum = run(
@@ -619,7 +627,7 @@
         8 * unit,
     )
     keep, send, e_up, e_down = bar(keep, send, e_up, e_down)
-    e_down = planes(list(e_down))
+    e_down = planes(list(added(e_down)))
     two_sum = fold(two_sum)
     own, other = joined(keep, send)
     own, other, e_down, two_sum = bar(own, other, e_down, two_sum)
@@ -666,7 +674,7 @@
 
     low = jnp.where(core == 0, y_own, y_other)
     high = jnp.where(core == 0, y_other, y_own)
-    result = (stream3 + jnp.concatenate([low, high], axis=1))[:tokens]
+    result = (stream3 + jnp.concatenate([low, high], axis=1).astype(f32))[:tokens]
 
     bit0, bit1 = plane % 2 == 1, plane // 2 == 1
 

time: 340 us -> 328 us (0.965)
  waiting for transfers between devices: 152 us -> 143 us
    ppermute x56, waiting for transfers between devices: 119 us -> 105 us  [across(): return lax.ppermute(value, 'fsdp', [(i, i ^ k) for i in range(fsdp)])]
    ppermute x30, waiting for transfers between devices: 33.4 us -> 38.3 us  [over(): return lax.ppermute(value, 'tensor', [(i, i ^ k) for i in range(tensor)])]
    add x8 -> x0, other arithmetic: 3.65 us -> none  [pair(): total = low.astype(f32) + over(low, 2).astype(f32)]
    unnamed x81 -> x105, local copies, waits for them, and re-layouts: 11.3 us -> 9.69 us
  transfers between devices with their start and end apart: 86 -> 86, of which waited for: 33 -> 33; matrix products, arithmetic and copies ran while one was open for 10% -> 9% of each run, Pallas kernels for 7% -> 8%
where the time goes in v3:
time: 328 us
  waiting for transfers between devices  143 us (44%)
  starting transfers between devices  98.8 us (30%)
  Pallas kernels  43.1 us (13%)
  other arithmetic  20.3 us (6%)
  local copies, waits for them, and re-layouts  19.3 us (6%)
    ppermute x56, waiting for transfers between devices, across(): return lax.ppermute(value, 'fsdp', [(i, i ^ k) for i in range(fsdp)])  105 us
    ppermute x56, starting transfers between devices, across(): return lax.ppermute(value, 'fsdp', [(i, i ^ k) for i in range(fsdp)])  89.8 us
    pallas_call x9, Pallas kernels, run(): pl.pallas_call(kernel, out_shape=outs, in_specs=[pl.BlockSpec(memory_spac...  43.1 us
    ppermute x30, waiting for transfers between devices, over(): return lax.ppermute(value, 'tensor', [(i, i ^ k) for i in range(tensor)])  38.3 us
    unnamed x105, local copies, waits for them, and re-layouts  9.69 us
    ppermute x30, starting transfers between devices, over(): return lax.ppermute(value, 'tensor', [(i, i ^ k) for i in range(tensor)])  8.97 us
  transfers between devices with their start and end apart: 86, of which 33 were waited for; matrix products, arithmetic and copies ran while one was open for 9% of the time, Pallas kernels for 8%

profile of v3, /device:TPU:0, one launch (start us, length us, event | category | flops | bytes accessed | tf_op | source)
XLA Modules:
  0.0 327.5 jit_solution(15463661122211515105)
XLA Ops:
  3.7 5.1 %collective-permute-start.8 = (bf16[96,896]{1,0:T(8,128)(2,1)S(1)}, bf16[96,896]{1,0:T(8,128)(2,1)S(1)}, u32[]{:S(2)}, u32[]{:S(2)}) collective-permute-start(bf16[96,896]{1,0:T(8,128)(2,1)S(1)} %get-tuple-element.386), channel_id=1, source_target_pairs={{0,24},{4,28},{8,16},{12,20},{16,8},{20,12},{24,0},{28,4},{1,25},{... | collective-permute-start | bytes 516104 | tf_op jit(solution)/shard_map/ppermute | solution.py:439
  9.4 4.7 %collective-permute-done.8 = bf16[96,896]{1,0:T(8,128)(2,1)S(1)} collective-permute-done((bf16[96,896]{1,0:T(8,128)(2,1)S(1)}, bf16[96,896]{1,0:T(8,128)(2,1)S(1)}, u32[]{:S(2)}, u32[]{:S(2)}) %collective-permute-start.8) | collective-permute-done | bytes 172064 | tf_op jit(solution)/shard_map/ppermute | solution.py:439
  14.1 9.3 %collective-permute-done.7 = bf16[96,896]{1,0:T(8,128)(2,1)S(1)} collective-permute-done((bf16[96,896]{1,0:T(8,128)(2,1)S(1)}, bf16[96,896]{1,0:T(8,128)(2,1)S(1)}, u32[]{:S(2)}, u32[]{:S(2)}) %collective-permute-start.7) | collective-permute-done | bytes 172064 | tf_op jit(solution)/shard_map/ppermute | solution.py:439
  29.7 10.3 %collective-permute-done.9.refs_2_.refs_8_ = bf16[4,96,896]{2,1,0:T(8,128)(2,1)S(1)} collective-permute-done((bf16[4,96,896]{2,1,0:T(8,128)(2,1)S(1)}, bf16[4,96,896]{2,1,0:T(8,128)(2,1)S(1)}, u32[]{:S(2)}, u32[]{:S(2)}) %collective-permute-start.9) | collective-permute-done | bytes 688160 | tf_op jit(solution)/shard_map/ppermute | solution.py:439
  43.2 7.7 %collective-permute-done.14 = bf16[2,96,768]{2,1,0:T(8,128)(2,1)} collective-permute-done((bf16[2,96,768]{2,1,0:T(8,128)(2,1)S(1)}, bf16[2,96,768]{2,1,0:T(8,128)(2,1)}, u32[]{:S(2)}, u32[]{:S(2)}) %collective-permute-start.14) | collective-permute-done | bytes 294944 | tf_op jit(solution)/shard_map/ppermute | solution.py:439
  64.5 4.5 %collective-permute-done.17 = bf16[96,768]{1,0:T(8,128)(2,1)S(1)} collective-permute-done((bf16[96,768]{1,0:T(8,128)(2,1)S(1)}, bf16[96,768]{1,0:T(8,128)(2,1)S(1)}, u32[]{:S(2)}, u32[]{:S(2)}) %collective-permute-start.17) | collective-permute-done | bytes 147488 | tf_op jit(solution)/shard_map/ppermute | solution.py:439
  76.3 6.9 %collective-permute-done.20 = bf16[96,768]{1,0:T(8,128)(2,1)S(1)} collective-permute-done((bf16[96,768]{1,0:T(8,128)(2,1)S(1)}, bf16[96,768]{1,0:T(8,128)(2,1)S(1)}, u32[]{:S(2)}, u32[]{:S(2)}) %collective-permute-start.20) | collective-permute-done | bytes 147488 | tf_op jit(solution)/shard_map/ppermute | solution.py:439
  91.2 13.0 %conditional.2 = (f32[208,768]{1,0:T(8,128)}, bf16[208,384]{1,0:T(8,128)(2,1)}, bf16[208,384]{1,0:T(8,128)(2,1)}) conditional(s32[]{:T(128)} %convert_element_type.357, () %tuple.37, (s32[4]{0:T(128)S(1)}, f32[208,768]{1,0:T(8,128)S(1)}, bf16[208,384]{1,0:T(8,128)(2,1)S(1)}, bf16[208,384]{1,0:T(8,128)(2,1)S(1)}, f32[8,768]{1,0:T(8,128)S(1)}, ...), branch_computations={%region_0.1_spmd, %region_1.2_spmd} | conditional | flops 491292672 | bytes 7495824 | solution.py:464
  96.1 5.7 %collective-permute-done.1 = bf16[208,384]{1,0:T(8,128)(2,1)S(1)} collective-permute-done((bf16[208,384]{1,0:T(8,128)(2,1)S(1)}, bf16[208,384]{1,0:T(8,128)(2,1)S(1)}, u32[]{:S(2)}, u32[]{:S(2)}) %collective-permute-start.1) | collective-permute-done | bytes 159776 | tf_op jit(solution)/shard_map/cond/branch_1_fun/ppermute | solution.py:442
  111.4 15.8 %conditional.3 = (f32[208,768]{1,0:T(8,128)}, f32[208,768]{1,0:T(8,128)}, bf16[208,768]{1,0:T(8,128)(2,1)}, bf16[208,384]{1,0:T(8,128)(2,1)S(1)}) conditional(s32[]{:T(128)} %convert_element_type.357, () %tuple.36, (s32[4]{0:T(128)S(1)}, f32[208,768]{1,0:T(8,128)}, bf16[208,384]{1,0:T(8,128)(2,1)}, bf16[208,384]{1,0:T(8,128)(2,1)}, ...), branch_computations={%region_2.3_spmd, %region_3.4_spmd} | conditional | flops 741566784 | bytes 8419096 | solution.py:464
  117.7 5.3 %collective-permute-done.4 = bf16[208,384]{1,0:T(8,128)(2,1)S(1)} collective-permute-done((bf16[208,384]{1,0:T(8,128)(2,1)S(1)}, bf16[208,384]{1,0:T(8,128)(2,1)S(1)}, u32[]{:S(2)}, u32[]{:S(2)}) %collective-permute-start.4) | collective-permute-done | bytes 159776 | tf_op jit(solution)/shard_map/cond/branch_1_fun/ppermute | solution.py:442
  137.0 6.6 %collective-permute-done.32.refs_2_ = bf16[208,384]{1,0:T(8,128)(2,1)S(1)} collective-permute-done((bf16[208,384]{1,0:T(8,128)(2,1)S(1)}, bf16[208,384]{1,0:T(8,128)(2,1)S(1)}, u32[]{:S(2)}, u32[]{:S(2)}) %collective-permute-start.32) | collective-permute-done | bytes 159776 | tf_op jit(solution)/shard_map/ppermute | solution.py:439
  147.8 10.5 %shard_map.281 = (f32[4,208,384]{2,1,0:T(8,128)S(1)}, bf16[4,208,384]{2,1,0:T(8,128)(2,1)S(1)}, f32[4,208,384]{2,1,0:T(8,128)S(1)}, bf16[4,208,384]{2,1,0:T(8,12...) custom-call(s32[4]{0:T(128)S(1)} %pad_add_fusion.scal, ...), custom_call_target="tpu_custom_call" | custom-call | flops 5888802816 | bytes 11108352 | tf_op jit(solution)/shard_map/pallas_call | solution.py:377
  169.7 9.5 %collective-permute-done.43 = bf16[208,384]{1,0:T(8,128)(2,1)S(1)} collective-permute-done((bf16[208,384]{1,0:T(8,128)(2,1)S(1)}, bf16[208,384]{1,0:T(8,128)(2,1)S(1)}, u32[]{:S(2)}, u32[]{:S(2)}) %collective-permute-start.43) | collective-permute-done | bytes 159776 | tf_op jit(solution)/shard_map/ppermute | solution.py:439
  180.9 4.6 %collective-permute-done.45 = bf16[208,384]{1,0:T(8,128)(2,1)} collective-permute-done((bf16[208,384]{1,0:T(8,128)(2,1)S(1)}, bf16[208,384]{1,0:T(8,128)(2,1)}, u32[]{:S(2)}, u32[]{:S(2)}) %collective-permute-start.45) | collective-permute-done | bytes 159776 | tf_op jit(solution)/shard_map/ppermute | solution.py:442
  192.5 7.5 %shard_map.282 = (f32[208,768]{1,0:T(8,128)S(1)}, f32[8,768]{1,0:T(8,128)S(1)}, f32[208,384]{1,0:T(8,128)S(1)}, bf16[208,384]{1,0:T(8,128)(2,1)S(1)}, bf16[4,96,...) custom-call(s32[4]{0:T(128)S(1)} %pad_add_fusion.scal, f32[208,768]{1,0:T(8,128)S(1)} %copy-done.22, ...), custom_call_target="tpu_custom_call" | custom-call | flops 1962934272 | bytes 5764736 | tf_op jit(solution)/shard_map/pallas_call | solution.py:377
  215.0 4.5 %collective-permute-done.56 = bf16[96,768]{1,0:T(8,128)(2,1)S(1)} collective-permute-done((bf16[96,768]{1,0:T(8,128)(2,1)S(1)}, bf16[96,768]{1,0:T(8,128)(2,1)S(1)}, u32[]{:S(2)}, u32[]{:S(2)}) %collective-permute-start.56) | collective-permute-done | bytes 147488 | tf_op jit(solution)/shard_map/ppermute | solution.py:439
  230.3 4.5 %collective-permute-done.60 = bf16[208,384]{1,0:T(8,128)(2,1)S(1)} collective-permute-done((bf16[208,384]{1,0:T(8,128)(2,1)S(1)}, bf16[208,384]{1,0:T(8,128)(2,1)S(1)}, u32[]{:S(2)}, u32[]{:S(2)}) %collective-permute-start.60) | collective-permute-done | bytes 159776 | tf_op jit(solution)/shard_map/ppermute | solution.py:442
  239.6 12.6 %collective-permute-done.62 = bf16[4,2,96,768]{3,2,1,0:T(8,128)(2,1)S(1)} collective-permute-done((bf16[4,2,96,768]{3,2,1,0:T(8,128)(2,1)S(1)}, bf16[4,2,96,768]{3,2,1,0:T(8,128)(2,1)S(1)}, u32[]{:S(2)}, u32[]{:S(2)}) %collective-permute-start.62) | collective-permute-done | bytes 1179680 | tf_op jit(solution)/shard_map/ppermute | solution.py:439
  262.9 7.1 %shard_map.284 = (f32[208,768]{1,0:T(8,128)S(1)}, f32[8,768]{1,0:T(8,128)S(1)}, f32[208,384]{1,0:T(8,128)S(1)}, bf16[208,384]{1,0:T(8,128)(2,1)S(1)}, bf16[4,96,...) custom-call(s32[4]{0:T(128)S(1)} %pad_add_fusion.scal, f32[208,768]{1,0:T(8,128)} %get-tuple-element.189.x_ref.refs_0_, ...), custom_call_target="tpu_custom_call" | custom-call | flops 1962934272 | bytes 5984256 | tf_op jit(solution)/shard_map/pallas_call | solution.py:377
  284.2 4.8 %collective-permute-done.73 = bf16[208,384]{1,0:T(8,128)(2,1)S(1)} collective-permute-done((bf16[208,384]{1,0:T(8,128)(2,1)S(1)}, bf16[208,384]{1,0:T(8,128)(2,1)S(1)}, u32[]{:S(2)}, u32[]{:S(2)}) %collective-permute-start.73) | collective-permute-done | bytes 159776 | tf_op jit(solution)/shard_map/ppermute | solution.py:442
  291.7 7.8 %collective-permute-done.77 = bf16[2,96,768]{2,1,0:T(8,128)(2,1)} collective-permute-done((bf16[2,96,768]{2,1,0:T(8,128)(2,1)}, bf16[2,96,768]{2,1,0:T(8,128)(2,1)}, u32[]{:S(2)}, u32[]{:S(2)}) %collective-permute-start.77) | collective-permute-done | bytes 294944 | tf_op jit(solution)/shard_map/ppermute | solution.py:439
  305.4 5.6 %collective-permute-start.84 = (bf16[96,768]{1,0:T(8,128)(2,1)S(1)}, bf16[96,768]{1,0:T(8,128)(2,1)S(1)}, u32[]{:S(2)}, u32[]{:S(2)}) collective-permute-start(bf16[96,768]{1,0:T(8,128)(2,1)S(1)} %get-tuple-element.363), channel_id=1, source_target_pairs={{0,16},{4,20},{8,24},{12,28},{16,0},{20,4},{24,8},{28,12},{1,17},{... | collective-permute-start | bytes 442376 | tf_op jit(solution)/shard_map/ppermute | solution.py:439
  318.1 4.5 %collective-permute-start.83 = (bf16[96,768]{1,0:T(8,128)(2,1)S(1)}, bf16[96,768]{1,0:T(8,128)(2,1)S(1)}, u32[]{:S(2)}, u32[]{:S(2)}) collective-permute-start(bf16[96,768]{1,0:T(8,128)(2,1)S(1)} %get-tuple-element.361), channel_id=1, source_target_pairs={{0,8},{4,12},{8,0},{12,4},{16,24},{20,28},{24,16},{28,20},{1,9},{5... | collective-permute-start | bytes 442376 | tf_op jit(solution)/shard_map/ppermute | solution.py:439
  (349 shorter events, 175.2 us)
Async XLA Ops:
  27.6 23.3 %collective-permute-start.14 = (bf16[2,96,768]{2,1,0:T(8,128)(2,1)S(1)}, bf16[2,96,768]{2,1,0:T(8,128)(2,1)}, u32[]{:S(2)}, u32[]{:S(2)}) collective-permute-start(bf16[2,96,768]{2,1,0:T(8,128)(2,1)S(1)} %pad_maximum_fusion.8), channel_id=1, source_target_pairs={{0,16},{4,20},{8,24},{12,28},{16,0},{20,4},{24,8},{28,12},{1,17},{... | collective-permute-start | bytes 884744 | tf_op jit(solution)/shard_map/ppermute | solution.py:439
  27.6 23.3 %collective-permute-start.13 = (bf16[2,96,768]{2,1,0:T(8,128)(2,1)S(1)}, bf16[2,96,768]{2,1,0:T(8,128)(2,1)}, u32[]{:S(2)}, u32[]{:S(2)}) collective-permute-start(bf16[2,96,768]{2,1,0:T(8,128)(2,1)S(1)} %pad_maximum_fusion.8), channel_id=1, source_target_pairs={{0,8},{4,12},{8,0},{12,4},{16,24},{20,28},{24,16},{28,20},{1,9},{5... | collective-permute-start | bytes 884744 | tf_op jit(solution)/shard_map/ppermute | solution.py:439
  53.1 38.1 %collective-permute-start.22 = (bf16[4,2,96,768]{3,2,1,0:T(8,128)(2,1)}, bf16[4,2,96,768]{3,2,1,0:T(8,128)(2,1)}, u32[]{:S(2)}, u32[]{:S(2)}) collective-permute-start(bf16[4,2,96,768]{3,2,1,0:T(8,128)(2,1)} %pad_maximum_fusion.refs_0_), channel_id=1, source_target_pairs={{0,4},{4,0},{8,12},{12,8},{16,20},{20,16},{24,28},{28,24},{1,5},{5... | collective-permute-start | bytes 3538952 | tf_op jit(solution)/shard_map/ppermute | solution.py:439
  60.9 22.4 %collective-permute-start.12 = (bf16[208,384]{1,0:T(8,128)(2,1)S(1)}, bf16[208,384]{1,0:T(8,128)(2,1)S(1)}, u32[]{:S(2)}, u32[]{:S(2)}) collective-permute-start(bf16[208,384]{1,0:T(8,128)(2,1)S(1)} %add_convert_fusion.13), channel_id=1, source_target_pairs={{0,1},{1,0},{2,3},{3,2},{4,5},{5,4},{6,7},{7,6},{8,9},{9,8},{10,11... | collective-permute-start | bytes 479240 | tf_op jit(solution)/shard_map/ppermute | solution.py:442
  83.2 22.5 %collective-permute-start.23 = (bf16[4,96,768]{2,1,0:T(8,128)(2,1)}, bf16[4,96,768]{2,1,0:T(8,128)(2,1)}, u32[]{:S(2)}, u32[]{:S(2)}) collective-permute-start(bf16[4,96,768]{2,1,0:T(8,128)(2,1)} %pad_maximum_fusion.4.refs_7_), channel_id=1, source_target_pairs={{0,4},{4,0},{8,12},{12,8},{16,20},{20,16},{24,28},{28,24},{1,5},{5... | collective-permute-start | bytes 1769480 | tf_op jit(solution)/shard_map/ppermute | solution.py:439
  85.5 20.3 %collective-permute-start.24 = (bf16[96,768]{1,0:T(8,128)(2,1)}, bf16[96,768]{1,0:T(8,128)(2,1)}, u32[]{:S(2)}, u32[]{:S(2)}) collective-permute-start(bf16[96,768]{1,0:T(8,128)(2,1)} %get-tuple-element.194), channel_id=1, source_target_pairs={{0,8},{4,12},{8,0},{12,4},{16,24},{20,28},{24,16},{28,20},{1,9},{5... | collective-permute-start | bytes 442376 | tf_op jit(solution)/shard_map/ppermute | solution.py:439
  87.6 18.2 %collective-permute-start.25 = (bf16[96,768]{1,0:T(8,128)(2,1)}, bf16[96,768]{1,0:T(8,128)(2,1)}, u32[]{:S(2)}, u32[]{:S(2)}) collective-permute-start(bf16[96,768]{1,0:T(8,128)(2,1)} %get-tuple-element.195), channel_id=1, source_target_pairs={{0,16},{4,20},{8,24},{12,28},{16,0},{20,4},{24,8},{28,12},{1,17},{... | collective-permute-start | bytes 442376 | tf_op jit(solution)/shard_map/ppermute | solution.py:439
  104.2 24.4 %collective-permute-start.27 = (bf16[4,96,768]{2,1,0:T(8,128)(2,1)S(1)}, bf16[4,96,768]{2,1,0:T(8,128)(2,1)S(1)}, u32[]{:S(2)}, u32[]{:S(2)}) collective-permute-start(bf16[4,96,768]{2,1,0:T(8,128)(2,1)S(1)} %pad_maximum_fusion.5.refs_14_), channel_id=1, source_target_pairs={{0,4},{4,0},{8,12},{12,8},{16,20},{20,16},{24,28},{28,24},{1,5},{5... | collective-permute-start | bytes 1769480 | tf_op jit(solution)/shard_map/ppermute | solution.py:439
  105.8 22.9 %collective-permute-start.28 = (bf16[208,384]{1,0:T(8,128)(2,1)}, bf16[208,384]{1,0:T(8,128)(2,1)S(1)}, u32[]{:S(2)}, u32[]{:S(2)}) collective-permute-start(bf16[208,384]{1,0:T(8,128)(2,1)} %slice_select_fusion), channel_id=1, source_target_pairs={{0,8},{4,12},{8,0},{12,4},{16,24},{20,28},{24,16},{28,20},{1,9},{5... | collective-permute-start | bytes 479240 | tf_op jit(solution)/shard_map/ppermute | solution.py:439
  106.9 21.8 %collective-permute-start.29 = (bf16[208,384]{1,0:T(8,128)(2,1)}, bf16[208,384]{1,0:T(8,128)(2,1)S(1)}, u32[]{:S(2)}, u32[]{:S(2)}) collective-permute-start(bf16[208,384]{1,0:T(8,128)(2,1)} %slice_select_fusion), channel_id=1, source_target_pairs={{0,16},{4,20},{8,24},{12,28},{16,0},{20,4},{24,8},{28,12},{1,17},{... | collective-permute-start | bytes 479240 | tf_op jit(solution)/shard_map/ppermute | solution.py:439
  108.1 20.5 %collective-permute-start.30 = (bf16[208,384]{1,0:T(8,128)(2,1)}, bf16[208,384]{1,0:T(8,128)(2,1)S(1)}, u32[]{:S(2)}, u32[]{:S(2)}) collective-permute-start(bf16[208,384]{1,0:T(8,128)(2,1)} %slice_select_fusion), channel_id=1, source_target_pairs={{0,24},{4,28},{8,16},{12,20},{16,8},{20,12},{24,0},{28,4},{1,25},{... | collective-permute-start | bytes 479240 | tf_op jit(solution)/shard_map/ppermute | solution.py:439
  127.2 18.6 %collective-permute-start.40 = (bf16[4,96,768]{2,1,0:T(8,128)(2,1)S(1)}, bf16[4,96,768]{2,1,0:T(8,128)(2,1)S(1)}, u32[]{:S(2)}, u32[]{:S(2)}) collective-permute-start(bf16[4,96,768]{2,1,0:T(8,128)(2,1)S(1)} %pad_maximum_fusion.6.refs_16_), channel_id=1, source_target_pairs={{0,4},{4,0},{8,12},{12,8},{16,20},{20,16},{24,28},{28,24},{1,5},{5... | collective-permute-start | bytes 1769480 | tf_op jit(solution)/shard_map/ppermute | solution.py:439
  165.3 21.3 %collective-permute-start.47 = (bf16[4,96,768]{2,1,0:T(8,128)(2,1)}, bf16[4,96,768]{2,1,0:T(8,128)(2,1)}, u32[]{:S(2)}, u32[]{:S(2)}) collective-permute-start(bf16[4,96,768]{2,1,0:T(8,128)(2,1)} %get-tuple-element.223), channel_id=1, source_target_pairs={{0,4},{4,0},{8,12},{12,8},{16,20},{20,16},{24,28},{28,24},{1,5},{5... | collective-permute-start | bytes 1769480 | tf_op jit(solution)/shard_map/ppermute | solution.py:439
  180.0 20.8 %collective-permute-start.51 = (bf16[4,96,768]{2,1,0:T(8,128)(2,1)}, bf16[4,96,768]{2,1,0:T(8,128)(2,1)S(1)}, u32[]{:S(2)}, u32[]{:S(2)}) collective-permute-start(bf16[4,96,768]{2,1,0:T(8,128)(2,1)} %copy-done.12), channel_id=1, source_target_pairs={{0,4},{4,0},{8,12},{12,8},{16,20},{20,16},{24,28},{28,24},{1,5},{5... | collective-permute-start | bytes 1769480 | tf_op jit(solution)/shard_map/ppermute | solution.py:439
  223.9 28.4 %collective-permute-start.62 = (bf16[4,2,96,768]{3,2,1,0:T(8,128)(2,1)S(1)}, bf16[4,2,96,768]{3,2,1,0:T(8,128)(2,1)S(1)}, u32[]{:S(2)}, u32[]{:S(2)}) collective-permute-start(bf16[4,2,96,768]{3,2,1,0:T(8,128)(2,1)S(1)} %get-tuple-element.244), channel_id=1, source_target_pairs={{0,4},{4,0},{8,12},{12,8},{16,20},{20,16},{24,28},{28,24},{1,5},{5... | collective-permute-start | bytes 3538952 | tf_op jit(solution)/shard_map/ppermute | solution.py:439
  234.8 20.9 %collective-permute-start.65 = (bf16[96,768]{1,0:T(8,128)(2,1)S(1)}, bf16[96,768]{1,0:T(8,128)(2,1)S(1)}, u32[]{:S(2)}, u32[]{:S(2)}) collective-permute-start(bf16[96,768]{1,0:T(8,128)(2,1)S(1)} %get-tuple-element.364), channel_id=1, source_target_pairs={{0,24},{4,28},{8,16},{12,20},{16,8},{20,12},{24,0},{28,4},{1,25},{... | collective-permute-start | bytes 442376 | tf_op jit(solution)/shard_map/ppermute | solution.py:439
  237.0 18.7 %collective-permute-start.61 = (bf16[208,384]{1,0:T(8,128)(2,1)S(1)}, bf16[208,384]{1,0:T(8,128)(2,1)S(1)}, u32[]{:S(2)}, u32[]{:S(2)}) collective-permute-start(bf16[208,384]{1,0:T(8,128)(2,1)S(1)} %add_convert_fusion.8.refs_1_), channel_id=1, source_target_pairs={{0,1},{1,0},{2,3},{3,2},{4,5},{5,4},{6,7},{7,6},{8,9},{9,8},{10,11... | collective-permute-start | bytes 479240 | tf_op jit(solution)/shard_map/ppermute | solution.py:442
  237.3 18.4 %collective-permute-start.67 = (bf16[208,384]{1,0:T(8,128)(2,1)S(1)}, bf16[208,384]{1,0:T(8,128)(2,1)S(1)}, u32[]{:S(2)}, u32[]{:S(2)}) collective-permute-start(bf16[208,384]{1,0:T(8,128)(2,1)S(1)} %get-tuple-element.355), channel_id=1, source_target_pairs={{0,8},{4,12},{8,0},{12,4},{16,24},{20,28},{24,16},{28,20},{1,9},{5... | collective-permute-start | bytes 479240 | tf_op jit(solution)/shard_map/ppermute | solution.py:439
  270.1 20.4 %collective-permute-start.75 = (bf16[4,96,768]{2,1,0:T(8,128)(2,1)}, bf16[4,96,768]{2,1,0:T(8,128)(2,1)}, u32[]{:S(2)}, u32[]{:S(2)}) collective-permute-start(bf16[4,96,768]{2,1,0:T(8,128)(2,1)} %get-tuple-element.261), channel_id=1, source_target_pairs={{0,4},{4,0},{8,12},{12,8},{16,20},{20,16},{24,28},{28,24},{1,5},{5... | collective-permute-start | bytes 1769480 | tf_op jit(solution)/shard_map/ppermute | solution.py:439
  271.9 19.8 %collective-permute-start.76 = (bf16[2,96,768]{2,1,0:T(8,128)(2,1)}, bf16[2,96,768]{2,1,0:T(8,128)(2,1)}, u32[]{:S(2)}, u32[]{:S(2)}) collective-permute-start(bf16[2,96,768]{2,1,0:T(8,128)(2,1)} %get-tuple-element.342), channel_id=1, source_target_pairs={{0,8},{4,12},{8,0},{12,4},{16,24},{20,28},{24,16},{28,20},{1,9},{5... | collective-permute-start | bytes 884744 | tf_op jit(solution)/shard_map/ppermute | solution.py:439
  275.8 23.7 %collective-permute-start.77 = (bf16[2,96,768]{2,1,0:T(8,128)(2,1)}, bf16[2,96,768]{2,1,0:T(8,128)(2,1)}, u32[]{:S(2)}, u32[]{:S(2)}) collective-permute-start(bf16[2,96,768]{2,1,0:T(8,128)(2,1)} %get-tuple-element.341), channel_id=1, source_target_pairs={{0,16},{4,20},{8,24},{12,28},{16,0},{20,4},{24,8},{28,12},{1,17},{... | collective-permute-start | bytes 884744 | tf_op jit(solution)/shard_map/ppermute | solution.py:439
  278.1 21.4 %collective-permute-start.78 = (bf16[2,96,768]{2,1,0:T(8,128)(2,1)S(1)}, bf16[2,96,768]{2,1,0:T(8,128)(2,1)S(1)}, u32[]{:S(2)}, u32[]{:S(2)}) collective-permute-start(bf16[2,96,768]{2,1,0:T(8,128)(2,1)S(1)} %get-tuple-element.340), channel_id=1, source_target_pairs={{0,24},{4,28},{8,16},{12,20},{16,8},{20,12},{24,0},{28,4},{1,25},{... | collective-permute-start | bytes 884744 | tf_op jit(solution)/shard_map/ppermute | solution.py:439
  303.7 20.3 %collective-permute-start.85 = (bf16[96,768]{1,0:T(8,128)(2,1)S(1)}, bf16[96,768]{1,0:T(8,128)(2,1)S(1)}, u32[]{:S(2)}, u32[]{:S(2)}) collective-permute-start(bf16[96,768]{1,0:T(8,128)(2,1)S(1)} %get-tuple-element.362), channel_id=1, source_target_pairs={{0,24},{4,28},{8,16},{12,20},{16,8},{20,12},{24,0},{28,4},{1,25},{... | collective-permute-start | bytes 442376 | tf_op jit(solution)/shard_map/ppermute | solution.py:439
  305.4 18.6 %collective-permute-start.84 = (bf16[96,768]{1,0:T(8,128)(2,1)S(1)}, bf16[96,768]{1,0:T(8,128)(2,1)S(1)}, u32[]{:S(2)}, u32[]{:S(2)}) collective-permute-start(bf16[96,768]{1,0:T(8,128)(2,1)S(1)} %get-tuple-element.363), channel_id=1, source_target_pairs={{0,16},{4,20},{8,24},{12,28},{16,0},{20,4},{24,8},{28,12},{1,17},{... | collective-permute-start | bytes 442376 | tf_op jit(solution)/shard_map/ppermute | solution.py:439
  (110 other events, 1154.3 us)

commit v4 on v3

--- a/solution.py
+++ b/solution.py
@@ -657,6 +657,7 @@
         [wide, square],
         8 * unit,
     )
+    keep, send, mlp_sum[1] = bar(keep, send, mlp_sum[1])
     one_sum = fold(one_sum)
     own, other = joined(keep, send)
     own, other, one_sum, mlp_sum = bar(own, other, one_sum, mlp_sum)

time: 328 us -> 324 us (0.988)
    unnamed x105 -> x87, local copies, waits for them, and re-layouts: 9.69 us -> 8.9 us
  transfers between devices with their start and end apart: 86 -> 86, of which waited for: 33 -> 33; matrix products, arithmetic and copies ran while one was open for 9% -> 8% of each run, Pallas kernels for 8% -> 8%
where the time goes in v4:
time: 324 us; the launch traced here: 323 us
  waiting for transfers between devices  143 us (44%)
  starting transfers between devices  101 us (31%)
  Pallas kernels  41.6 us (13%)
  local copies, waits for them, and re-layouts  18.6 us (6%)
  other arithmetic  17.2 us (5%)
    ppermute x56, waiting for transfers between devices, across(): return lax.ppermute(value, 'fsdp', [(i, i ^ k) for i in range(fsdp)])  106 us
    ppermute x56, starting transfers between devices, across(): return lax.ppermute(value, 'fsdp', [(i, i ^ k) for i in range(fsdp)])  91.1 us
    pallas_call x9, Pallas kernels, run(): pl.pallas_call(kernel, out_shape=outs, in_specs=[pl.BlockSpec(memory_spac...  41.6 us
    ppermute x30, waiting for transfers between devices, over(): return lax.ppermute(value, 'tensor', [(i, i ^ k) for i in range(tensor)])  36.9 us
    ppermute x30, starting transfers between devices, over(): return lax.ppermute(value, 'tensor', [(i, i ^ k) for i in range(tensor)])  9.5 us
    unnamed x87, local copies, waits for them, and re-layouts  8.9 us
  transfers between devices with their start and end apart: 86, of which 33 were waited for; matrix products, arithmetic and copies ran while one was open for 8% of the time, Pallas kernels for 8%

profile of v4, /device:TPU:0, one launch (start us, length us, event | category | flops | bytes accessed | tf_op | source)
XLA Modules:
  0.0 323.2 jit_solution(15064445935750228204)
XLA Ops:
  3.7 5.1 %collective-permute-start.8 = (bf16[96,896]{1,0:T(8,128)(2,1)S(1)}, bf16[96,896]{1,0:T(8,128)(2,1)S(1)}, u32[]{:S(2)}, u32[]{:S(2)}) collective-permute-start(bf16[96,896]{1,0:T(8,128)(2,1)S(1)} %get-tuple-element.392), channel_id=1, source_target_pairs={{0,24},{4,28},{8,16},{12,20},{16,8},{20,12},{24,0},{28,4},{1,25},{... | collective-permute-start | bytes 516104 | tf_op jit(solution)/shard_map/ppermute | solution.py:439
  9.4 4.7 %collective-permute-done.8 = bf16[96,896]{1,0:T(8,128)(2,1)S(1)} collective-permute-done((bf16[96,896]{1,0:T(8,128)(2,1)S(1)}, bf16[96,896]{1,0:T(8,128)(2,1)S(1)}, u32[]{:S(2)}, u32[]{:S(2)}) %collective-permute-start.8) | collective-permute-done | bytes 172064 | tf_op jit(solution)/shard_map/ppermute | solution.py:439
  14.1 9.3 %collective-permute-done.7 = bf16[96,896]{1,0:T(8,128)(2,1)S(1)} collective-permute-done((bf16[96,896]{1,0:T(8,128)(2,1)S(1)}, bf16[96,896]{1,0:T(8,128)(2,1)S(1)}, u32[]{:S(2)}, u32[]{:S(2)}) %collective-permute-start.7) | collective-permute-done | bytes 172064 | tf_op jit(solution)/shard_map/ppermute | solution.py:439
  29.7 10.3 %collective-permute-done.9.refs_2_.refs_8_ = bf16[4,96,896]{2,1,0:T(8,128)(2,1)S(1)} collective-permute-done((bf16[4,96,896]{2,1,0:T(8,128)(2,1)S(1)}, bf16[4,96,896]{2,1,0:T(8,128)(2,1)S(1)}, u32[]{:S(2)}, u32[]{:S(2)}) %collective-permute-start.9) | collective-permute-done | bytes 688160 | tf_op jit(solution)/shard_map/ppermute | solution.py:439
  43.1 7.8 %collective-permute-done.14 = bf16[2,96,768]{2,1,0:T(8,128)(2,1)} collective-permute-done((bf16[2,96,768]{2,1,0:T(8,128)(2,1)S(1)}, bf16[2,96,768]{2,1,0:T(8,128)(2,1)}, u32[]{:S(2)}, u32[]{:S(2)}) %collective-permute-start.14) | collective-permute-done | bytes 294944 | tf_op jit(solution)/shard_map/ppermute | solution.py:439
  64.5 4.5 %collective-permute-done.17 = bf16[96,768]{1,0:T(8,128)(2,1)S(1)} collective-permute-done((bf16[96,768]{1,0:T(8,128)(2,1)S(1)}, bf16[96,768]{1,0:T(8,128)(2,1)S(1)}, u32[]{:S(2)}, u32[]{:S(2)}) %collective-permute-start.17) | collective-permute-done | bytes 147488 | tf_op jit(solution)/shard_map/ppermute | solution.py:439
  76.3 6.9 %collective-permute-done.20 = bf16[96,768]{1,0:T(8,128)(2,1)S(1)} collective-permute-done((bf16[96,768]{1,0:T(8,128)(2,1)S(1)}, bf16[96,768]{1,0:T(8,128)(2,1)S(1)}, u32[]{:S(2)}, u32[]{:S(2)}) %collective-permute-start.20) | collective-permute-done | bytes 147488 | tf_op jit(solution)/shard_map/ppermute | solution.py:439
  91.2 13.0 %conditional.2 = (f32[208,768]{1,0:T(8,128)}, bf16[208,384]{1,0:T(8,128)(2,1)}, bf16[208,384]{1,0:T(8,128)(2,1)}) conditional(s32[]{:T(128)} %convert_element_type.357, () %tuple.38, (s32[4]{0:T(128)S(1)}, f32[208,768]{1,0:T(8,128)S(1)}, bf16[208,384]{1,0:T(8,128)(2,1)S(1)}, bf16[208,384]{1,0:T(8,128)(2,1)S(1)}, f32[8,768]{1,0:T(8,128)S(1)}, ...), branch_computations={%region_0.1_spmd, %region_1.2_spmd} | conditional | flops 491292672 | bytes 7495824 | solution.py:464
  96.1 5.7 %collective-permute-done.1 = bf16[208,384]{1,0:T(8,128)(2,1)S(1)} collective-permute-done((bf16[208,384]{1,0:T(8,128)(2,1)S(1)}, bf16[208,384]{1,0:T(8,128)(2,1)S(1)}, u32[]{:S(2)}, u32[]{:S(2)}) %collective-permute-start.1) | collective-permute-done | bytes 159776 | tf_op jit(solution)/shard_map/cond/branch_1_fun/ppermute | solution.py:442
  111.4 15.8 %conditional.3 = (f32[208,768]{1,0:T(8,128)}, f32[208,768]{1,0:T(8,128)}, bf16[208,768]{1,0:T(8,128)(2,1)}, bf16[208,384]{1,0:T(8,128)(2,1)S(1)}) conditional(s32[]{:T(128)} %convert_element_type.357, () %tuple.37, (s32[4]{0:T(128)S(1)}, f32[208,768]{1,0:T(8,128)}, bf16[208,384]{1,0:T(8,128)(2,1)}, bf16[208,384]{1,0:T(8,128)(2,1)}, ...), branch_computations={%region_2.3_spmd, %region_3.4_spmd} | conditional | flops 741566784 | bytes 8419096 | solution.py:464
  117.7 5.4 %collective-permute-done.4 = bf16[208,384]{1,0:T(8,128)(2,1)S(1)} collective-permute-done((bf16[208,384]{1,0:T(8,128)(2,1)S(1)}, bf16[208,384]{1,0:T(8,128)(2,1)S(1)}, u32[]{:S(2)}, u32[]{:S(2)}) %collective-permute-start.4) | collective-permute-done | bytes 159776 | tf_op jit(solution)/shard_map/cond/branch_1_fun/ppermute | solution.py:442
  137.0 6.6 %collective-permute-done.32.refs_2_ = bf16[208,384]{1,0:T(8,128)(2,1)S(1)} collective-permute-done((bf16[208,384]{1,0:T(8,128)(2,1)S(1)}, bf16[208,384]{1,0:T(8,128)(2,1)S(1)}, u32[]{:S(2)}, u32[]{:S(2)}) %collective-permute-start.32) | collective-permute-done | bytes 159776 | tf_op jit(solution)/shard_map/ppermute | solution.py:439
  147.8 10.5 %shard_map.281 = (f32[4,208,384]{2,1,0:T(8,128)S(1)}, bf16[4,208,384]{2,1,0:T(8,128)(2,1)S(1)}, f32[4,208,384]{2,1,0:T(8,128)S(1)}, bf16[4,208,384]{2,1,0:T(8,12...) custom-call(s32[4]{0:T(128)S(1)} %pad_add_fusion.scal, ...), custom_call_target="tpu_custom_call" | custom-call | flops 5888802816 | bytes 11108352 | tf_op jit(solution)/shard_map/pallas_call | solution.py:377
  169.7 9.5 %collective-permute-done.43 = bf16[208,384]{1,0:T(8,128)(2,1)S(1)} collective-permute-done((bf16[208,384]{1,0:T(8,128)(2,1)S(1)}, bf16[208,384]{1,0:T(8,128)(2,1)S(1)}, u32[]{:S(2)}, u32[]{:S(2)}) %collective-permute-start.43) | collective-permute-done | bytes 159776 | tf_op jit(solution)/shard_map/ppermute | solution.py:439
  180.9 4.6 %collective-permute-done.45 = bf16[208,384]{1,0:T(8,128)(2,1)} collective-permute-done((bf16[208,384]{1,0:T(8,128)(2,1)S(1)}, bf16[208,384]{1,0:T(8,128)(2,1)}, u32[]{:S(2)}, u32[]{:S(2)}) %collective-permute-start.45) | collective-permute-done | bytes 159776 | tf_op jit(solution)/shard_map/ppermute | solution.py:442
  192.5 7.5 %shard_map.282 = (f32[208,768]{1,0:T(8,128)S(1)}, f32[8,768]{1,0:T(8,128)S(1)}, f32[208,384]{1,0:T(8,128)S(1)}, bf16[208,384]{1,0:T(8,128)(2,1)S(1)}, bf16[4,96,...) custom-call(s32[4]{0:T(128)S(1)} %pad_add_fusion.scal, f32[208,768]{1,0:T(8,128)S(1)} %copy-done.20, ...), custom_call_target="tpu_custom_call" | custom-call | flops 1962934272 | bytes 5764736 | tf_op jit(solution)/shard_map/pallas_call | solution.py:377
  215.0 4.5 %collective-permute-done.56 = bf16[96,768]{1,0:T(8,128)(2,1)S(1)} collective-permute-done((bf16[96,768]{1,0:T(8,128)(2,1)S(1)}, bf16[96,768]{1,0:T(8,128)(2,1)S(1)}, u32[]{:S(2)}, u32[]{:S(2)}) %collective-permute-start.56) | collective-permute-done | bytes 147488 | tf_op jit(solution)/shard_map/ppermute | solution.py:439
  230.3 4.5 %collective-permute-done.60 = bf16[208,384]{1,0:T(8,128)(2,1)S(1)} collective-permute-done((bf16[208,384]{1,0:T(8,128)(2,1)S(1)}, bf16[208,384]{1,0:T(8,128)(2,1)S(1)}, u32[]{:S(2)}, u32[]{:S(2)}) %collective-permute-start.60) | collective-permute-done | bytes 159776 | tf_op jit(solution)/shard_map/ppermute | solution.py:442
  239.7 12.7 %collective-permute-done.62 = bf16[4,2,96,768]{3,2,1,0:T(8,128)(2,1)S(1)} collective-permute-done((bf16[4,2,96,768]{3,2,1,0:T(8,128)(2,1)S(1)}, bf16[4,2,96,768]{3,2,1,0:T(8,128)(2,1)S(1)}, u32[]{:S(2)}, u32[]{:S(2)}) %collective-permute-start.62) | collective-permute-done | bytes 1179680 | tf_op jit(solution)/shard_map/ppermute | solution.py:439
  254.3 5.6 %collective-permute-done.69 = bf16[208,384]{1,0:T(8,128)(2,1)S(1)} collective-permute-done((bf16[208,384]{1,0:T(8,128)(2,1)S(1)}, bf16[208,384]{1,0:T(8,128)(2,1)S(1)}, u32[]{:S(2)}, u32[]{:S(2)}) %collective-permute-start.69) | collective-permute-done | bytes 159776 | tf_op jit(solution)/shard_map/ppermute | solution.py:439
  265.5 5.6 %shard_map.284 = (f32[208,768]{1,0:T(8,128)S(1)}, f32[8,768]{1,0:T(8,128)S(1)}, f32[208,384]{1,0:T(8,128)S(1)}, bf16[208,384]{1,0:T(8,128)(2,1)S(1)}, bf16[4,96,...) custom-call(s32[4]{0:T(128)S(1)} %pad_add_fusion.scal, f32[208,768]{1,0:T(8,128)S(1)} %copy-done.19, ...), custom_call_target="tpu_custom_call" | custom-call | flops 1962934272 | bytes 5984256 | tf_op jit(solution)/shard_map/pallas_call | solution.py:377
  287.7 6.9 %collective-permute-done.77 = bf16[2,96,768]{2,1,0:T(8,128)(2,1)} collective-permute-done((bf16[2,96,768]{2,1,0:T(8,128)(2,1)}, bf16[2,96,768]{2,1,0:T(8,128)(2,1)}, u32[]{:S(2)}, u32[]{:S(2)}) %collective-permute-start.77) | collective-permute-done | bytes 294944 | tf_op jit(solution)/shard_map/ppermute | solution.py:439
  300.4 6.1 %collective-permute-start.84 = (bf16[96,768]{1,0:T(8,128)(2,1)S(1)}, bf16[96,768]{1,0:T(8,128)(2,1)S(1)}, u32[]{:S(2)}, u32[]{:S(2)}) collective-permute-start(bf16[96,768]{1,0:T(8,128)(2,1)S(1)} %get-tuple-element.369), channel_id=1, source_target_pairs={{0,16},{4,20},{8,24},{12,28},{16,0},{20,4},{24,8},{28,12},{1,17},{... | collective-permute-start | bytes 442376 | tf_op jit(solution)/shard_map/ppermute | solution.py:439
  313.7 4.6 %collective-permute-start.83 = (bf16[96,768]{1,0:T(8,128)(2,1)S(1)}, bf16[96,768]{1,0:T(8,128)(2,1)S(1)}, u32[]{:S(2)}, u32[]{:S(2)}) collective-permute-start(bf16[96,768]{1,0:T(8,128)(2,1)S(1)} %get-tuple-element.367), channel_id=1, source_target_pairs={{0,8},{4,12},{8,0},{12,4},{16,24},{20,28},{24,16},{28,20},{1,9},{5... | collective-permute-start | bytes 442376 | tf_op jit(solution)/shard_map/ppermute | solution.py:439
  (331 shorter events, 171.8 us)
Async XLA Ops:
  25.1 18.1 %collective-permute-start.15 = (bf16[2,96,768]{2,1,0:T(8,128)(2,1)S(1)}, bf16[2,96,768]{2,1,0:T(8,128)(2,1)S(1)}, u32[]{:S(2)}, u32[]{:S(2)}) collective-permute-start(bf16[2,96,768]{2,1,0:T(8,128)(2,1)S(1)} %pad_maximum_fusion.8), channel_id=1, source_target_pairs={{0,24},{4,28},{8,16},{12,20},{16,8},{20,12},{24,0},{28,4},{1,25},{... | collective-permute-start | bytes 884744 | tf_op jit(solution)/shard_map/ppermute | solution.py:439
  27.6 23.3 %collective-permute-start.14 = (bf16[2,96,768]{2,1,0:T(8,128)(2,1)S(1)}, bf16[2,96,768]{2,1,0:T(8,128)(2,1)}, u32[]{:S(2)}, u32[]{:S(2)}) collective-permute-start(bf16[2,96,768]{2,1,0:T(8,128)(2,1)S(1)} %pad_maximum_fusion.8), channel_id=1, source_target_pairs={{0,16},{4,20},{8,24},{12,28},{16,0},{20,4},{24,8},{28,12},{1,17},{... | collective-permute-start | bytes 884744 | tf_op jit(solution)/shard_map/ppermute | solution.py:439
  27.6 23.3 %collective-permute-start.13 = (bf16[2,96,768]{2,1,0:T(8,128)(2,1)S(1)}, bf16[2,96,768]{2,1,0:T(8,128)(2,1)}, u32[]{:S(2)}, u32[]{:S(2)}) collective-permute-start(bf16[2,96,768]{2,1,0:T(8,128)(2,1)S(1)} %pad_maximum_fusion.8), channel_id=1, source_target_pairs={{0,8},{4,12},{8,0},{12,4},{16,24},{20,28},{24,16},{28,20},{1,9},{5... | collective-permute-start | bytes 884744 | tf_op jit(solution)/shard_map/ppermute | solution.py:439
  53.1 38.1 %collective-permute-start.22 = (bf16[4,2,96,768]{3,2,1,0:T(8,128)(2,1)}, bf16[4,2,96,768]{3,2,1,0:T(8,128)(2,1)}, u32[]{:S(2)}, u32[]{:S(2)}) collective-permute-start(bf16[4,2,96,768]{3,2,1,0:T(8,128)(2,1)} %pad_maximum_fusion.refs_0_), channel_id=1, source_target_pairs={{0,4},{4,0},{8,12},{12,8},{16,20},{20,16},{24,28},{28,24},{1,5},{5... | collective-permute-start | bytes 3538952 | tf_op jit(solution)/shard_map/ppermute | solution.py:439
  60.9 22.4 %collective-permute-start.12 = (bf16[208,384]{1,0:T(8,128)(2,1)S(1)}, bf16[208,384]{1,0:T(8,128)(2,1)S(1)}, u32[]{:S(2)}, u32[]{:S(2)}) collective-permute-start(bf16[208,384]{1,0:T(8,128)(2,1)S(1)} %add_convert_fusion.13), channel_id=1, source_target_pairs={{0,1},{1,0},{2,3},{3,2},{4,5},{5,4},{6,7},{7,6},{8,9},{9,8},{10,11... | collective-permute-start | bytes 479240 | tf_op jit(solution)/shard_map/ppermute | solution.py:442
  83.2 22.5 %collective-permute-start.23 = (bf16[4,96,768]{2,1,0:T(8,128)(2,1)}, bf16[4,96,768]{2,1,0:T(8,128)(2,1)}, u32[]{:S(2)}, u32[]{:S(2)}) collective-permute-start(bf16[4,96,768]{2,1,0:T(8,128)(2,1)} %pad_maximum_fusion.4.refs_7_), channel_id=1, source_target_pairs={{0,4},{4,0},{8,12},{12,8},{16,20},{20,16},{24,28},{28,24},{1,5},{5... | collective-permute-start | bytes 1769480 | tf_op jit(solution)/shard_map/ppermute | solution.py:439
  85.5 20.3 %collective-permute-start.24 = (bf16[96,768]{1,0:T(8,128)(2,1)}, bf16[96,768]{1,0:T(8,128)(2,1)}, u32[]{:S(2)}, u32[]{:S(2)}) collective-permute-start(bf16[96,768]{1,0:T(8,128)(2,1)} %get-tuple-element.197), channel_id=1, source_target_pairs={{0,8},{4,12},{8,0},{12,4},{16,24},{20,28},{24,16},{28,20},{1,9},{5... | collective-permute-start | bytes 442376 | tf_op jit(solution)/shard_map/ppermute | solution.py:439
  87.6 18.2 %collective-permute-start.25 = (bf16[96,768]{1,0:T(8,128)(2,1)}, bf16[96,768]{1,0:T(8,128)(2,1)}, u32[]{:S(2)}, u32[]{:S(2)}) collective-permute-start(bf16[96,768]{1,0:T(8,128)(2,1)} %get-tuple-element.198), channel_id=1, source_target_pairs={{0,16},{4,20},{8,24},{12,28},{16,0},{20,4},{24,8},{28,12},{1,17},{... | collective-permute-start | bytes 442376 | tf_op jit(solution)/shard_map/ppermute | solution.py:439
  87.9 17.8 %collective-permute-start.26 = (bf16[96,768]{1,0:T(8,128)(2,1)}, bf16[96,768]{1,0:T(8,128)(2,1)}, u32[]{:S(2)}, u32[]{:S(2)}) collective-permute-start(bf16[96,768]{1,0:T(8,128)(2,1)} %get-tuple-element.199), channel_id=1, source_target_pairs={{0,24},{4,28},{8,16},{12,20},{16,8},{20,12},{24,0},{28,4},{1,25},{... | collective-permute-start | bytes 442376 | tf_op jit(solution)/shard_map/ppermute | solution.py:439
  104.2 24.4 %collective-permute-start.27 = (bf16[4,96,768]{2,1,0:T(8,128)(2,1)S(1)}, bf16[4,96,768]{2,1,0:T(8,128)(2,1)S(1)}, u32[]{:S(2)}, u32[]{:S(2)}) collective-permute-start(bf16[4,96,768]{2,1,0:T(8,128)(2,1)S(1)} %pad_maximum_fusion.5.refs_14_), channel_id=1, source_target_pairs={{0,4},{4,0},{8,12},{12,8},{16,20},{20,16},{24,28},{28,24},{1,5},{5... | collective-permute-start | bytes 1769480 | tf_op jit(solution)/shard_map/ppermute | solution.py:439
  105.8 22.9 %collective-permute-start.28 = (bf16[208,384]{1,0:T(8,128)(2,1)}, bf16[208,384]{1,0:T(8,128)(2,1)S(1)}, u32[]{:S(2)}, u32[]{:S(2)}) collective-permute-start(bf16[208,384]{1,0:T(8,128)(2,1)} %slice_select_fusion), channel_id=1, source_target_pairs={{0,8},{4,12},{8,0},{12,4},{16,24},{20,28},{24,16},{28,20},{1,9},{5... | collective-permute-start | bytes 479240 | tf_op jit(solution)/shard_map/ppermute | solution.py:439
  106.9 21.8 %collective-permute-start.29 = (bf16[208,384]{1,0:T(8,128)(2,1)}, bf16[208,384]{1,0:T(8,128)(2,1)S(1)}, u32[]{:S(2)}, u32[]{:S(2)}) collective-permute-start(bf16[208,384]{1,0:T(8,128)(2,1)} %slice_select_fusion), channel_id=1, source_target_pairs={{0,16},{4,20},{8,24},{12,28},{16,0},{20,4},{24,8},{28,12},{1,17},{... | collective-permute-start | bytes 479240 | tf_op jit(solution)/shard_map/ppermute | solution.py:439
  108.1 20.5 %collective-permute-start.30 = (bf16[208,384]{1,0:T(8,128)(2,1)}, bf16[208,384]{1,0:T(8,128)(2,1)S(1)}, u32[]{:S(2)}, u32[]{:S(2)}) collective-permute-start(bf16[208,384]{1,0:T(8,128)(2,1)} %slice_select_fusion), channel_id=1, source_target_pairs={{0,24},{4,28},{8,16},{12,20},{16,8},{20,12},{24,0},{28,4},{1,25},{... | collective-permute-start | bytes 479240 | tf_op jit(solution)/shard_map/ppermute | solution.py:439
  127.2 18.6 %collective-permute-start.40 = (bf16[4,96,768]{2,1,0:T(8,128)(2,1)S(1)}, bf16[4,96,768]{2,1,0:T(8,128)(2,1)S(1)}, u32[]{:S(2)}, u32[]{:S(2)}) collective-permute-start(bf16[4,96,768]{2,1,0:T(8,128)(2,1)S(1)} %pad_maximum_fusion.6.refs_16_), channel_id=1, source_target_pairs={{0,4},{4,0},{8,12},{12,8},{16,20},{20,16},{24,28},{28,24},{1,5},{5... | collective-permute-start | bytes 1769480 | tf_op jit(solution)/shard_map/ppermute | solution.py:439
  165.3 21.3 %collective-permute-start.47 = (bf16[4,96,768]{2,1,0:T(8,128)(2,1)}, bf16[4,96,768]{2,1,0:T(8,128)(2,1)}, u32[]{:S(2)}, u32[]{:S(2)}) collective-permute-start(bf16[4,96,768]{2,1,0:T(8,128)(2,1)} %get-tuple-element.226), channel_id=1, source_target_pairs={{0,4},{4,0},{8,12},{12,8},{16,20},{20,16},{24,28},{28,24},{1,5},{5... | collective-permute-start | bytes 1769480 | tf_op jit(solution)/shard_map/ppermute | solution.py:439
  180.0 20.8 %collective-permute-start.51 = (bf16[4,96,768]{2,1,0:T(8,128)(2,1)}, bf16[4,96,768]{2,1,0:T(8,128)(2,1)S(1)}, u32[]{:S(2)}, u32[]{:S(2)}) collective-permute-start(bf16[4,96,768]{2,1,0:T(8,128)(2,1)} %copy-done.10), channel_id=1, source_target_pairs={{0,4},{4,0},{8,12},{12,8},{16,20},{20,16},{24,28},{28,24},{1,5},{5... | collective-permute-start | bytes 1769480 | tf_op jit(solution)/shard_map/ppermute | solution.py:439
  223.9 28.4 %collective-permute-start.62 = (bf16[4,2,96,768]{3,2,1,0:T(8,128)(2,1)S(1)}, bf16[4,2,96,768]{3,2,1,0:T(8,128)(2,1)S(1)}, u32[]{:S(2)}, u32[]{:S(2)}) collective-permute-start(bf16[4,2,96,768]{3,2,1,0:T(8,128)(2,1)S(1)} %get-tuple-element.247), channel_id=1, source_target_pairs={{0,4},{4,0},{8,12},{12,8},{16,20},{20,16},{24,28},{28,24},{1,5},{5... | collective-permute-start | bytes 3538952 | tf_op jit(solution)/shard_map/ppermute | solution.py:439
  234.8 19.5 %collective-permute-start.65 = (bf16[96,768]{1,0:T(8,128)(2,1)S(1)}, bf16[96,768]{1,0:T(8,128)(2,1)S(1)}, u32[]{:S(2)}, u32[]{:S(2)}) collective-permute-start(bf16[96,768]{1,0:T(8,128)(2,1)S(1)} %get-tuple-element.370), channel_id=1, source_target_pairs={{0,24},{4,28},{8,16},{12,20},{16,8},{20,12},{24,0},{28,4},{1,25},{... | collective-permute-start | bytes 442376 | tf_op jit(solution)/shard_map/ppermute | solution.py:439
  237.0 17.3 %collective-permute-start.61 = (bf16[208,384]{1,0:T(8,128)(2,1)S(1)}, bf16[208,384]{1,0:T(8,128)(2,1)S(1)}, u32[]{:S(2)}, u32[]{:S(2)}) collective-permute-start(bf16[208,384]{1,0:T(8,128)(2,1)S(1)} %add_convert_fusion.8.refs_1_), channel_id=1, source_target_pairs={{0,1},{1,0},{2,3},{3,2},{4,5},{5,4},{6,7},{7,6},{8,9},{9,8},{10,11... | collective-permute-start | bytes 479240 | tf_op jit(solution)/shard_map/ppermute | solution.py:442
  260.0 17.0 %collective-permute-start.70 = (bf16[208,384]{1,0:T(8,128)(2,1)S(1)}, bf16[208,384]{1,0:T(8,128)(2,1)S(1)}, u32[]{:S(2)}, u32[]{:S(2)}) collective-permute-start(bf16[208,384]{1,0:T(8,128)(2,1)S(1)} %add_convert_fusion.7), channel_id=1, source_target_pairs={{0,2},{1,3},{2,0},{3,1},{4,6},{5,7},{6,4},{7,5},{8,10},{9,11},{10,... | collective-permute-start | bytes 479240 | tf_op jit(solution)/shard_map/ppermute | solution.py:442
  272.1 22.5 %collective-permute-start.77 = (bf16[2,96,768]{2,1,0:T(8,128)(2,1)}, bf16[2,96,768]{2,1,0:T(8,128)(2,1)}, u32[]{:S(2)}, u32[]{:S(2)}) collective-permute-start(bf16[2,96,768]{2,1,0:T(8,128)(2,1)} %get-tuple-element.347), channel_id=1, source_target_pairs={{0,16},{4,20},{8,24},{12,28},{16,0},{20,4},{24,8},{28,12},{1,17},{... | collective-permute-start | bytes 884744 | tf_op jit(solution)/shard_map/ppermute | solution.py:439
  273.0 21.6 %collective-permute-start.78 = (bf16[2,96,768]{2,1,0:T(8,128)(2,1)}, bf16[2,96,768]{2,1,0:T(8,128)(2,1)}, u32[]{:S(2)}, u32[]{:S(2)}) collective-permute-start(bf16[2,96,768]{2,1,0:T(8,128)(2,1)} %get-tuple-element.346), channel_id=1, source_target_pairs={{0,24},{4,28},{8,16},{12,20},{16,8},{20,12},{24,0},{28,4},{1,25},{... | collective-permute-start | bytes 884744 | tf_op jit(solution)/shard_map/ppermute | solution.py:439
  298.7 21.1 %collective-permute-start.85 = (bf16[96,768]{1,0:T(8,128)(2,1)S(1)}, bf16[96,768]{1,0:T(8,128)(2,1)S(1)}, u32[]{:S(2)}, u32[]{:S(2)}) collective-permute-start(bf16[96,768]{1,0:T(8,128)(2,1)S(1)} %get-tuple-element.368), channel_id=1, source_target_pairs={{0,24},{4,28},{8,16},{12,20},{16,8},{20,12},{24,0},{28,4},{1,25},{... | collective-permute-start | bytes 442376 | tf_op jit(solution)/shard_map/ppermute | solution.py:439
  300.4 19.3 %collective-permute-start.84 = (bf16[96,768]{1,0:T(8,128)(2,1)S(1)}, bf16[96,768]{1,0:T(8,128)(2,1)S(1)}, u32[]{:S(2)}, u32[]{:S(2)}) collective-permute-start(bf16[96,768]{1,0:T(8,128)(2,1)S(1)} %get-tuple-element.369), channel_id=1, source_target_pairs={{0,16},{4,20},{8,24},{12,28},{16,0},{20,4},{24,8},{28,12},{1,17},{... | collective-permute-start | bytes 442376 | tf_op jit(solution)/shard_map/ppermute | solution.py:439
  (101 other events, 943.1 us)

commit v5 on v4

--- a/solution.py
+++ b/solution.py
@@ -660,8 +660,8 @@
     keep, send, mlp_sum[1] = bar(keep, send, mlp_sum[1])
     one_sum = fold(one_sum)
     own, other = joined(keep, send)
-    own, other, one_sum, mlp_sum = bar(own, other, one_sum, mlp_sum)
     one_sum = planes(list(one_sum))
+    own, other, one_sum[1], mlp_sum = bar(own, other, one_sum[1], mlp_sum)
     input_grad, *small_grads = run(
         functools.partial(final_kernel, tokens, 4),
         scal,

time: 324 us -> 329 us (1.015)
  waiting for transfers between devices: 143 us -> 156 us
  starting transfers between devices: 101 us -> 90.2 us
    ppermute x56, waiting for transfers between devices: 106 us -> 123 us  [across(): return lax.ppermute(value, 'fsdp', [(i, i ^ k) for i in range(fsdp)])]
    ppermute x56, starting transfers between devices: 91.1 us -> 81.3 us  [across(): return lax.ppermute(value, 'fsdp', [(i, i ^ k) for i in range(fsdp)])]
    ppermute x30, waiting for transfers between devices: 36.9 us -> 32.7 us  [over(): return lax.ppermute(value, 'tensor', [(i, i ^ k) for i in range(tensor)])]
    unnamed x87 -> x89, local copies, waits for them, and re-layouts: 8.9 us -> 8.9 us
  transfers between devices with their start and end apart: 86 -> 86, of which waited for: 33 -> 33; matrix products, arithmetic and copies ran while one was open for 8% -> 10% of each run, Pallas kernels for 8% -> 8%
where the time goes in v5:
time: 329 us; the launch traced here: 328 us
  waiting for transfers between devices  156 us (47%)
  starting transfers between devices  90.2 us (27%)
  Pallas kernels  41.6 us (13%)
  local copies, waits for them, and re-layouts  19.3 us (6%)
  other arithmetic  18.9 us (6%)
    ppermute x56, waiting for transfers between devices, across(): return lax.ppermute(value, 'fsdp', [(i, i ^ k) for i in range(fsdp)])  123 us
    ppermute x56, starting transfers between devices, across(): return lax.ppermute(value, 'fsdp', [(i, i ^ k) for i in range(fsdp)])  81.3 us
    pallas_call x9, Pallas kernels, run(): pl.pallas_call(kernel, out_shape=outs, in_specs=[pl.BlockSpec(memory_spac...  41.6 us
    ppermute x30, waiting for transfers between devices, over(): return lax.ppermute(value, 'tensor', [(i, i ^ k) for i in range(tensor)])  32.7 us
    ppermute x30, starting transfers between devices, over(): return lax.ppermute(value, 'tensor', [(i, i ^ k) for i in range(tensor)])  8.92 us
    unnamed x89, local copies, waits for them, and re-layouts  8.9 us
  transfers between devices with their start and end apart: 86, of which 33 were waited for; matrix products, arithmetic and copies ran while one was open for 10% of the time, Pallas kernels for 8%

profile of v5, /device:TPU:0, one launch (start us, length us, event | category | flops | bytes accessed | tf_op | source)
XLA Modules:
  0.0 328.2 jit_solution(14295611567260832026)
XLA Ops:
  3.7 5.1 %collective-permute-start.8 = (bf16[96,896]{1,0:T(8,128)(2,1)S(1)}, bf16[96,896]{1,0:T(8,128)(2,1)S(1)}, u32[]{:S(2)}, u32[]{:S(2)}) collective-permute-start(bf16[96,896]{1,0:T(8,128)(2,1)S(1)} %get-tuple-element.394), channel_id=1, source_target_pairs={{0,24},{4,28},{8,16},{12,20},{16,8},{20,12},{24,0},{28,4},{1,25},{... | collective-permute-start | bytes 516104 | tf_op jit(solution)/shard_map/ppermute | solution.py:439
  9.4 4.7 %collective-permute-done.8 = bf16[96,896]{1,0:T(8,128)(2,1)S(1)} collective-permute-done((bf16[96,896]{1,0:T(8,128)(2,1)S(1)}, bf16[96,896]{1,0:T(8,128)(2,1)S(1)}, u32[]{:S(2)}, u32[]{:S(2)}) %collective-permute-start.8) | collective-permute-done | bytes 172064 | tf_op jit(solution)/shard_map/ppermute | solution.py:439
  14.1 9.3 %collective-permute-done.7 = bf16[96,896]{1,0:T(8,128)(2,1)S(1)} collective-permute-done((bf16[96,896]{1,0:T(8,128)(2,1)S(1)}, bf16[96,896]{1,0:T(8,128)(2,1)S(1)}, u32[]{:S(2)}, u32[]{:S(2)}) %collective-permute-start.7) | collective-permute-done | bytes 172064 | tf_op jit(solution)/shard_map/ppermute | solution.py:439
  29.7 10.3 %collective-permute-done.9.refs_2_.refs_8_ = bf16[4,96,896]{2,1,0:T(8,128)(2,1)S(1)} collective-permute-done((bf16[4,96,896]{2,1,0:T(8,128)(2,1)S(1)}, bf16[4,96,896]{2,1,0:T(8,128)(2,1)S(1)}, u32[]{:S(2)}, u32[]{:S(2)}) %collective-permute-start.9) | collective-permute-done | bytes 688160 | tf_op jit(solution)/shard_map/ppermute | solution.py:439
  43.1 7.8 %collective-permute-done.14 = bf16[2,96,768]{2,1,0:T(8,128)(2,1)} collective-permute-done((bf16[2,96,768]{2,1,0:T(8,128)(2,1)S(1)}, bf16[2,96,768]{2,1,0:T(8,128)(2,1)}, u32[]{:S(2)}, u32[]{:S(2)}) %collective-permute-start.14) | collective-permute-done | bytes 294944 | tf_op jit(solution)/shard_map/ppermute | solution.py:439
  64.5 4.5 %collective-permute-done.17 = bf16[96,768]{1,0:T(8,128)(2,1)S(1)} collective-permute-done((bf16[96,768]{1,0:T(8,128)(2,1)S(1)}, bf16[96,768]{1,0:T(8,128)(2,1)S(1)}, u32[]{:S(2)}, u32[]{:S(2)}) %collective-permute-start.17) | collective-permute-done | bytes 147488 | tf_op jit(solution)/shard_map/ppermute | solution.py:439
  76.3 6.9 %collective-permute-done.20 = bf16[96,768]{1,0:T(8,128)(2,1)S(1)} collective-permute-done((bf16[96,768]{1,0:T(8,128)(2,1)S(1)}, bf16[96,768]{1,0:T(8,128)(2,1)S(1)}, u32[]{:S(2)}, u32[]{:S(2)}) %collective-permute-start.20) | collective-permute-done | bytes 147488 | tf_op jit(solution)/shard_map/ppermute | solution.py:439
  91.2 13.0 %conditional.2 = (f32[208,768]{1,0:T(8,128)}, bf16[208,384]{1,0:T(8,128)(2,1)}, bf16[208,384]{1,0:T(8,128)(2,1)}) conditional(s32[]{:T(128)} %convert_element_type.357, () %tuple.38, (s32[4]{0:T(128)S(1)}, f32[208,768]{1,0:T(8,128)S(1)}, bf16[208,384]{1,0:T(8,128)(2,1)S(1)}, bf16[208,384]{1,0:T(8,128)(2,1)S(1)}, f32[8,768]{1,0:T(8,128)S(1)}, ...), branch_computations={%region_0.1_spmd, %region_1.2_spmd} | conditional | flops 491292672 | bytes 7495824 | solution.py:464
  96.1 5.7 %collective-permute-done.1 = bf16[208,384]{1,0:T(8,128)(2,1)S(1)} collective-permute-done((bf16[208,384]{1,0:T(8,128)(2,1)S(1)}, bf16[208,384]{1,0:T(8,128)(2,1)S(1)}, u32[]{:S(2)}, u32[]{:S(2)}) %collective-permute-start.1) | collective-permute-done | bytes 159776 | tf_op jit(solution)/shard_map/cond/branch_1_fun/ppermute | solution.py:442
  111.4 15.8 %conditional.3 = (f32[208,768]{1,0:T(8,128)}, f32[208,768]{1,0:T(8,128)}, bf16[208,768]{1,0:T(8,128)(2,1)}, bf16[208,384]{1,0:T(8,128)(2,1)S(1)}) conditional(s32[]{:T(128)} %convert_element_type.357, () %tuple.37, (s32[4]{0:T(128)S(1)}, f32[208,768]{1,0:T(8,128)}, bf16[208,384]{1,0:T(8,128)(2,1)}, bf16[208,384]{1,0:T(8,128)(2,1)}, ...), branch_computations={%region_2.3_spmd, %region_3.4_spmd} | conditional | flops 741566784 | bytes 8419096 | solution.py:464
  117.7 5.4 %collective-permute-done.4 = bf16[208,384]{1,0:T(8,128)(2,1)S(1)} collective-permute-done((bf16[208,384]{1,0:T(8,128)(2,1)S(1)}, bf16[208,384]{1,0:T(8,128)(2,1)S(1)}, u32[]{:S(2)}, u32[]{:S(2)}) %collective-permute-start.4) | collective-permute-done | bytes 159776 | tf_op jit(solution)/shard_map/cond/branch_1_fun/ppermute | solution.py:442
  137.0 6.6 %collective-permute-done.32.refs_2_ = bf16[208,384]{1,0:T(8,128)(2,1)S(1)} collective-permute-done((bf16[208,384]{1,0:T(8,128)(2,1)S(1)}, bf16[208,384]{1,0:T(8,128)(2,1)S(1)}, u32[]{:S(2)}, u32[]{:S(2)}) %collective-permute-start.32) | collective-permute-done | bytes 159776 | tf_op jit(solution)/shard_map/ppermute | solution.py:439
  147.8 10.6 %shard_map.281 = (f32[4,208,384]{2,1,0:T(8,128)S(1)}, bf16[4,208,384]{2,1,0:T(8,128)(2,1)S(1)}, f32[4,208,384]{2,1,0:T(8,128)S(1)}, bf16[4,208,384]{2,1,0:T(8,12...) custom-call(s32[4]{0:T(128)S(1)} %pad_add_fusion.scal, ...), custom_call_target="tpu_custom_call" | custom-call | flops 5888802816 | bytes 11108352 | tf_op jit(solution)/shard_map/pallas_call | solution.py:377
  169.8 9.5 %collective-permute-done.43 = bf16[208,384]{1,0:T(8,128)(2,1)S(1)} collective-permute-done((bf16[208,384]{1,0:T(8,128)(2,1)S(1)}, bf16[208,384]{1,0:T(8,128)(2,1)S(1)}, u32[]{:S(2)}, u32[]{:S(2)}) %collective-permute-start.43) | collective-permute-done | bytes 159776 | tf_op jit(solution)/shard_map/ppermute | solution.py:439
  180.9 4.6 %collective-permute-done.45 = bf16[208,384]{1,0:T(8,128)(2,1)} collective-permute-done((bf16[208,384]{1,0:T(8,128)(2,1)S(1)}, bf16[208,384]{1,0:T(8,128)(2,1)}, u32[]{:S(2)}, u32[]{:S(2)}) %collective-permute-start.45) | collective-permute-done | bytes 159776 | tf_op jit(solution)/shard_map/ppermute | solution.py:442
  192.5 7.5 %shard_map.282 = (f32[208,768]{1,0:T(8,128)S(1)}, f32[8,768]{1,0:T(8,128)S(1)}, f32[208,384]{1,0:T(8,128)S(1)}, bf16[208,384]{1,0:T(8,128)(2,1)S(1)}, bf16[4,96,...) custom-call(s32[4]{0:T(128)S(1)} %pad_add_fusion.scal, f32[208,768]{1,0:T(8,128)S(1)} %copy-done.20, ...), custom_call_target="tpu_custom_call" | custom-call | flops 1962934272 | bytes 5764736 | tf_op jit(solution)/shard_map/pallas_call | solution.py:377
  215.0 4.5 %collective-permute-done.56 = bf16[96,768]{1,0:T(8,128)(2,1)S(1)} collective-permute-done((bf16[96,768]{1,0:T(8,128)(2,1)S(1)}, bf16[96,768]{1,0:T(8,128)(2,1)S(1)}, u32[]{:S(2)}, u32[]{:S(2)}) %collective-permute-start.56) | collective-permute-done | bytes 147488 | tf_op jit(solution)/shard_map/ppermute | solution.py:439
  219.5 4.3 %shard_map.283 = (f32[208,768]{1,0:T(8,128)S(1)}, f32[8,768]{1,0:T(8,128)S(1)}, f32[208,384]{1,0:T(8,128)S(1)}, bf16[208,384]{1,0:T(8,128)(2,1)S(1)}, bf16[4,2,9...) custom-call(s32[4]{0:T(128)S(1)} %pad_add_fusion.scal, f32[208,768]{1,0:T(8,128)} %get-tuple-element.205.refs_6_.x_up, ...), custom_call_target="tpu_custom_call" | custom-call | flops 1226833920 | bytes 8146944 | tf_op jit(solution)/shard_map/pallas_call | solution.py:377
  230.3 4.5 %collective-permute-done.60 = bf16[208,384]{1,0:T(8,128)(2,1)S(1)} collective-permute-done((bf16[208,384]{1,0:T(8,128)(2,1)S(1)}, bf16[208,384]{1,0:T(8,128)(2,1)S(1)}, u32[]{:S(2)}, u32[]{:S(2)}) %collective-permute-start.60) | collective-permute-done | bytes 159776 | tf_op jit(solution)/shard_map/ppermute | solution.py:442
  239.6 12.7 %collective-permute-done.62 = bf16[4,2,96,768]{3,2,1,0:T(8,128)(2,1)S(1)} collective-permute-done((bf16[4,2,96,768]{3,2,1,0:T(8,128)(2,1)S(1)}, bf16[4,2,96,768]{3,2,1,0:T(8,128)(2,1)S(1)}, u32[]{:S(2)}, u32[]{:S(2)}) %collective-permute-start.62) | collective-permute-done | bytes 1179680 | tf_op jit(solution)/shard_map/ppermute | solution.py:439
  254.3 5.6 %collective-permute-done.69 = bf16[208,384]{1,0:T(8,128)(2,1)S(1)} collective-permute-done((bf16[208,384]{1,0:T(8,128)(2,1)S(1)}, bf16[208,384]{1,0:T(8,128)(2,1)S(1)}, u32[]{:S(2)}, u32[]{:S(2)}) %collective-permute-start.69) | collective-permute-done | bytes 159776 | tf_op jit(solution)/shard_map/ppermute | solution.py:439
  265.5 5.6 %shard_map.284 = (f32[208,768]{1,0:T(8,128)S(1)}, f32[8,768]{1,0:T(8,128)S(1)}, f32[208,384]{1,0:T(8,128)S(1)}, bf16[208,384]{1,0:T(8,128)(2,1)S(1)}, bf16[4,96,...) custom-call(s32[4]{0:T(128)S(1)} %pad_add_fusion.scal, f32[208,768]{1,0:T(8,128)S(1)} %copy-done.19, ...), custom_call_target="tpu_custom_call" | custom-call | flops 1962934272 | bytes 5984256 | tf_op jit(solution)/shard_map/pallas_call | solution.py:377
  291.6 10.9 %collective-permute-done.78 = bf16[2,96,768]{2,1,0:T(8,128)(2,1)S(1)} collective-permute-done((bf16[2,96,768]{2,1,0:T(8,128)(2,1)}, bf16[2,96,768]{2,1,0:T(8,128)(2,1)S(1)}, u32[]{:S(2)}, u32[]{:S(2)}) %collective-permute-start.78) | collective-permute-done | bytes 294944 | tf_op jit(solution)/shard_map/ppermute | solution.py:439
  309.3 8.8 %collective-permute-done.84 = bf16[96,768]{1,0:T(8,128)(2,1)S(1)} collective-permute-done((bf16[96,768]{1,0:T(8,128)(2,1)S(1)}, bf16[96,768]{1,0:T(8,128)(2,1)S(1)}, u32[]{:S(2)}, u32[]{:S(2)}) %collective-permute-start.84) | collective-permute-done | bytes 147488 | tf_op jit(solution)/shard_map/ppermute | solution.py:439
  (332 shorter events, 170.3 us)
Async XLA Ops:
  25.1 18.1 %collective-permute-start.15 = (bf16[2,96,768]{2,1,0:T(8,128)(2,1)S(1)}, bf16[2,96,768]{2,1,0:T(8,128)(2,1)S(1)}, u32[]{:S(2)}, u32[]{:S(2)}) collective-permute-start(bf16[2,96,768]{2,1,0:T(8,128)(2,1)S(1)} %pad_maximum_fusion.8), channel_id=1, source_target_pairs={{0,24},{4,28},{8,16},{12,20},{16,8},{20,12},{24,0},{28,4},{1,25},{... | collective-permute-start | bytes 884744 | tf_op jit(solution)/shard_map/ppermute | solution.py:439
  27.6 23.3 %collective-permute-start.14 = (bf16[2,96,768]{2,1,0:T(8,128)(2,1)S(1)}, bf16[2,96,768]{2,1,0:T(8,128)(2,1)}, u32[]{:S(2)}, u32[]{:S(2)}) collective-permute-start(bf16[2,96,768]{2,1,0:T(8,128)(2,1)S(1)} %pad_maximum_fusion.8), channel_id=1, source_target_pairs={{0,16},{4,20},{8,24},{12,28},{16,0},{20,4},{24,8},{28,12},{1,17},{... | collective-permute-start | bytes 884744 | tf_op jit(solution)/shard_map/ppermute | solution.py:439
  27.6 23.3 %collective-permute-start.13 = (bf16[2,96,768]{2,1,0:T(8,128)(2,1)S(1)}, bf16[2,96,768]{2,1,0:T(8,128)(2,1)}, u32[]{:S(2)}, u32[]{:S(2)}) collective-permute-start(bf16[2,96,768]{2,1,0:T(8,128)(2,1)S(1)} %pad_maximum_fusion.8), channel_id=1, source_target_pairs={{0,8},{4,12},{8,0},{12,4},{16,24},{20,28},{24,16},{28,20},{1,9},{5... | collective-permute-start | bytes 884744 | tf_op jit(solution)/shard_map/ppermute | solution.py:439
  53.1 38.1 %collective-permute-start.22 = (bf16[4,2,96,768]{3,2,1,0:T(8,128)(2,1)}, bf16[4,2,96,768]{3,2,1,0:T(8,128)(2,1)}, u32[]{:S(2)}, u32[]{:S(2)}) collective-permute-start(bf16[4,2,96,768]{3,2,1,0:T(8,128)(2,1)} %pad_maximum_fusion.refs_0_), channel_id=1, source_target_pairs={{0,4},{4,0},{8,12},{12,8},{16,20},{20,16},{24,28},{28,24},{1,5},{5... | collective-permute-start | bytes 3538952 | tf_op jit(solution)/shard_map/ppermute | solution.py:439
  60.9 22.4 %collective-permute-start.12 = (bf16[208,384]{1,0:T(8,128)(2,1)S(1)}, bf16[208,384]{1,0:T(8,128)(2,1)S(1)}, u32[]{:S(2)}, u32[]{:S(2)}) collective-permute-start(bf16[208,384]{1,0:T(8,128)(2,1)S(1)} %add_convert_fusion.13), channel_id=1, source_target_pairs={{0,1},{1,0},{2,3},{3,2},{4,5},{5,4},{6,7},{7,6},{8,9},{9,8},{10,11... | collective-permute-start | bytes 479240 | tf_op jit(solution)/shard_map/ppermute | solution.py:442
  83.2 22.5 %collective-permute-start.23 = (bf16[4,96,768]{2,1,0:T(8,128)(2,1)}, bf16[4,96,768]{2,1,0:T(8,128)(2,1)}, u32[]{:S(2)}, u32[]{:S(2)}) collective-permute-start(bf16[4,96,768]{2,1,0:T(8,128)(2,1)} %pad_maximum_fusion.4.refs_7_), channel_id=1, source_target_pairs={{0,4},{4,0},{8,12},{12,8},{16,20},{20,16},{24,28},{28,24},{1,5},{5... | collective-permute-start | bytes 1769480 | tf_op jit(solution)/shard_map/ppermute | solution.py:439
  85.5 20.3 %collective-permute-start.24 = (bf16[96,768]{1,0:T(8,128)(2,1)}, bf16[96,768]{1,0:T(8,128)(2,1)}, u32[]{:S(2)}, u32[]{:S(2)}) collective-permute-start(bf16[96,768]{1,0:T(8,128)(2,1)} %get-tuple-element.197), channel_id=1, source_target_pairs={{0,8},{4,12},{8,0},{12,4},{16,24},{20,28},{24,16},{28,20},{1,9},{5... | collective-permute-start | bytes 442376 | tf_op jit(solution)/shard_map/ppermute | solution.py:439
  87.6 18.2 %collective-permute-start.25 = (bf16[96,768]{1,0:T(8,128)(2,1)}, bf16[96,768]{1,0:T(8,128)(2,1)}, u32[]{:S(2)}, u32[]{:S(2)}) collective-permute-start(bf16[96,768]{1,0:T(8,128)(2,1)} %get-tuple-element.198), channel_id=1, source_target_pairs={{0,16},{4,20},{8,24},{12,28},{16,0},{20,4},{24,8},{28,12},{1,17},{... | collective-permute-start | bytes 442376 | tf_op jit(solution)/shard_map/ppermute | solution.py:439
  87.9 17.8 %collective-permute-start.26 = (bf16[96,768]{1,0:T(8,128)(2,1)}, bf16[96,768]{1,0:T(8,128)(2,1)}, u32[]{:S(2)}, u32[]{:S(2)}) collective-permute-start(bf16[96,768]{1,0:T(8,128)(2,1)} %get-tuple-element.199), channel_id=1, source_target_pairs={{0,24},{4,28},{8,16},{12,20},{16,8},{20,12},{24,0},{28,4},{1,25},{... | collective-permute-start | bytes 442376 | tf_op jit(solution)/shard_map/ppermute | solution.py:439
  104.2 24.4 %collective-permute-start.27 = (bf16[4,96,768]{2,1,0:T(8,128)(2,1)S(1)}, bf16[4,96,768]{2,1,0:T(8,128)(2,1)S(1)}, u32[]{:S(2)}, u32[]{:S(2)}) collective-permute-start(bf16[4,96,768]{2,1,0:T(8,128)(2,1)S(1)} %pad_maximum_fusion.5.refs_14_), channel_id=1, source_target_pairs={{0,4},{4,0},{8,12},{12,8},{16,20},{20,16},{24,28},{28,24},{1,5},{5... | collective-permute-start | bytes 1769480 | tf_op jit(solution)/shard_map/ppermute | solution.py:439
  105.8 22.9 %collective-permute-start.28 = (bf16[208,384]{1,0:T(8,128)(2,1)}, bf16[208,384]{1,0:T(8,128)(2,1)S(1)}, u32[]{:S(2)}, u32[]{:S(2)}) collective-permute-start(bf16[208,384]{1,0:T(8,128)(2,1)} %slice_select_fusion), channel_id=1, source_target_pairs={{0,8},{4,12},{8,0},{12,4},{16,24},{20,28},{24,16},{28,20},{1,9},{5... | collective-permute-start | bytes 479240 | tf_op jit(solution)/shard_map/ppermute | solution.py:439
  106.9 21.8 %collective-permute-start.29 = (bf16[208,384]{1,0:T(8,128)(2,1)}, bf16[208,384]{1,0:T(8,128)(2,1)S(1)}, u32[]{:S(2)}, u32[]{:S(2)}) collective-permute-start(bf16[208,384]{1,0:T(8,128)(2,1)} %slice_select_fusion), channel_id=1, source_target_pairs={{0,16},{4,20},{8,24},{12,28},{16,0},{20,4},{24,8},{28,12},{1,17},{... | collective-permute-start | bytes 479240 | tf_op jit(solution)/shard_map/ppermute | solution.py:439
  108.1 20.5 %collective-permute-start.30 = (bf16[208,384]{1,0:T(8,128)(2,1)}, bf16[208,384]{1,0:T(8,128)(2,1)S(1)}, u32[]{:S(2)}, u32[]{:S(2)}) collective-permute-start(bf16[208,384]{1,0:T(8,128)(2,1)} %slice_select_fusion), channel_id=1, source_target_pairs={{0,24},{4,28},{8,16},{12,20},{16,8},{20,12},{24,0},{28,4},{1,25},{... | collective-permute-start | bytes 479240 | tf_op jit(solution)/shard_map/ppermute | solution.py:439
  127.2 18.6 %collective-permute-start.40 = (bf16[4,96,768]{2,1,0:T(8,128)(2,1)S(1)}, bf16[4,96,768]{2,1,0:T(8,128)(2,1)S(1)}, u32[]{:S(2)}, u32[]{:S(2)}) collective-permute-start(bf16[4,96,768]{2,1,0:T(8,128)(2,1)S(1)} %pad_maximum_fusion.6.refs_16_), channel_id=1, source_target_pairs={{0,4},{4,0},{8,12},{12,8},{16,20},{20,16},{24,28},{28,24},{1,5},{5... | collective-permute-start | bytes 1769480 | tf_op jit(solution)/shard_map/ppermute | solution.py:439
  165.3 21.3 %collective-permute-start.47 = (bf16[4,96,768]{2,1,0:T(8,128)(2,1)}, bf16[4,96,768]{2,1,0:T(8,128)(2,1)}, u32[]{:S(2)}, u32[]{:S(2)}) collective-permute-start(bf16[4,96,768]{2,1,0:T(8,128)(2,1)} %get-tuple-element.226), channel_id=1, source_target_pairs={{0,4},{4,0},{8,12},{12,8},{16,20},{20,16},{24,28},{28,24},{1,5},{5... | collective-permute-start | bytes 1769480 | tf_op jit(solution)/shard_map/ppermute | solution.py:439
  180.0 20.8 %collective-permute-start.51 = (bf16[4,96,768]{2,1,0:T(8,128)(2,1)}, bf16[4,96,768]{2,1,0:T(8,128)(2,1)S(1)}, u32[]{:S(2)}, u32[]{:S(2)}) collective-permute-start(bf16[4,96,768]{2,1,0:T(8,128)(2,1)} %copy-done.10), channel_id=1, source_target_pairs={{0,4},{4,0},{8,12},{12,8},{16,20},{20,16},{24,28},{28,24},{1,5},{5... | collective-permute-start | bytes 1769480 | tf_op jit(solution)/shard_map/ppermute | solution.py:439
  223.9 28.4 %collective-permute-start.62 = (bf16[4,2,96,768]{3,2,1,0:T(8,128)(2,1)S(1)}, bf16[4,2,96,768]{3,2,1,0:T(8,128)(2,1)S(1)}, u32[]{:S(2)}, u32[]{:S(2)}) collective-permute-start(bf16[4,2,96,768]{3,2,1,0:T(8,128)(2,1)S(1)} %get-tuple-element.247), channel_id=1, source_target_pairs={{0,4},{4,0},{8,12},{12,8},{16,20},{20,16},{24,28},{28,24},{1,5},{5... | collective-permute-start | bytes 3538952 | tf_op jit(solution)/shard_map/ppermute | solution.py:439
  234.8 19.5 %collective-permute-start.65 = (bf16[96,768]{1,0:T(8,128)(2,1)S(1)}, bf16[96,768]{1,0:T(8,128)(2,1)S(1)}, u32[]{:S(2)}, u32[]{:S(2)}) collective-permute-start(bf16[96,768]{1,0:T(8,128)(2,1)S(1)} %get-tuple-element.372), channel_id=1, source_target_pairs={{0,24},{4,28},{8,16},{12,20},{16,8},{20,12},{24,0},{28,4},{1,25},{... | collective-permute-start | bytes 442376 | tf_op jit(solution)/shard_map/ppermute | solution.py:439
  236.9 17.3 %collective-permute-start.61 = (bf16[208,384]{1,0:T(8,128)(2,1)S(1)}, bf16[208,384]{1,0:T(8,128)(2,1)S(1)}, u32[]{:S(2)}, u32[]{:S(2)}) collective-permute-start(bf16[208,384]{1,0:T(8,128)(2,1)S(1)} %add_convert_fusion.8.refs_1_), channel_id=1, source_target_pairs={{0,1},{1,0},{2,3},{3,2},{4,5},{5,4},{6,7},{7,6},{8,9},{9,8},{10,11... | collective-permute-start | bytes 479240 | tf_op jit(solution)/shard_map/ppermute | solution.py:442
  261.6 18.3 %collective-permute-start.72 = (bf16[2,96,768]{2,1,0:T(8,128)(2,1)}, bf16[2,96,768]{2,1,0:T(8,128)(2,1)}, u32[]{:S(2)}, u32[]{:S(2)}) collective-permute-start(bf16[2,96,768]{2,1,0:T(8,128)(2,1)} %get-tuple-element.350), channel_id=1, source_target_pairs={{0,8},{4,12},{8,0},{12,4},{16,24},{20,28},{24,16},{28,20},{1,9},{5... | collective-permute-start | bytes 884744 | tf_op jit(solution)/shard_map/ppermute | solution.py:439
  276.0 26.5 %collective-permute-start.78 = (bf16[2,96,768]{2,1,0:T(8,128)(2,1)}, bf16[2,96,768]{2,1,0:T(8,128)(2,1)S(1)}, u32[]{:S(2)}, u32[]{:S(2)}) collective-permute-start(bf16[2,96,768]{2,1,0:T(8,128)(2,1)} %get-tuple-element.349), channel_id=1, source_target_pairs={{0,16},{4,20},{8,24},{12,28},{16,0},{20,4},{24,8},{28,12},{1,17},{... | collective-permute-start | bytes 884744 | tf_op jit(solution)/shard_map/ppermute | solution.py:439
  276.9 25.6 %collective-permute-start.79 = (bf16[2,96,768]{2,1,0:T(8,128)(2,1)}, bf16[2,96,768]{2,1,0:T(8,128)(2,1)}, u32[]{:S(2)}, u32[]{:S(2)}) collective-permute-start(bf16[2,96,768]{2,1,0:T(8,128)(2,1)} %get-tuple-element.348), channel_id=1, source_target_pairs={{0,24},{4,28},{8,16},{12,20},{16,8},{20,12},{24,0},{28,4},{1,25},{... | collective-permute-start | bytes 884744 | tf_op jit(solution)/shard_map/ppermute | solution.py:439
  287.2 18.2 %collective-permute-start.77 = (bf16[96,768]{1,0:T(8,128)(2,1)S(1)}, bf16[96,768]{1,0:T(8,128)(2,1)S(1)}, u32[]{:S(2)}, u32[]{:S(2)}) collective-permute-start(bf16[96,768]{1,0:T(8,128)(2,1)S(1)} %get-tuple-element.371), channel_id=1, source_target_pairs={{0,8},{4,12},{8,0},{12,4},{16,24},{20,28},{24,16},{28,20},{1,9},{5... | collective-permute-start | bytes 442376 | tf_op jit(solution)/shard_map/ppermute | solution.py:439
  289.9 19.3 %collective-permute-start.85 = (bf16[96,768]{1,0:T(8,128)(2,1)S(1)}, bf16[96,768]{1,0:T(8,128)(2,1)S(1)}, u32[]{:S(2)}, u32[]{:S(2)}) collective-permute-start(bf16[96,768]{1,0:T(8,128)(2,1)S(1)} %get-tuple-element.370), channel_id=1, source_target_pairs={{0,24},{4,28},{8,16},{12,20},{16,8},{20,12},{24,0},{28,4},{1,25},{... | collective-permute-start | bytes 442376 | tf_op jit(solution)/shard_map/ppermute | solution.py:439
  (102 other events, 983.8 us)
